TPU v7x, 32 devices: a whole 2x2x4 slice. The times are simulated.
32 devices in a mesh: parts: 2 (over x), leaf: 16 (over z, y, core).
Axes of the slice: x: 2, y: 2, z: 4, core: 2. Of those that a mesh axis runs over, the one named last changes fastest.
Arguments:
- inputs: bfloat16 [65536, 64], P(('parts', 'leaf')), parts along dimension 0, may hold values from -6 to 6
- geometry: float32 [4, 65536], P(None, ('parts', 'leaf')), parts along dimension 1, as said below
- leaf_basis: bfloat16 [512, 128, 64], P(('parts', 'leaf')), parts along dimension 0, may hold values from -0.5 to 0.5
- transfer: bfloat16 [512, 64, 64], P(('parts', 'leaf')), parts along dimension 0, may hold values from -0.25 to 0.25
- leaf_coupling: bfloat16 [512, 16, 64, 64], P(('parts', 'leaf')), parts along dimension 0, may hold values from -0.1875 to 0.1875
- top_coupling: bfloat16 [64, 8, 64, 64], P(('parts', 'leaf')), parts along dimension 0, may hold values from -0.25 to 0.25
- near_list: int32 [512, 24], P(('parts', 'leaf')), parts along dimension 0, may hold values from -16 to 271, as said below
- recv_slot: int32 [512, 16], P(('parts', 'leaf')), parts along dimension 0, may hold values from 0 to 383, as said below
- send_leaf: int32 [32, 16, 24], P(('parts', 'leaf')), parts along dimension 0, may hold values from 0 to 15, as said below
- top_source: int32 [64, 8], P(('parts', 'leaf')), parts along dimension 0, may hold values from 0 to 31
Outputs:
- result_field: float32 [65536, 64], P(('parts', 'leaf')), parts along dimension 0
There are 2 independent parts, one for each index of `parts`. A program takes and returns all parts, laid end to end along the dimension named above; each array names one. Nothing has to cross between parts.
Inputs may be any that keep to these rules, and one draw needn't show every extreme that they name: `geometry`: point q of leaf l = q // 128 has row 0 in [l / 16, l / 16 + 1), rows 1 and 2 in [0, 1), row 3 in [0.1, 1]. `near_list`: each leaf's 24 partners are distinct leaves within 16 of it, always including itself and the leaves 16 below and above it. `recv_slot`: within one block of 16 leaves the values are distinct: each of the 384 received slots is read by at most one far interaction. `send_leaf`: slots that no interaction reads hold 0.
All inputs are finite; a program needn't handle non-finite values.
Results may differ from a plain program's by a relative error of at most 0.003.
Values may be sent and summed in bfloat16 or wider, within the bound.
No kernel may reach another device: no remote copies, remote signals or barrier semaphores. Data moves between devices by JAX's collectives and lax.ppermute only.
A program may use at most 128 MiB of HBM per device.

v0:
```python
import jax
import jax.numpy as jnp
from jax import lax
from jax.sharding import PartitionSpec as P

BRANCH = 8
REACH = 16


coulomb_scale = 0.07957747154594767
soften = 0.0025


def with_halo(cells, sides, width):
    for axis, dim in sides:
        count = lax.axis_size(axis)
        ends = count - 1
        head = lax.slice_in_dim(cells, 0, width, axis=dim)
        tail = lax.slice_in_dim(cells, cells.shape[dim] - width, cells.shape[dim], axis=dim)
        cells = jnp.concatenate(
            [
                lax.ppermute(tail, axis, [(i, (i + 1) % count) for i in range(ends)]),
                cells,
                lax.ppermute(head, axis, [((i + 1) % count, i) for i in range(ends)]),
            ],
            axis=dim,
        )
    return cells


def kernel_block(targets, sources):
    delta_x = targets[0][None, :, None] - sources[0][:, None, :]
    delta_y = targets[1][None, :, None] - sources[1][:, None, :]
    delta_z = targets[2][None, :, None] - sources[2][:, None, :]
    dist_sq = delta_x * delta_x + delta_y * delta_y + delta_z * delta_z
    return (sources[3][:, None, :] * (coulomb_scale * lax.rsqrt(dist_sq + soften))).astype(
        jnp.bfloat16
    )


def body(
    inputs,
    geometry,
    leaf_basis,
    transfer,
    leaf_coupling,
    top_coupling,
    near_list,
    recv_slot,
    send_leaf,
    top_source,
):
    leaves_here = leaf_basis.shape[0]
    leaf_size = leaf_basis.shape[1]
    rank_size = leaf_basis.shape[2]
    columns_rhs = inputs.shape[1]
    slot_count = send_leaf.shape[2]
    upper_here = leaves_here // BRANCH
    leaf_inputs = inputs.reshape(leaves_here, leaf_size, columns_rhs)
    leaf_coef = jnp.einsum(
        "lpr,lps->lrs", leaf_basis, leaf_inputs, preferred_element_type=jnp.float32
    ).astype(jnp.bfloat16)
    upper_coef = jnp.einsum(
        "pcqr,pcqs->prs",
        transfer.reshape(upper_here, BRANCH, rank_size, rank_size),
        leaf_coef.reshape(upper_here, BRANCH, rank_size, columns_rhs),
        preferred_element_type=jnp.float32,
    ).astype(jnp.bfloat16)
    skeleton = lax.all_gather(upper_coef, "leaf", axis=0, tiled=True)
    upper_field = jnp.einsum(
        "pkab,pkbs->pas", top_coupling, skeleton[top_source], preferred_element_type=jnp.float32
    ).astype(jnp.bfloat16)
    owners = lax.all_to_all(send_leaf[0], "leaf", split_axis=0, concat_axis=0, tiled=True)
    sources = recv_slot // slot_count * leaves_here + owners.reshape(-1)[recv_slot]
    everyone = lax.all_gather(leaf_coef, "leaf", axis=0, tiled=True)
    panels = everyone[sources]
    leaf_potential = jnp.einsum(
        "lkab,lkbs->las", leaf_coupling, panels, preferred_element_type=jnp.float32
    )
    upper_representation = jnp.repeat(upper_field, BRANCH, axis=0)
    summed_potential = (
        leaf_potential
        + jnp.einsum(
            "qjz,qzr->qjr", transfer, upper_representation, preferred_element_type=jnp.float32
        )
    ).astype(jnp.bfloat16)
    far_part = jnp.einsum(
        "lpa,las->lps", leaf_basis, summed_potential, preferred_element_type=jnp.float32
    )
    margin = REACH * leaf_size
    wide_inputs = with_halo(inputs, (("leaf", 0),), margin)
    wide_points = with_halo(geometry, (("leaf", 1),), margin)
    span_leaves = leaves_here + 2 * REACH
    block_inputs = wide_inputs.reshape(span_leaves, leaf_size, columns_rhs)
    block_points = wide_points.reshape(4, span_leaves, leaf_size)
    local_ids = near_list - (lax.axis_index("leaf") * leaves_here - REACH)

    def near_leaf(item):
        near_ids, leaf_pos = item
        targets = block_points[:, leaf_pos + REACH]
        green_function = kernel_block(targets, block_points[:, near_ids])
        return jnp.einsum(
            "kpq,kqs->ps",
            green_function,
            block_inputs[near_ids],
            preferred_element_type=jnp.float32,
        )

    near_part = lax.map(near_leaf, (local_ids, jnp.arange(leaves_here, dtype=jnp.int32)))
    return (near_part + far_part).reshape(leaves_here * leaf_size, columns_rhs)


def solution(mesh):
    in_specs = (
        P(("parts", "leaf"), None),
        P(None, ("parts", "leaf")),
        P(("parts", "leaf"), None, None),
        P(("parts", "leaf"), None, None),
        P(("parts", "leaf"), None, None, None),
        P(("parts", "leaf"), None, None, None),
        P(("parts", "leaf"), None),
        P(("parts", "leaf"), None),
        P(("parts", "leaf"), None, None),
        P(("parts", "leaf"), None),
    )
    out_specs = P(("parts", "leaf"), None)
    return jax.shard_map(body, mesh=mesh, in_specs=in_specs, out_specs=out_specs, check_vma=False)
```

profile of v0, /device:TPU:0, one launch (start us, length us, event | category | flops | bytes accessed | tf_op | source)
XLA Modules:
  0.0 145.7 jit_solution(7527611885702213975)
XLA Ops:
  6.6 2.5 %collective-permute-start.2 = (bf16[2048,64]{0,1:T(8,128)(2,1)}, bf16[2048,64]{0,1:T(8,128)(2,1)S(1)}, u32[]{:S(2)}, u32[]{:S(2)}) collective-permute-start(bf16[2048,64]{0,1:T(8,128)(2,1)} %param.12), channel_id=1, source_target_pairs={{0,1},{1,2},{2,3},{3,4},{4,5},{5,6},{6,7},{7,8},{8,9},{9,10},{10,1... | collective-permute-start | bytes 786440 | tf_op jit(solution)/shard_map/ppermute | solution.py:22
  9.1 1.3 collective-permute-start.3
  10.4 5.2 %collective-permute-start = (f32[4,2048]{1,0:T(4,128)}, f32[4,2048]{1,0:T(4,128)S(1)}, u32[]{:S(2)}, u32[]{:S(2)}) collective-permute-start(f32[4,2048]{1,0:T(4,128)} %param.13), channel_id=1, source_target_pairs={{0,1},{1,2},{2,3},{3,4},{4,5},{5,6},{6,7},{7,8},{8,9},{9,10},{10,1... | collective-permute-start | bytes 98312 | tf_op jit(solution)/shard_map/ppermute | solution.py:22
  15.6 1.3 collective-permute-start.1
  16.9 2.0 %convolution_convert_fusion = bf16[16,64,64]{2,1,0:T(8,128)(2,1)} fusion(bf16[16,128,64]{1,2,0:T(8,128)(2,1)} %param.14, bf16[2048,64]{0,1:T(8,128)(2,1)} %param.12), kind=kOutput, calls=%fused_computation.32 | convolution fusion | flops 16842752 | bytes 655360 | tf_op jit(solution)/shard_map/lpr,lps->lrs/dot_general | solution.py:60
  18.9 9.3 %all-to-all-start = ((s32[16,1,24]{2,1,0:T(1,128)}), s32[16,1,24]{2,1,0:T(1,128)S(1)}, u32[]{:S(2)}, u32[]{:S(2)}) async-start(s32[16,1,24]{2,1,0:T(1,128)} %bitcast.120), calls=%async_computation | async-start | bytes 16384 | tf_op jit(solution)/shard_map/all_to_all | solution.py:73
  28.2 0.7 compare_select_fusion.2
  28.9 1.2 fusion.18
  30.2 24.4 %all_gather.7 = bf16[32,64,64]{2,1,0:T(8,128)(2,1)S(1)} all-gather(bf16[2,64,64]{2,1,0:T(8,128)(2,1)S(1)} %copy.27), channel_id=1, replica_groups=mesh['parts'=2,'leaf'=16] {'leaf'}, dimensions={0}, use_global_device_ids=true | all-gather | bytes 278528 | tf_op jit(solution)/shard_map/all_gather | solution.py:69
  56.2 0.7 reduce.3
  57.0 1.9 %gather_fusion.2 = s32[256]{0:T(256)S(1)} fusion(s32[384]{0:T(512)S(1)} %reshape.85, s32[1024]{0:T(1024)S(1)} %pad_clamp_fusion.3), kind=kCustom, calls=%fused_computation.2 | custom fusion | bytes 3072 | tf_op jit(solution)/shard_map/gather | solution.py:74
  59.3 0.9 copy.23
  60.2 67.3 %while.12 = (s32[]{:T(128)}, f32[16,128,64]{1,2,0:T(8,128)S(1)}, s32[16]{0:T(128)S(1)}, f32[4,48,128]{2,0,1:T(4,128)S(1)}, s32[16,24]{1,0:T(8,128)S(1)}, /*index...) while((s32[]{:T(128)}, f32[16,128,64]{1,2,0:T(8,128)S(1)}, ...), condition=%wide.region_1.2_spmd, body=%wide.region_0.1_spmd.sunk | while | flops 54661196 | bytes 1864843 | solution.py:109
  62.8 0.7 gather_fusion
  63.5 0.9 fusion.44
  67.0 0.7 gather_fusion
  67.7 0.9 fusion.44
  71.2 0.7 gather_fusion
  71.9 0.9 fusion.44
  75.4 0.7 gather_fusion
  76.1 0.9 fusion.44
  79.6 0.7 gather_fusion
  80.3 0.9 fusion.44
  83.8 0.7 gather_fusion
  84.5 0.9 fusion.44
  88.0 0.7 gather_fusion
  88.7 0.9 fusion.44
  92.2 0.7 gather_fusion
  92.9 0.9 fusion.44
  96.4 0.7 gather_fusion
  97.1 0.9 fusion.44
  100.6 0.7 gather_fusion
  101.3 0.9 fusion.44
  104.8 0.7 gather_fusion
  105.5 0.9 fusion.44
  109.0 0.7 gather_fusion
  109.7 0.9 fusion.44
  113.2 0.7 gather_fusion
  113.9 0.9 fusion.44
  117.4 0.7 gather_fusion
  118.1 0.9 fusion.44
  121.7 0.7 gather_fusion
  122.4 0.9 fusion.44
  125.9 0.7 gather_fusion
  126.6 0.9 fusion.44
  127.5 5.3 %gather_fusion.3 = bf16[256,64,64]{2,1,0:T(8,128)(2,1)} fusion(bf16[256,64,64]{2,1,0:T(8,128)(2,1)} %all-gather.2.cloned.1.call-done, s32[1024]{0:T(1024)S(1)} %pad_clamp_fusion.2), kind=kCustom, calls=%fused_computation.3 | custom fusion | bytes 4195328 | tf_op jit(solution)/shard_map/gather | solution.py:76
  132.7 4.8 %convolution_bitcast_fusion.2 = f32[16,64,64]{2,1,0:T(8,128)S(1)} fusion(bf16[16,16,64,64]{3,2,1,0:T(8,128)(2,1)} %bitcast.111, bf16[16,16,64,64]{3,2,1,0:T(8,128)(2,1)} %param.16), kind=kOutput, calls=%fused_computation.28 | convolution fusion | flops 134217728 | bytes 4456448 | tf_op jit(solution)/shard_map/lkab,lkbs->las/dot_general | solution.py:77
  138.0 0.8 copy.44
  (157 shorter events, 23.1 us)
Async XLA Ops:
  6.5 22.4 %copy-start = (bf16[16,64,64]{2,1,0:T(8,128)(2,1)S(1)}, bf16[16,64,64]{2,1,0:T(8,128)(2,1)}, u32[]{:S(2)}) copy-start(bf16[16,64,64]{2,1,0:T(8,128)(2,1)} %param.15) | copy-start | bytes 393220
  6.5 48.1 %copy-start.7 = (s32[2,8]{1,0:T(2,128)S(1)}, s32[2,8]{1,0:T(2,128)}, u32[]{:S(2)}) copy-start(s32[2,8]{1,0:T(2,128)} %param.21) | copy-start | bytes 196
  6.5 48.8 %copy-start.3 = (bf16[2,8,64,64]{3,2,1,0:T(8,128)(2,1)S(1)}, bf16[2,8,64,64]{3,2,1,0:T(8,128)(2,1)}, u32[]{:S(2)}) copy-start(bf16[2,8,64,64]{3,2,1,0:T(8,128)(2,1)} %param.17) | copy-start | bytes 393220
  6.5 49.1 %copy-start.6 = (s32[16,24]{1,0:T(8,128)S(1)}, s32[16,24]{1,0:T(8,128)}, u32[]{:S(2)}) copy-start(s32[16,24]{1,0:T(8,128)} %param.18) | copy-start | bytes 4612
  6.5 120.9 %all-gather.2.cloned.1.call-start = ((), (), s32[]{:S(2)}) async-start(), calls=%async_computation.1 | async-start | bytes 4456448 | tf_op jit(solution)/shard_map/all_gather | solution.py:75
  6.6 52.6 %collective-permute-start.2 = (bf16[2048,64]{0,1:T(8,128)(2,1)}, bf16[2048,64]{0,1:T(8,128)(2,1)S(1)}, u32[]{:S(2)}, u32[]{:S(2)}) collective-permute-start(bf16[2048,64]{0,1:T(8,128)(2,1)} %param.12), channel_id=1, source_target_pairs={{0,1},{1,2},{2,3},{3,4},{4,5},{5,6},{6,7},{7,8},{8,9},{9,10},{10,1... | collective-permute-start | bytes 786440 | tf_op jit(solution)/shard_map/ppermute | solution.py:22
  9.1 50.1 %collective-permute-start.3 = (bf16[2048,64]{0,1:T(8,128)(2,1)}, bf16[2048,64]{0,1:T(8,128)(2,1)S(1)}, u32[]{:S(2)}, u32[]{:S(2)}) collective-permute-start(bf16[2048,64]{0,1:T(8,128)(2,1)} %param.12), channel_id=1, source_target_pairs={{1,0},{2,1},{3,2},{4,3},{5,4},{6,5},{7,6},{8,7},{9,8},{10,9},{11,1... | collective-permute-start | bytes 786440 | tf_op jit(solution)/shard_map/ppermute | solution.py:24
  10.4 48.7 %collective-permute-start = (f32[4,2048]{1,0:T(4,128)}, f32[4,2048]{1,0:T(4,128)S(1)}, u32[]{:S(2)}, u32[]{:S(2)}) collective-permute-start(f32[4,2048]{1,0:T(4,128)} %param.13), channel_id=1, source_target_pairs={{0,1},{1,2},{2,3},{3,4},{4,5},{5,6},{6,7},{7,8},{8,9},{9,10},{10,1... | collective-permute-start | bytes 98312 | tf_op jit(solution)/shard_map/ppermute | solution.py:22
  15.6 43.6 %collective-permute-start.1 = (f32[4,2048]{1,0:T(4,128)}, f32[4,2048]{1,0:T(4,128)S(1)}, u32[]{:S(2)}, u32[]{:S(2)}) collective-permute-start(f32[4,2048]{1,0:T(4,128)} %param.13), channel_id=1, source_target_pairs={{1,0},{2,1},{3,2},{4,3},{5,4},{6,5},{7,6},{8,7},{9,8},{10,9},{11,1... | collective-permute-start | bytes 98312 | tf_op jit(solution)/shard_map/ppermute | solution.py:24
  18.9 36.8 %all-to-all-start = ((s32[16,1,24]{2,1,0:T(1,128)}), s32[16,1,24]{2,1,0:T(1,128)S(1)}, u32[]{:S(2)}, u32[]{:S(2)}) async-start(s32[16,1,24]{2,1,0:T(1,128)} %bitcast.120), calls=%async_computation | async-start | bytes 16384 | tf_op jit(solution)/shard_map/all_to_all | solution.py:73
  56.9 2.1 %copy-start.4 = (s32[16,16]{1,0:T(8,128)S(1)}, s32[16,16]{1,0:T(8,128)}, u32[]{:S(2)}) copy-start(s32[16,16]{1,0:T(8,128)} %param.19) | copy-start | bytes 3076
  57.0 2.2 %copy-start.5 = (f32[4,2048]{1,0:T(4,128)S(1)}, f32[4,2048]{1,0:T(4,128)}, u32[]{:S(2)}) copy-start(f32[4,2048]{1,0:T(4,128)} %param.13) | copy-start | bytes 98308
  57.0 2.2 %copy-start.2 = (bf16[2048,64]{0,1:T(8,128)(2,1)S(1)}, bf16[2048,64]{0,1:T(8,128)(2,1)}, u32[]{:S(2)}) copy-start(bf16[2048,64]{0,1:T(8,128)(2,1)} %param.12) | copy-start | bytes 786436
  132.7 4.9 %copy-start.1 = (bf16[16,128,64]{1,2,0:T(8,128)(2,1)S(1)}, bf16[16,128,64]{1,2,0:T(8,128)(2,1)}, u32[]{:S(2)}) copy-start(bf16[16,128,64]{1,2,0:T(8,128)(2,1)} %param.14) | copy-start | bytes 786436
Sparse Core Ops, SparseCore 0:
  19.0 56.5 all-gather.1
where the time goes:
time: 146 us
  local copies, waits for them, and re-layouts  41.3 us (28%)
  blocking collectives  24.4 us (17%)
  matrix products  22.8 us (16%)
  loops' own time  21.5 us (15%)
  starting transfers between devices  19.5 us (13%)
  between operations  13.7 us (9%)
  other arithmetic  2.45 us (2%)
    all_gather x1, blocking collectives, body(): skeleton = lax.all_gather(upper_coef, 'leaf', axis=0, tiled=True)  24.4 us
    another operation x1, loops' own time, body(): lax.map(near_leaf, (local_ids, jnp.arange(leaves_here, dtype=jnp.int32)))  21.5 us
    dot_general x16, matrix products, near_leaf(): jnp.einsum('kpq,kqs->ps', green_function, block_inputs[near_ids], preferr...  14.1 us
    gather x16, local copies, waits for them, and re-layouts, near_leaf(): block_inputs[near_ids]  11.2 us
    dynamic_slice x16, local copies, waits for them, and re-layouts, body(): lax.map(near_leaf, (local_ids, jnp.arange(leaves_here, dtype=jnp.int32)))  9.8 us
    gather x16, local copies, waits for them, and re-layouts, near_leaf(): green_function = kernel_block(targets, block_points[:, near_ids])  9.53 us
    all_to_all x1, starting transfers between devices, body(): lax.all_to_all(send_leaf[0], 'leaf', split_axis=0, concat_axis=0, tiled=T...  9.26 us
    ppermute x2, starting transfers between devices, with_halo(): lax.ppermute(tail, axis, [(i, (i + 1) % count) for i in range(ends)])  7.66 us
  transfers between devices with their start and end apart: 6, of which 0 were waited for; matrix products, arithmetic and copies ran while one was open for 38% of the time, Pallas kernels for 0%

commit v1 on v0

v1 whole, which is shorter than its diff:
```python
import functools

import jax
import jax.numpy as jnp
from jax import lax
from jax.experimental import pallas as pl
from jax.experimental.pallas import tpu as pltpu
from jax.sharding import PartitionSpec as P

BRANCH = 8
REACH = 16
SCALE = 0.07957747154594767
SOFTEN = 0.0025
BF, F32 = jnp.bfloat16, jnp.float32
NN = (((1,), (0,)), ((), ()))
NT = (((1,), (1,)), ((), ()))
TN = (((0,), (0,)), ((), ()))
VMEM = pl.BlockSpec(memory_space=pltpu.VMEM)
SMEM = pl.BlockSpec(memory_space=pltpu.SMEM)
FEATS = 16


def dot(a, b, dims=NN):
    return lax.dot_general(a, b, dims, preferred_element_type=F32)


def params(mib):
    return pltpu.CompilerParams(vmem_limit_bytes=mib * 2**20)


def parts_of(x):
    high = x.astype(BF).astype(F32)
    mid = (x - high).astype(BF).astype(F32)
    low = (x - high - mid).astype(BF).astype(F32)
    return high, mid, low


def by_row(rows, values):
    which = lax.rem(rows, 5)
    out = jnp.zeros(rows.shape, F32)
    for j, value in enumerate(values):
        out = jnp.where(which == j, value, out)
    return jnp.where(rows < 15, out, 0.0)


def source_rows(rows, x, y, z, gain):
    wide = by_row(
        rows,
        (-2.0 * gain * x, -2.0 * gain * y, -2.0 * gain * z, gain, gain * (x * x + y * y + z * z + SOFTEN)),
    )
    high, mid, low = parts_of(wide)
    return jnp.where(rows < 5, high, jnp.where(rows < 10, mid, low)).astype(BF)


def pack_kernel(me_ref, in_ref, geo_ref, basis_ref, transfer_ref, send_ref, shard_ref, left_ref, right_ref, own_ref, target_ref):
    leaves, rank, leaf = basis_ref.shape
    rhs, points = in_ref.shape
    center = (me_ref[0] + 1).astype(F32)
    x = geo_ref[0:1, :] - center
    y = geo_ref[1:2, :] - 0.5
    z = geo_ref[2:3, :] - 0.5
    scaled = SCALE * geo_ref[3:4, :]
    gain = 1.0 / (scaled * scaled)
    rows = lax.broadcasted_iota(jnp.int32, (FEATS, points), 0)
    right_ref[rhs:, :] = source_rows(rows, x - 1.0, y, z, gain)
    left_ref[rhs:, :] = source_rows(rows, x + 1.0, y, z, gain)
    own_ref[rhs:, :] = source_rows(rows, x, y, z, gain)
    all_in = in_ref[...]
    right_ref[:rhs, :] = all_in
    left_ref[:rhs, :] = all_in
    own_ref[:rhs, :] = all_in
    high, mid, low = parts_of(by_row(rows, (x, y, z, x * x + y * y + z * z, jnp.ones_like(x))))
    target_ref[0:FEATS, :] = high.astype(BF)
    target_ref[FEATS : 2 * FEATS, :] = jnp.where(rows < 10, mid, 0.0).astype(BF)
    target_ref[2 * FEATS : 3 * FEATS, :] = jnp.where(rows < 5, low, 0.0).astype(BF)

    blank = jnp.zeros((rhs, leaf), BF)
    lanes = lax.broadcasted_iota(jnp.int32, (rank, 2 * rhs), 1)
    uppers = leaves // BRANCH
    upper = [jnp.zeros((rank, 2 * rhs), F32) for _ in range(uppers)]
    for pair in range(leaves // 2):
        a, b = 2 * pair, 2 * pair + 1
        xa = in_ref[:, a * leaf : (a + 1) * leaf]
        xb = in_ref[:, b * leaf : (b + 1) * leaf]
        weights = jnp.concatenate(
            [jnp.concatenate([xa, blank], axis=1), jnp.concatenate([blank, xb], axis=1)], axis=0
        )
        coef = dot(jnp.concatenate([basis_ref[a], basis_ref[b]], axis=1), weights, NT).astype(BF)
        shard_ref[pair * rank : (pair + 1) * rank, :] = coef
        both = jnp.concatenate(
            [jnp.where(lanes < rhs, coef, jnp.zeros_like(coef)), jnp.where(lanes < rhs, jnp.zeros_like(coef), coef)],
            axis=0,
        )
        moved = jnp.concatenate([transfer_ref[a], transfer_ref[b]], axis=0)
        upper[a // BRANCH] += dot(moved, both, TN)
    for p in range(0, uppers, 2):
        left = upper[p] + pltpu.roll(upper[p], rhs, 1)
        right = upper[p + 1] + pltpu.roll(upper[p + 1], rhs, 1)
        at = leaves // 2 * rank + p // 2 * rank
        shard_ref[at : at + rank, :] = jnp.where(lanes < rhs, left, right).astype(BF)
    at = (leaves + uppers) // 2 * rank
    shard_ref[at:, :] = jnp.zeros((shard_ref.shape[0] - at, 2 * rhs), BF)
    shard_ref[at : at + send_ref.shape[0], 0 : send_ref.shape[1]] = send_ref[...].astype(F32).astype(BF)


def near_kernel(count, me_ref, list_ref, own_ref, left_ref, right_ref, target_ref, out_ref, block_ref):
    wide, points = own_ref.shape
    rhs = out_ref.shape[0]
    leaves, near = list_ref.shape
    leaf = points // leaves
    for side, ref in enumerate((left_ref, own_ref, right_ref)):
        for j in range(leaves):
            block_ref[side * leaves + j] = ref[:, j * leaf : (j + 1) * leaf]

    def blank(side):
        rows = lax.broadcasted_iota(jnp.int32, (wide - rhs, leaf), 0)
        for j in range(leaves):
            block_ref[side * leaves + j, rhs:, :] = jnp.where(rows == 4, 1.0, 0.0).astype(BF)

    pl.when(me_ref[0] == 0)(lambda: blank(0))
    pl.when(me_ref[0] == count - 1)(lambda: blank(2))

    def one(l, carry):
        at = pl.ds(pl.multiple_of(l * leaf, leaf), leaf)
        targets = target_ref[:, at].T
        total = jnp.zeros((rhs, leaf), F32)
        for k in range(0, near, 2):
            a, b = list_ref[l, k], list_ref[l, k + 1]
            feats = jnp.concatenate([block_ref[a, rhs:, :], block_ref[b, rhs:, :]], axis=1)
            feats = jnp.concatenate([feats, feats, feats], axis=0)
            green = lax.rsqrt(dot(targets, feats)).astype(BF)
            values = jnp.concatenate([block_ref[a, 0:rhs, :], block_ref[b, 0:rhs, :]], axis=1)
            total = total + dot(values, green, NT)
        out_ref[:, at] = total
        return carry

    lax.fori_loop(0, leaves, one, 0)


def coupling_kernel(c_ref, out_ref):
    leaves, far, rank, _ = c_ref.shape

    def one(l, carry):
        for k in range(0, far, 2):
            out_ref[l, :, k * rank : (k + 2) * rank] = jnp.concatenate([c_ref[l, k], c_ref[l, k + 1]], axis=1)
        return carry

    lax.fori_loop(0, leaves, one, 0)


def far_kernel(count, slots, me_ref, recv_ref, top_ref, all_ref, coupling_ref, top_coupling_ref, transfer_ref, basis_ref, near_ref, out_ref, owner_vmem, owner_ref, sem):
    leaves, rank, leaf = basis_ref.shape
    rhs = out_ref.shape[0]
    far = recv_ref.shape[1]
    uppers, top = top_ref.shape
    me = me_ref[0]
    bits = count.bit_length() - 1

    def place(device):
        gap = lax.bitwise_xor(device, me)
        out = jnp.int32(0)
        for i in range(bits):
            out = out + ((gap >> (bits - 1 - i)) & 1) * (1 << i)
        return out

    table_at = (leaves + uppers) // 2 * rank
    table_rows = all_ref.shape[1] - table_at
    rows = lax.broadcasted_iota(jnp.int32, (table_rows, 2 * rhs), 0)

    for p in range(count):
        table = all_ref[p, table_at:, :].astype(F32)
        mine = jnp.sum(jnp.where(rows == me, table, 0.0), axis=0, keepdims=True)
        owner_vmem[p : p + 1, :] = mine.astype(jnp.int32)
    copy = pltpu.make_async_copy(owner_vmem, owner_ref, sem)
    copy.start()
    copy.wait()

    lanes = lax.broadcasted_iota(jnp.int32, (rank, 2 * rhs), 1)
    half_of = (lanes >= rhs).astype(jnp.int32)

    def panel(position, index, base):
        at = pl.multiple_of(base + (index // 2) * rank, rank)
        both = all_ref[position, pl.ds(at, rank), :]
        return jnp.where(half_of == index % 2, both, jnp.zeros_like(both))

    for p in range(uppers):
        total = jnp.zeros((rank, 2 * rhs), F32)
        for k in range(top):
            source = top_ref[p, k]
            total = total + dot(top_coupling_ref[p, k], panel(place(source // uppers), source % uppers, leaves // 2 * rank))
        field = (total + pltpu.roll(total, rhs, 1)).astype(BF)

        def one(l, carry, field=field):
            total = jnp.zeros((rank, 2 * rhs), F32)
            for quad in range(far // 4):
                panels = []
                for k in range(4 * quad, 4 * quad + 4):
                    slot = recv_ref[l, k]
                    position = place(slot // slots)
                    panels.append(panel(position, owner_ref[position, slot % slots], 0))
                total = total + dot(
                    coupling_ref[l, :, 4 * quad * rank : 4 * (quad + 1) * rank], jnp.concatenate(panels, axis=0)
                )
            total = total + pltpu.roll(total, rhs, 1)
            total = (total + dot(transfer_ref[l], field)).astype(BF)
            at = pl.ds(pl.multiple_of(l * leaf, leaf), leaf)
            out_ref[:, at] = near_ref[:, at] + dot(total[:, 0:rhs], basis_ref[l], TN)
            return carry

        lax.fori_loop(p * BRANCH, (p + 1) * BRANCH, one, 0)


def body(count, inputs, geometry, leaf_basis, transfer, leaf_coupling, top_coupling, near_list, recv_slot, send_leaf, top_source):
    leaves, leaf, rank = leaf_basis.shape
    rhs = inputs.shape[1]
    points = leaves * leaf
    far = recv_slot.shape[1]
    slots = send_leaf.shape[2]
    uppers = leaves // BRANCH
    me = lax.axis_index("leaf").astype(jnp.int32)
    me_list = me.reshape(1)
    in_t = inputs.T
    basis_t = leaf_basis.transpose(0, 2, 1)
    table_rows = -(-count // 16) * 16
    shard_rows = (leaves + uppers) // 2 * rank + table_rows
    wide = jax.ShapeDtypeStruct((rhs + FEATS, points), BF)
    shard, to_left, to_right, own, targets = pl.pallas_call(
        pack_kernel,
        out_shape=(
            jax.ShapeDtypeStruct((shard_rows, 2 * rhs), BF),
            wide,
            wide,
            wide,
            jax.ShapeDtypeStruct((3 * FEATS, points), BF),
        ),
        in_specs=[SMEM] + [VMEM] * 5,
        out_specs=(VMEM,) * 5,
        compiler_params=params(32),
        name="pack",
    )(me_list, in_t, geometry, basis_t, transfer, send_leaf[0])

    up = [(i, i + 1) for i in range(count - 1)]
    down = [(i + 1, i) for i in range(count - 1)]
    left = lax.ppermute(to_right, "leaf", up)
    right = lax.ppermute(to_left, "leaf", down)

    everyone = shard[None]
    bit = count // 2
    while bit:
        other = lax.ppermute(everyone, "leaf", [(i, i ^ bit) for i in range(count)])
        everyone = jnp.concatenate([everyone, other], axis=0)
        bit //= 2

    local_ids = near_list - (me * leaves - REACH)
    near = pl.pallas_call(
        functools.partial(near_kernel, count),
        out_shape=jax.ShapeDtypeStruct((rhs, points), F32),
        in_specs=[SMEM] * 2 + [VMEM] * 4,
        out_specs=VMEM,
        scratch_shapes=[pltpu.VMEM((leaves + 2 * REACH, rhs + FEATS, leaf), BF)],
        compiler_params=params(32),
        name="near",
    )(me_list, local_ids, own, left, right, targets)

    coupling = pl.pallas_call(
        coupling_kernel,
        out_shape=jax.ShapeDtypeStruct((leaves, rank, far * rank), BF),
        in_specs=[VMEM],
        out_specs=VMEM,
        compiler_params=params(32),
        name="coupling",
    )(leaf_coupling)

    out = pl.pallas_call(
        functools.partial(far_kernel, count, slots),
        out_shape=jax.ShapeDtypeStruct((rhs, points), F32),
        in_specs=[SMEM] * 3 + [VMEM] * 6,
        out_specs=VMEM,
        scratch_shapes=[
            pltpu.VMEM((count, 2 * rhs), jnp.int32),
            pltpu.SMEM((count, 2 * rhs), jnp.int32),
            pltpu.SemaphoreType.DMA,
        ],
        compiler_params=params(40),
        name="far",
    )(me_list, recv_slot, top_source, everyone, coupling, top_coupling, transfer, basis_t, near)
    return out.T


def solution(mesh):
    spec = ("parts", "leaf")
    in_specs = (
        P(spec, None),
        P(None, spec),
        P(spec, None, None),
        P(spec, None, None),
        P(spec, None, None, None),
        P(spec, None, None, None),
        P(spec, None),
        P(spec, None),
        P(spec, None, None),
        P(spec, None),
    )
    step = functools.partial(body, mesh.shape["leaf"])
    return jax.shard_map(step, mesh=mesh, in_specs=in_specs, out_specs=P(spec, None), check_vma=False)
```

time: 146 us -> 84.9 us (0.58)
  the two profiles are of different devices: /device:TPU:0 before, /device:TPU:13 now
where the time goes in v1:
time: 84.9 us; the launch traced here: 84.5 us
  waiting for transfers between devices  33.4 us (39%)
  Pallas kernels  31.6 us (37%)
  starting transfers between devices  10.9 us (13%)
  local copies, waits for them, and re-layouts  6.99 us (8%)
  other arithmetic  1.35 us (2%)
    ppermute x4, waiting for transfers between devices, body(): other = lax.ppermute(everyone, 'leaf', [(i, i ^ bit) for i in range(count)])  28.6 us
    pallas_call x1, Pallas kernels, body(): pl.pallas_call(functools.partial(near_kernel, count), out_shape=jax.Shape...  15.1 us
    pallas_call x1, Pallas kernels, body(): pl.pallas_call(functools.partial(far_kernel, count, slots), out_shape=jax...  13.2 us
    unnamed x38, local copies, waits for them, and re-layouts  5.5 us
    ppermute x4, starting transfers between devices, body(): other = lax.ppermute(everyone, 'leaf', [(i, i ^ bit) for i in range(count)])  4.98 us
    ppermute x1, waiting for transfers between devices, body(): right = lax.ppermute(to_left, 'leaf', down)  4.84 us
    ppermute x1, starting transfers between devices, body(): left = lax.ppermute(to_right, 'leaf', up)  3.97 us
    ppermute x1, starting transfers between devices, body(): right = lax.ppermute(to_left, 'leaf', down)  1.92 us
  transfers between devices with their start and end apart: 6, of which 4 were waited for; matrix products, arithmetic and copies ran while one was open for 1% of the time, Pallas kernels for 20%

profile of v1, /device:TPU:13, one launch (start us, length us, event | category | flops | bytes accessed | tf_op | source)
XLA Modules:
  0.0 84.5 jit_solution(15726795010884919841)
XLA Ops:
  0.0 0.0 copy-start.1
  0.0 0.9 %copy-done.1 = bf16[16,128,64]{1,2,0:T(8,128)(2,1)S(1)} copy-done((bf16[16,128,64]{1,2,0:T(8,128)(2,1)S(1)}, bf16[16,128,64]{1,2,0:T(8,128)(2,1)}, u32[]{:S(2)}) %copy-start.1) | copy-done | bytes 262168
  1.0 0.0 copy-start.3
  1.0 0.9 %copy-done.3 = bf16[16,64,64]{2,1,0:T(8,128)(2,1)S(1)} copy-done((bf16[16,64,64]{2,1,0:T(8,128)(2,1)S(1)}, bf16[16,64,64]{2,1,0:T(8,128)(2,1)}, u32[]{:S(2)}) %copy-start.3) | copy-done | bytes 131096
  1.9 0.9 %copy-done.6 = bf16[2048,64]{0,1:T(8,128)(2,1)S(1)} copy-done((bf16[2048,64]{0,1:T(8,128)(2,1)S(1)}, bf16[2048,64]{0,1:T(8,128)(2,1)}, u32[]{:S(2)}) %copy-start.6) | copy-done | bytes 262168
  2.9 0.8 copy-done.7
  3.6 0.7 copy-done.8
  4.3 1.6 %pack.1 = (bf16[592,128]{1,0:T(8,128)(2,1)S(1)}, bf16[80,2048]{1,0:T(8,128)(2,1)}, bf16[80,2048]{1,0:T(8,128)(2,1)}, bf16[80,2048]{1,0:T(8,128)(2,1)S(1)}, bf16[48,2048]{1,0:T(8,128)(2,1)S(1)}) custom-call(s32[1]{0:T(128)} %bitcast.me_ref, bf16[64,2048]{1,0:T(8,128)(2,1)S(1)} %bitcast.13, f32[4,2048]{1,0:T(4,128)S(1)} %copy-done.7, ...), custom_call_target="tpu_custom_call" | custom-call | tf_op jit(solution)/shard_map/pack/pallas_call | solution.py:227
  5.9 2.3 %collective-permute-start = (bf16[1,592,128]{2,1,0:T(8,128)(2,1)S(1)}, bf16[1,592,128]{2,1,0:T(8,128)(2,1)S(1)}, u32[]{:S(2)}, u32[]{:S(2)}) collective-permute-start(bf16[1,592,128]{2,1,0:T(8,128)(2,1)S(1)} %bitcast.7), channel_id=1, source_target_pairs={{0,8},{1,9},{2,10},{3,11},{4,12},{5,13},{6,14},{7,15},{8,0},{9,1},... | collective-permute-start | bytes 454664 | tf_op jit(solution)/shard_map/ppermute | solution.py:250
  8.2 6.8 %collective-permute-done = bf16[1,592,128]{2,1,0:T(8,128)(2,1)S(1)} collective-permute-done((bf16[1,592,128]{2,1,0:T(8,128)(2,1)S(1)}, bf16[1,592,128]{2,1,0:T(8,128)(2,1)S(1)}, u32[]{:S(2)}, u32[]{:S(2)}) %collective-permute-start) | collective-permute-done | bytes 151584 | tf_op jit(solution)/shard_map/ppermute | solution.py:250
  15.0 0.1 collective-permute-start.1
  15.2 8.2 %collective-permute-done.1 = bf16[2,592,128]{2,1,0:T(8,128)(2,1)S(1)} collective-permute-done((bf16[2,592,128]{2,1,0:T(8,128)(2,1)S(1)}, bf16[2,592,128]{2,1,0:T(8,128)(2,1)S(1)}, u32[]{:S(2)}, u32[]{:S(2)}) %collective-permute-start.1) | collective-permute-done | bytes 303136 | tf_op jit(solution)/shard_map/ppermute | solution.py:250
  23.4 0.1 pad_maximum_fusion.1
  23.4 0.3 collective-permute-start.2
  23.7 13.6 %collective-permute-done.2 = bf16[4,592,128]{2,1,0:T(8,128)(2,1)S(1)} collective-permute-done((bf16[4,592,128]{2,1,0:T(8,128)(2,1)S(1)}, bf16[4,592,128]{2,1,0:T(8,128)(2,1)S(1)}, u32[]{:S(2)}, u32[]{:S(2)}) %collective-permute-start.2) | collective-permute-done | bytes 606240 | tf_op jit(solution)/shard_map/ppermute | solution.py:250
  37.3 1.3 %pad_maximum_fusion = bf16[8,592,128]{2,1,0:T(8,128)(2,1)} fusion(bf16[4,592,128]{2,1,0:T(8,128)(2,1)S(1)} %collective-permute-done.2, bf16[2,592,128]{2,1,0:T(8,128)(2,1)S(1)} %collective-permute-done.1, bf16[1,592,128]{2,1,0:T(8,128)(2,1)S(1)} %collective-permute-done, bf16[1,592,128]{2,1,0:T(8,128)(2,1)S(1)} %bitcast.10), kind=kLoop, calls=%fused_computation | loop fusion | flops 1818624 | bytes 2424832 | tf_op jit(solution)/shard_map/concatenate | solution.py:251
  38.6 2.3 %collective-permute-start.3 = (bf16[8,592,128]{2,1,0:T(8,128)(2,1)}, bf16[8,592,128]{2,1,0:T(8,128)(2,1)}, u32[]{:S(2)}, u32[]{:S(2)}) collective-permute-start(bf16[8,592,128]{2,1,0:T(8,128)(2,1)} %pad_maximum_fusion), channel_id=1, source_target_pairs={{0,1},{1,0},{2,3},{3,2},{4,5},{5,4},{6,7},{7,6},{8,9},{9,8},{10,11... | collective-permute-start | bytes 3637256 | tf_op jit(solution)/shard_map/ppermute | solution.py:250
  40.8 0.0 copy-done.11
  40.8 4.0 %collective-permute-start.4 = (bf16[80,2048]{1,0:T(8,128)(2,1)}, bf16[80,2048]{1,0:T(8,128)(2,1)S(1)}, u32[]{:S(2)}, u32[]{:S(2)}) collective-permute-start(bf16[80,2048]{1,0:T(8,128)(2,1)} %get-tuple-element.12), channel_id=1, source_target_pairs={{0,1},{1,2},{2,3},{3,4},{4,5},{5,6},{6,7},{7,8},{8,9},{9,10},{10,1... | collective-permute-start | bytes 983048 | tf_op jit(solution)/shard_map/ppermute | solution.py:244
  44.8 0.0 copy-done.13
  44.8 0.0 copy-done.14
  44.8 0.0 copy-start.16
  44.9 1.9 %collective-permute-start.5 = (bf16[80,2048]{1,0:T(8,128)(2,1)}, bf16[80,2048]{1,0:T(8,128)(2,1)S(1)}, u32[]{:S(2)}, u32[]{:S(2)}) collective-permute-start(bf16[80,2048]{1,0:T(8,128)(2,1)} %get-tuple-element.13), channel_id=1, source_target_pairs={{1,0},{2,1},{3,2},{4,3},{5,4},{6,5},{7,6},{8,7},{9,8},{10,9},{11,1... | collective-permute-start | bytes 983048 | tf_op jit(solution)/shard_map/ppermute | solution.py:245
  46.8 0.0 copy-done
  46.8 1.6 %coupling.1.coupling_ref = bf16[16,64,1024]{2,1,0:T(8,128)(2,1)S(1)} custom-call(bf16[16,16,64,64]{3,2,1,0:T(8,128)(2,1)S(1)} %copy-done), custom_call_target="tpu_custom_call" | custom-call | tf_op jit(solution)/shard_map/coupling/pallas_call | solution.py:265
  48.4 0.0 copy-start.12
  48.5 0.0 copy-start.15
  48.5 0.0 copy-done.16
  48.5 1.0 %constant_dynamic-update-slice_fusion.3 = bf16[16,592,128]{2,1,0:T(8,128)(2,1)S(1)} fusion(bf16[16,592,128]{2,1,0:T(8,128)(2,1)S(1)} %constant_dynamic-update-slice_fusion.4, bf16[1,592,128]{2,1,0:T(8,128)(2,1)} %copy-done.13), kind=kLoop, calls=%fused_computation.6 | loop fusion | bytes 303104
  49.5 0.0 collective-permute-done.4.left_ref
  49.5 4.8 %collective-permute-done.5.right_ref = bf16[80,2048]{1,0:T(8,128)(2,1)S(1)} collective-permute-done((bf16[80,2048]{1,0:T(8,128)(2,1)}, bf16[80,2048]{1,0:T(8,128)(2,1)S(1)}, u32[]{:S(2)}, u32[]{:S(2)}) %collective-permute-start.5) | collective-permute-done | bytes 327712 | tf_op jit(solution)/shard_map/ppermute | solution.py:245
  54.4 15.1 %near.1.near_ref = f32[64,2048]{1,0:T(8,128)S(1)} custom-call(s32[1]{0:T(128)} %bitcast.me_ref, s32[16,24]{1,0:T(8,128)S(1)} %broadcast_subtract_fusion.list_ref, bf16[80,2048]{1,0:T(8,128)(2,1)S(1)} %get-tuple-element.11.own_ref, bf16[80,2048]{1,0:T(8,128)(2,1)S(1)} %collective-permute-done.4.left_ref, ...), custom_call_target="tpu_custom_call" | custom-call | tf_op jit(solution)/shard_map/near/pallas_call | solution.py:255
  69.5 0.0 copy-done.12
  69.5 0.0 copy-start.2
  69.5 0.0 copy-start.4
  69.5 0.0 copy-start.5
  69.5 0.0 copy-start.9
  69.5 0.0 copy-start.10
  69.6 0.0 copy-done.15
  69.6 0.1 constant_dynamic-update-slice_fusion.1
  69.7 0.0 collective-permute-done.3
  69.7 1.5 %constant_dynamic-update-slice_fusion.all_ref = bf16[16,592,128]{2,1,0:T(8,128)(2,1)S(1)} fusion(bf16[16,592,128]{2,1,0:T(8,128)(2,1)S(1)} %constant_dynamic-update-slice_fusion.1, bf16[8,592,128]{2,1,0:T(8,128)(2,1)} %collective-permute-done.3), kind=kLoop, calls=%fused_computation.3 | loop fusion | bytes 2424832 | tf_op jit(solution)/shard_map/concatenate | solution.py:251
  71.2 0.0 copy-done.2
  71.2 0.0 copy-done.4
  71.2 0.0 copy-done.5
  71.2 0.0 copy-done.9
  71.2 0.0 copy-done.10
  71.3 13.2 %far.1 = f32[64,2048]{1,0:T(8,128)} custom-call(s32[1]{0:T(128)} %bitcast.me_ref, s32[16,16]{1,0:T(8,128)S(1)} %copy-done.9, s32[2,8]{1,0:T(2,128)S(1)} %copy-done.10, bf16[16,592,128]{2,1,0:T(8,128)(2,1)S(1)} %constant_dynamic-update-slice_fusion.all_ref, bf16[16,64,1024]{2,1,0:T(8,128)(2,1)S(1)} %coupling.1.coupling_ref, ...), custom_call_target="tpu_custom_call" | custom-call | tf_op jit(solution)/shard_map/far/pallas_call | solution.py:274
  (11 shorter events, 0.1 us)
Async XLA Ops:
  0.0 0.9 %copy-start.1 = (bf16[16,128,64]{1,2,0:T(8,128)(2,1)S(1)}, bf16[16,128,64]{1,2,0:T(8,128)(2,1)}, u32[]{:S(2)}) copy-start(bf16[16,128,64]{1,2,0:T(8,128)(2,1)} %param.12) | copy-start | bytes 786436
  1.0 0.9 %copy-start.3 = (bf16[16,64,64]{2,1,0:T(8,128)(2,1)S(1)}, bf16[16,64,64]{2,1,0:T(8,128)(2,1)}, u32[]{:S(2)}) copy-start(bf16[16,64,64]{2,1,0:T(8,128)(2,1)} %transfer_ref.3) | copy-start | bytes 393220
  1.9 0.9 %copy-start.6 = (bf16[2048,64]{0,1:T(8,128)(2,1)S(1)}, bf16[2048,64]{0,1:T(8,128)(2,1)}, u32[]{:S(2)}) copy-start(bf16[2048,64]{0,1:T(8,128)(2,1)} %param.10) | copy-start | bytes 786436
  2.9 0.8 copy-start.7
  3.6 0.7 copy-start.8
  4.3 42.5 %copy-start = (bf16[16,16,64,64]{3,2,1,0:T(8,128)(2,1)S(1)}, bf16[16,16,64,64]{3,2,1,0:T(8,128)(2,1)}, u32[]{:S(2)}) copy-start(bf16[16,16,64,64]{3,2,1,0:T(8,128)(2,1)} %c_ref.1) | copy-start | bytes 6291460
  5.9 9.1 %collective-permute-start = (bf16[1,592,128]{2,1,0:T(8,128)(2,1)S(1)}, bf16[1,592,128]{2,1,0:T(8,128)(2,1)S(1)}, u32[]{:S(2)}, u32[]{:S(2)}) collective-permute-start(bf16[1,592,128]{2,1,0:T(8,128)(2,1)S(1)} %bitcast.7), channel_id=1, source_target_pairs={{0,8},{1,9},{2,10},{3,11},{4,12},{5,13},{6,14},{7,15},{8,0},{9,1},... | collective-permute-start | bytes 454664 | tf_op jit(solution)/shard_map/ppermute | solution.py:250
  15.0 29.8 %copy-start.13 = (bf16[1,592,128]{2,1,0:T(8,128)(2,1)}, bf16[1,592,128]{2,1,0:T(8,128)(2,1)S(1)}, u32[]{:S(2)}) copy-start(bf16[1,592,128]{2,1,0:T(8,128)(2,1)S(1)} %collective-permute-done) | copy-start | bytes 454660
  15.0 8.3 %collective-permute-start.1 = (bf16[2,592,128]{2,1,0:T(8,128)(2,1)S(1)}, bf16[2,592,128]{2,1,0:T(8,128)(2,1)S(1)}, u32[]{:S(2)}, u32[]{:S(2)}) collective-permute-start(bf16[2,592,128]{2,1,0:T(8,128)(2,1)S(1)} %pad_maximum_fusion.2), channel_id=1, source_target_pairs={{0,4},{1,5},{2,6},{3,7},{4,0},{5,1},{6,2},{7,3},{8,12},{9,13},{10,... | collective-permute-start | bytes 909320 | tf_op jit(solution)/shard_map/ppermute | solution.py:250
  23.4 17.5 %copy-start.11 = (bf16[2,592,128]{2,1,0:T(8,128)(2,1)}, bf16[2,592,128]{2,1,0:T(8,128)(2,1)S(1)}, u32[]{:S(2)}) copy-start(bf16[2,592,128]{2,1,0:T(8,128)(2,1)S(1)} %collective-permute-done.1) | copy-start | bytes 909316
  23.4 13.9 %collective-permute-start.2 = (bf16[4,592,128]{2,1,0:T(8,128)(2,1)S(1)}, bf16[4,592,128]{2,1,0:T(8,128)(2,1)S(1)}, u32[]{:S(2)}, u32[]{:S(2)}) collective-permute-start(bf16[4,592,128]{2,1,0:T(8,128)(2,1)S(1)} %pad_maximum_fusion.1), channel_id=1, source_target_pairs={{0,2},{1,3},{2,0},{3,1},{4,6},{5,7},{6,4},{7,5},{8,10},{9,11},{10,... | collective-permute-start | bytes 1818632 | tf_op jit(solution)/shard_map/ppermute | solution.py:250
  37.3 7.5 %copy-start.14 = (bf16[4,592,128]{2,1,0:T(8,128)(2,1)}, bf16[4,592,128]{2,1,0:T(8,128)(2,1)S(1)}, u32[]{:S(2)}) copy-start(bf16[4,592,128]{2,1,0:T(8,128)(2,1)S(1)} %collective-permute-done.2) | copy-start | bytes 1818628
  38.6 31.1 %collective-permute-start.3 = (bf16[8,592,128]{2,1,0:T(8,128)(2,1)}, bf16[8,592,128]{2,1,0:T(8,128)(2,1)}, u32[]{:S(2)}, u32[]{:S(2)}) collective-permute-start(bf16[8,592,128]{2,1,0:T(8,128)(2,1)} %pad_maximum_fusion), channel_id=1, source_target_pairs={{0,1},{1,0},{2,3},{3,2},{4,5},{5,4},{6,7},{7,6},{8,9},{9,8},{10,11... | collective-permute-start | bytes 3637256 | tf_op jit(solution)/shard_map/ppermute | solution.py:250
  40.8 8.7 %collective-permute-start.4 = (bf16[80,2048]{1,0:T(8,128)(2,1)}, bf16[80,2048]{1,0:T(8,128)(2,1)S(1)}, u32[]{:S(2)}, u32[]{:S(2)}) collective-permute-start(bf16[80,2048]{1,0:T(8,128)(2,1)} %get-tuple-element.12), channel_id=1, source_target_pairs={{0,1},{1,2},{2,3},{3,4},{4,5},{5,6},{6,7},{7,8},{8,9},{9,10},{10,1... | collective-permute-start | bytes 983048 | tf_op jit(solution)/shard_map/ppermute | solution.py:244
  44.8 3.6 %copy-start.16 = (s32[16,24]{1,0:T(8,128)S(1)}, s32[16,24]{1,0:T(8,128)}, u32[]{:S(2)}) copy-start(s32[16,24]{1,0:T(8,128)} %param.16) | copy-start | bytes 4612
  44.9 9.5 %collective-permute-start.5 = (bf16[80,2048]{1,0:T(8,128)(2,1)}, bf16[80,2048]{1,0:T(8,128)(2,1)S(1)}, u32[]{:S(2)}, u32[]{:S(2)}) collective-permute-start(bf16[80,2048]{1,0:T(8,128)(2,1)} %get-tuple-element.13), channel_id=1, source_target_pairs={{1,0},{2,1},{3,2},{4,3},{5,4},{6,5},{7,6},{8,7},{9,8},{10,9},{11,1... | collective-permute-start | bytes 983048 | tf_op jit(solution)/shard_map/ppermute | solution.py:245
  48.4 21.0 %copy-start.12 = (bf16[2,592,128]{2,1,0:T(8,128)(2,1)S(1)}, bf16[2,592,128]{2,1,0:T(8,128)(2,1)}, u32[]{:S(2)}) copy-start(bf16[2,592,128]{2,1,0:T(8,128)(2,1)} %copy-done.11) | copy-start | bytes 909316
  48.5 21.1 %copy-start.15 = (bf16[4,592,128]{2,1,0:T(8,128)(2,1)S(1)}, bf16[4,592,128]{2,1,0:T(8,128)(2,1)}, u32[]{:S(2)}) copy-start(bf16[4,592,128]{2,1,0:T(8,128)(2,1)} %copy-done.14) | copy-start | bytes 1818628
  69.5 1.7 %copy-start.2 = (bf16[16,128,64]{1,2,0:T(8,128)(2,1)S(1)}, bf16[16,128,64]{1,2,0:T(8,128)(2,1)}, u32[]{:S(2)}) copy-start(bf16[16,128,64]{1,2,0:T(8,128)(2,1)} %param.12) | copy-start | bytes 786436
  69.5 1.7 %copy-start.4 = (bf16[16,64,64]{2,1,0:T(8,128)(2,1)S(1)}, bf16[16,64,64]{2,1,0:T(8,128)(2,1)}, u32[]{:S(2)}) copy-start(bf16[16,64,64]{2,1,0:T(8,128)(2,1)} %transfer_ref.3) | copy-start | bytes 393220
  69.5 1.7 %copy-start.5 = (bf16[2,8,64,64]{3,2,1,0:T(8,128)(2,1)S(1)}, bf16[2,8,64,64]{3,2,1,0:T(8,128)(2,1)}, u32[]{:S(2)}) copy-start(bf16[2,8,64,64]{3,2,1,0:T(8,128)(2,1)} %top_coupling_ref.1) | copy-start | bytes 393220
  69.5 1.7 %copy-start.9 = (s32[16,16]{1,0:T(8,128)S(1)}, s32[16,16]{1,0:T(8,128)}, u32[]{:S(2)}) copy-start(s32[16,16]{1,0:T(8,128)} %recv_ref.1) | copy-start | bytes 3076
  69.5 1.7 %copy-start.10 = (s32[2,8]{1,0:T(2,128)S(1)}, s32[2,8]{1,0:T(2,128)}, u32[]{:S(2)}) copy-start(s32[2,8]{1,0:T(2,128)} %top_ref.1) | copy-start | bytes 196

commit v2 on v1

v2 whole, which is shorter than its diff:
```python
import functools

import jax
import jax.numpy as jnp
from jax import lax
from jax.experimental import pallas as pl
from jax.experimental.pallas import tpu as pltpu
from jax.sharding import PartitionSpec as P

BRANCH = 8
REACH = 16
SCALE = 0.07957747154594767
SOFTEN = 0.0025
BF, F32 = jnp.bfloat16, jnp.float32
NN = (((1,), (0,)), ((), ()))
NT = (((1,), (1,)), ((), ()))
TN = (((0,), (0,)), ((), ()))
VMEM = pl.BlockSpec(memory_space=pltpu.VMEM)
SMEM = pl.BlockSpec(memory_space=pltpu.SMEM)
FEATS = 16


def dot(a, b, dims=NN):
    return lax.dot_general(a, b, dims, preferred_element_type=F32)


def params(mib):
    return pltpu.CompilerParams(vmem_limit_bytes=mib * 2**20)


def cost(us):
    return pl.CostEstimate(flops=int(us * 1e9), bytes_accessed=int(us * 1e6), transcendentals=0)


def parts_of(x):
    high = x.astype(BF).astype(F32)
    mid = (x - high).astype(BF).astype(F32)
    low = (x - high - mid).astype(BF).astype(F32)
    return high, mid, low


def by_row(rows, values):
    which = lax.rem(rows, 5)
    out = jnp.zeros(rows.shape, F32)
    for j, value in enumerate(values):
        out = jnp.where(which == j, value, out)
    return jnp.where(rows < 15, out, 0.0)


def source_rows(rows, x, y, z, gain):
    wide = by_row(
        rows,
        (-2.0 * gain * x, -2.0 * gain * y, -2.0 * gain * z, gain, gain * (x * x + y * y + z * z + SOFTEN)),
    )
    high, mid, low = parts_of(wide)
    return jnp.where(rows < 5, high, jnp.where(rows < 10, mid, low)).astype(BF)


def pack_kernel(me_ref, in_hbm, geo_hbm, basis_hbm, transfer_hbm, send_hbm, shard_ref, left_ref, right_ref, own_ref, target_ref, in_ref, geo_ref, basis_ref, transfer_ref, send_ref, sems):
    pairs = ((geo_hbm, geo_ref), (in_hbm, in_ref), (basis_hbm, basis_ref), (transfer_hbm, transfer_ref), (send_hbm, send_ref))
    copies = [pltpu.make_async_copy(src, dst, sems.at[i]) for i, (src, dst) in enumerate(pairs)]
    for copy in copies:
        copy.start()
    leaves, rank, leaf = basis_ref.shape
    rhs, points = in_ref.shape
    center = (me_ref[0] + 1).astype(F32)
    copies[0].wait()
    x = geo_ref[0:1, :] - center
    y = geo_ref[1:2, :] - 0.5
    z = geo_ref[2:3, :] - 0.5
    scaled = SCALE * geo_ref[3:4, :]
    gain = 1.0 / (scaled * scaled)
    rows = lax.broadcasted_iota(jnp.int32, (FEATS, points), 0)
    right_ref[rhs:, :] = source_rows(rows, x - 1.0, y, z, gain)
    left_ref[rhs:, :] = source_rows(rows, x + 1.0, y, z, gain)
    own_ref[rhs:, :] = source_rows(rows, x, y, z, gain)
    high, mid, low = parts_of(by_row(rows, (x, y, z, x * x + y * y + z * z, jnp.ones_like(x))))
    target_ref[0:FEATS, :] = high.astype(BF)
    target_ref[FEATS : 2 * FEATS, :] = jnp.where(rows < 10, mid, 0.0).astype(BF)
    target_ref[2 * FEATS : 3 * FEATS, :] = jnp.where(rows < 5, low, 0.0).astype(BF)
    copies[1].wait()
    all_in = in_ref[...]
    right_ref[:rhs, :] = all_in
    left_ref[:rhs, :] = all_in
    own_ref[:rhs, :] = all_in

    for copy in copies[2:]:
        copy.wait()
    blank = jnp.zeros((rhs, leaf), BF)
    lanes = lax.broadcasted_iota(jnp.int32, (rank, 2 * rhs), 1)
    uppers = leaves // BRANCH
    upper = [jnp.zeros((rank, 2 * rhs), F32) for _ in range(uppers)]
    for pair in range(leaves // 2):
        a, b = 2 * pair, 2 * pair + 1
        xa = in_ref[:, a * leaf : (a + 1) * leaf]
        xb = in_ref[:, b * leaf : (b + 1) * leaf]
        weights = jnp.concatenate(
            [jnp.concatenate([xa, blank], axis=1), jnp.concatenate([blank, xb], axis=1)], axis=0
        )
        coef = dot(jnp.concatenate([basis_ref[a], basis_ref[b]], axis=1), weights, NT).astype(BF)
        shard_ref[pair * rank : (pair + 1) * rank, :] = coef
        both = jnp.concatenate(
            [jnp.where(lanes < rhs, coef, jnp.zeros_like(coef)), jnp.where(lanes < rhs, jnp.zeros_like(coef), coef)],
            axis=0,
        )
        moved = jnp.concatenate([transfer_ref[a], transfer_ref[b]], axis=0)
        upper[a // BRANCH] += dot(moved, both, TN)
    for p in range(0, uppers, 2):
        left = upper[p] + pltpu.roll(upper[p], rhs, 1)
        right = upper[p + 1] + pltpu.roll(upper[p + 1], rhs, 1)
        at = leaves // 2 * rank + p // 2 * rank
        shard_ref[at : at + rank, :] = jnp.where(lanes < rhs, left, right).astype(BF)
    at = (leaves + uppers) // 2 * rank
    shard_ref[at:, :] = jnp.zeros((shard_ref.shape[0] - at, 2 * rhs), BF)
    shard_ref[at : at + send_ref.shape[0], 0 : send_ref.shape[1]] = send_ref[...].astype(F32).astype(BF)


def near_kernel(count, first, me_ref, list_ref, own_ref, left_ref, right_ref, target_ref, out_ref, block_ref):
    wide, points = own_ref.shape
    rhs, some = out_ref.shape
    leaves, near = list_ref.shape
    leaf = points // leaves
    me = me_ref[0]
    start = me * leaves - REACH
    for side, ref in enumerate((left_ref, own_ref, right_ref)):
        for j in range(leaves):
            block_ref[side * leaves + j] = ref[:, j * leaf : (j + 1) * leaf]

    def blank(side):
        rows = lax.broadcasted_iota(jnp.int32, (wide - rhs, leaf), 0)
        for j in range(leaves):
            block_ref[side * leaves + j, rhs:, :] = jnp.where(rows == 4, 1.0, 0.0).astype(BF)

    pl.when(me == 0)(lambda: blank(0))
    pl.when(me == count - 1)(lambda: blank(2))

    def one(l, carry):
        at = pl.ds(pl.multiple_of(l * leaf, leaf), leaf)
        targets = target_ref[:, pl.ds(pl.multiple_of((first + l) * leaf, leaf), leaf)].T
        total = jnp.zeros((rhs, leaf), F32)
        for k in range(0, near, 4):
            ids = [list_ref[first + l, k + i] - start for i in range(4)]
            feats = jnp.concatenate([block_ref[i, rhs:, :] for i in ids], axis=1)
            feats = jnp.concatenate([feats, feats, feats], axis=0)
            green = lax.rsqrt(dot(targets, feats)).astype(BF)
            values = jnp.concatenate([block_ref[i, 0:rhs, :] for i in ids], axis=1)
            total = total + dot(values, green, NT)
        out_ref[:, at] = total
        return carry

    lax.fori_loop(0, some // leaf, one, 0)


def coupling_kernel(c_ref, out_ref):
    leaves, far, rank, _ = c_ref.shape

    def one(l, carry):
        for k in range(0, far, 2):
            out_ref[l, :, k * rank : (k + 2) * rank] = jnp.concatenate([c_ref[l, k], c_ref[l, k + 1]], axis=1)
        return carry

    lax.fori_loop(0, leaves, one, 0)


def far_kernel(pieces, nears, me_ref, recv_ref, top_ref, *refs):
    piece_refs, refs = refs[:pieces], refs[pieces:]
    near_refs, refs = refs[:nears], refs[nears:]
    coupling_ref, top_coupling_ref, transfer_ref, basis_ref, out_ref, all_ref, owner_vmem, owner_ref, sem = refs
    leaves, rank, leaf = basis_ref.shape
    rhs = out_ref.shape[0]
    far = recv_ref.shape[1]
    uppers, top = top_ref.shape
    me = me_ref[0]
    table_at = (leaves + uppers) // 2 * rank
    table_rows = all_ref.shape[1] - table_at
    rows = lax.broadcasted_iota(jnp.int32, (table_rows, 2 * rhs), 0)
    depth = piece_refs[0].shape[0]
    for j, ref in enumerate(piece_refs):
        for i in range(depth):
            table = ref[i, table_at:, :].astype(F32)
            mine = jnp.sum(jnp.where(rows == me, table, 0.0), axis=0, keepdims=True)
            p = j * depth + i
            owner_vmem[p : p + 1, :] = mine.astype(jnp.int32)
    copy = pltpu.make_async_copy(owner_vmem, owner_ref, sem)
    copy.start()
    for j, ref in enumerate(piece_refs):
        all_ref[j * depth : (j + 1) * depth, :, :] = ref[...]

    lanes = lax.broadcasted_iota(jnp.int32, (rank, 2 * rhs), 1)
    half_of = (lanes >= rhs).astype(jnp.int32)

    def panel(position, index, base):
        at = pl.multiple_of(base + (index >> 1) * rank, rank)
        both = all_ref[position, pl.ds(at, rank), :]
        return jnp.where(half_of == (index & 1), both, jnp.zeros_like(both))

    fields = []
    for p in range(uppers):
        total = jnp.zeros((rank, 2 * rhs), F32)
        for k in range(top):
            word = top_ref[p, k]
            total = total + dot(top_coupling_ref[p, k], panel(word >> 8, word & 255, leaves // 2 * rank))
        fields.append((total + pltpu.roll(total, rhs, 1)).astype(BF))
    copy.wait()

    step = leaves // nears
    for part, near_ref in enumerate(near_refs):
        for j in range(step):
            l = part * step + j
            total = jnp.zeros((rank, 2 * rhs), F32)
            for quad in range(far // 4):
                panels = []
                for k in range(4 * quad, 4 * quad + 4):
                    word = recv_ref[l, k]
                    position = word >> 8
                    panels.append(panel(position, owner_ref[position, word & 255], 0))
                total = total + dot(
                    coupling_ref[l, :, 4 * quad * rank : 4 * (quad + 1) * rank], jnp.concatenate(panels, axis=0)
                )
            total = total + pltpu.roll(total, rhs, 1)
            total = (total + dot(transfer_ref[l], fields[l // BRANCH])).astype(BF)
            out_ref[:, l * leaf : (l + 1) * leaf] = near_ref[:, j * leaf : (j + 1) * leaf] + dot(
                total[:, 0:rhs], basis_ref[l], TN
            )


def body(count, inputs, geometry, leaf_basis, transfer, leaf_coupling, top_coupling, near_list, recv_slot, send_leaf, top_source):
    leaves, leaf, rank = leaf_basis.shape
    rhs = inputs.shape[1]
    points = leaves * leaf
    far = recv_slot.shape[1]
    slots = send_leaf.shape[2]
    uppers = leaves // BRANCH
    me = lax.axis_index("leaf").astype(jnp.int32)
    me_list = me.reshape(1)
    in_t = inputs.T
    basis_t = leaf_basis.transpose(0, 2, 1)
    table_rows = -(-count // 16) * 16
    shard_rows = (leaves + uppers) // 2 * rank + table_rows
    wide = jax.ShapeDtypeStruct((rhs + FEATS, points), BF)
    staged = (in_t, geometry, basis_t, transfer, send_leaf[0])
    shard, to_left, to_right, own, targets = pl.pallas_call(
        pack_kernel,
        out_shape=(
            jax.ShapeDtypeStruct((shard_rows, 2 * rhs), BF),
            wide,
            wide,
            wide,
            jax.ShapeDtypeStruct((3 * FEATS, points), BF),
        ),
        in_specs=[SMEM] + [pl.BlockSpec(memory_space=pltpu.HBM)] * 5,
        out_specs=(VMEM,) * 5,
        scratch_shapes=[pltpu.VMEM(a.shape, a.dtype) for a in staged] + [pltpu.SemaphoreType.DMA((5,))],
        compiler_params=params(32),
        cost_estimate=cost(2),
        name="pack",
    )(me_list, *staged)

    def swap(x, bit):
        return lax.ppermute(x, "leaf", [(i, i ^ bit) for i in range(count)])

    base = shard[None]
    high = count // 2
    while high > 8:
        base = jnp.concatenate([base, swap(base, high)], axis=0)
        high //= 2
    piece = {0: base}
    piece[8] = swap(base, 8)
    piece[4] = swap(base, 4)
    left = lax.ppermute(to_right, "leaf", [(i, i + 1) for i in range(count - 1)])
    right = lax.ppermute(to_left, "leaf", [(i + 1, i) for i in range(count - 1)])
    piece[2] = swap(base, 2)
    piece[12] = swap(piece[8], 4)
    piece[6] = swap(piece[4], 2)
    piece[10] = swap(piece[8], 2)
    piece[14] = swap(piece[12], 2)
    for j in (0, 2, 4, 8, 6, 10, 12, 14):
        piece[j + 1] = swap(piece[j], 1)

    def place(device):
        gap = lax.bitwise_xor(device, me)
        top = gap >> 4
        deep = jnp.zeros_like(gap)
        bits = (count // 16).bit_length() - 1
        for i in range(bits):
            deep = deep + ((top >> (bits - 1 - i)) & 1) * (1 << i)
        return (gap & 15) * (count // 16) + deep

    recv_words = place(recv_slot // slots) * 256 + recv_slot % slots
    top_words = place(top_source // uppers) * 256 + top_source % uppers

    coupling = pl.pallas_call(
        coupling_kernel,
        out_shape=jax.ShapeDtypeStruct((leaves, rank, far * rank), BF),
        in_specs=[VMEM],
        out_specs=VMEM,
        compiler_params=params(32),
        cost_estimate=cost(2),
        name="coupling",
    )(leaf_coupling)

    chunks = 4
    some = leaves // chunks
    nears = [
        pl.pallas_call(
            functools.partial(near_kernel, count, c * some),
            out_shape=jax.ShapeDtypeStruct((rhs, some * leaf), F32),
            in_specs=[SMEM] * 2 + [VMEM] * 4,
            out_specs=VMEM,
            scratch_shapes=[pltpu.VMEM((leaves + 2 * REACH, rhs + FEATS, leaf), BF)],
            compiler_params=params(32),
            cost_estimate=cost(4),
            name=f"near{c}",
        )(me_list, near_list, own, left, right, targets)
        for c in range(chunks)
    ]

    out = pl.pallas_call(
        functools.partial(far_kernel, 16, chunks),
        out_shape=jax.ShapeDtypeStruct((rhs, points), F32),
        in_specs=[SMEM] * 3 + [VMEM] * (16 + chunks + 4),
        out_specs=VMEM,
        scratch_shapes=[
            pltpu.VMEM((count, shard_rows, 2 * rhs), BF),
            pltpu.VMEM((count, 2 * rhs), jnp.int32),
            pltpu.SMEM((count, 2 * rhs), jnp.int32),
            pltpu.SemaphoreType.DMA,
        ],
        compiler_params=params(48),
        cost_estimate=cost(6),
        name="far",
    )(me_list, recv_words, top_words, *[piece[j] for j in range(16)], *nears, coupling, top_coupling, transfer, basis_t)
    return out.T


def solution(mesh):
    spec = ("parts", "leaf")
    in_specs = (
        P(spec, None),
        P(None, spec),
        P(spec, None, None),
        P(spec, None, None),
        P(spec, None, None, None),
        P(spec, None, None, None),
        P(spec, None),
        P(spec, None),
        P(spec, None, None),
        P(spec, None),
    )
    step = functools.partial(body, mesh.shape["leaf"])
    return jax.shard_map(step, mesh=mesh, in_specs=in_specs, out_specs=P(spec, None), check_vma=False)
```

time: 84.9 us -> 57 us (0.67)
  the two profiles are of different devices: /device:TPU:13 before, /device:TPU:0 now
where the time goes in v2:
time: 57 us; the launch traced here: 56.7 us
  Pallas kernels  26.5 us (46%)
  starting transfers between devices  23.4 us (41%)
  local copies, waits for them, and re-layouts  4.74 us (8%)
  waiting for transfers between devices  1.82 us (3%)
    ppermute x15, starting transfers between devices, swap(): return lax.ppermute(x, 'leaf', [(i, i ^ bit) for i in range(count)])  20.8 us
    pallas_call x4, Pallas kernels, body(): pl.pallas_call(functools.partial(near_kernel, count, c * some), out_shape...  16.6 us
    pallas_call x1, Pallas kernels, body(): pl.pallas_call(functools.partial(far_kernel, 16, chunks), out_shape=jax.S...  7.22 us
    unnamed x24, local copies, waits for them, and re-layouts  4.74 us
    ppermute x15, waiting for transfers between devices, swap(): return lax.ppermute(x, 'leaf', [(i, i ^ bit) for i in range(count)])  1.81 us
    pallas_call x1, Pallas kernels, body(): pl.pallas_call(coupling_kernel, out_shape=jax.ShapeDtypeStruct((leaves, r...  1.64 us
    ppermute x1, starting transfers between devices, body(): lax.ppermute(to_right, 'leaf', [(i, i + 1) for i in range(count - 1)])  1.3 us
    ppermute x1, starting transfers between devices, body(): lax.ppermute(to_left, 'leaf', [(i + 1, i) for i in range(count - 1)])  1.29 us
  transfers between devices with their start and end apart: 17, of which 1 were waited for; matrix products, arithmetic and copies ran while one was open for 0% of the time, Pallas kernels for 32%

profile of v2, /device:TPU:0, one launch (start us, length us, event | category | flops | bytes accessed | tf_op | source)
XLA Modules:
  0.0 56.7 jit_solution(15430298856926847707)
XLA Ops:
  0.0 1.1 %copy-done.1 = bf16[2048,64]{0,1:T(8,128)(2,1)S(1)} copy-done((bf16[2048,64]{0,1:T(8,128)(2,1)S(1)}, bf16[2048,64]{0,1:T(8,128)(2,1)}, u32[]{:S(2)}) %copy-start.1) | copy-done | bytes 262168
  1.1 1.2 %copy-done.2 = bf16[16,128,64]{1,2,0:T(8,128)(2,1)S(1)} copy-done((bf16[16,128,64]{1,2,0:T(8,128)(2,1)S(1)}, bf16[16,128,64]{1,2,0:T(8,128)(2,1)}, u32[]{:S(2)}) %copy-start.2) | copy-done | bytes 262168
  2.3 0.9 %copy-done.4 = bf16[16,64,64]{2,1,0:T(8,128)(2,1)S(1)} copy-done((bf16[16,64,64]{2,1,0:T(8,128)(2,1)S(1)}, bf16[16,64,64]{2,1,0:T(8,128)(2,1)}, u32[]{:S(2)}) %copy-start.4) | copy-done | bytes 131096
  3.3 0.8 %copy-done.7 = f32[4,2048]{1,0:T(4,128)S(1)} copy-done((f32[4,2048]{1,0:T(4,128)S(1)}, f32[4,2048]{1,0:T(4,128)}, u32[]{:S(2)}) %copy-start.7) | copy-done | bytes 32792
  4.0 0.7 %copy-done.8 = s32[1,16,24]{2,1,0:T(8,128)S(1)} copy-done((s32[1,16,24]{2,1,0:T(8,128)S(1)}, s32[1,16,24]{2,1,0:T(8,128)}, u32[]{:S(2)}) %copy-start.8) | copy-done | bytes 1560
  4.7 1.1 %pack.1 = (bf16[592,128]{1,0:T(8,128)(2,1)S(1)}, bf16[80,2048]{1,0:T(8,128)(2,1)S(1)}, bf16[80,2048]{1,0:T(8,128)(2,1)S(1)}, bf16[80,2048]{1,0:T(8,128)(2,1)S(1)}, bf16[48,2048]{1,0:T(8,128)(2,1)S(1)}) custom-call(s32[1]{0:T(128)} %bitcast.me_ref, bf16[64,2048]{1,0:T(8,128)(2,1)S(1)} %bitcast.6, f32[4,2048]{1,0:T(4,128)S(1)} %copy-done.7, ...), custom_call_target="tpu_custom_call" | custom-call | flops 2000000000 | bytes 2000000 | tf_op jit(solution)/shard_map/pack/pallas_call | solution.py:242
  5.8 0.0 copy-start.9
  5.8 4.1 %collective-permute-start.7 = (bf16[1,592,128]{2,1,0:T(8,128)(2,1)S(1)}, bf16[1,592,128]{2,1,0:T(8,128)(2,1)S(1)}, u32[]{:S(2)}, u32[]{:S(2)}) collective-permute-start(bf16[1,592,128]{2,1,0:T(8,128)(2,1)S(1)} %bitcast.9), channel_id=1, source_target_pairs={{0,8},{1,9},{2,10},{3,11},{4,12},{5,13},{6,14},{7,15},{8,0},{9,1},... | collective-permute-start | bytes 454664 | tf_op jit(solution)/shard_map/ppermute | solution.py:260
  9.9 1.6 %collective-permute-start.3 = (bf16[1,592,128]{2,1,0:T(8,128)(2,1)S(1)}, bf16[1,592,128]{2,1,0:T(8,128)(2,1)S(1)}, u32[]{:S(2)}, u32[]{:S(2)}) collective-permute-start(bf16[1,592,128]{2,1,0:T(8,128)(2,1)S(1)} %bitcast.10), channel_id=1, source_target_pairs={{0,4},{1,5},{2,6},{3,7},{4,0},{5,1},{6,2},{7,3},{8,12},{9,13},{10,... | collective-permute-start | bytes 454664 | tf_op jit(solution)/shard_map/ppermute | solution.py:260
  11.5 1.5 %collective-permute-start.1 = (bf16[1,592,128]{2,1,0:T(8,128)(2,1)S(1)}, bf16[1,592,128]{2,1,0:T(8,128)(2,1)S(1)}, u32[]{:S(2)}, u32[]{:S(2)}) collective-permute-start(bf16[1,592,128]{2,1,0:T(8,128)(2,1)S(1)} %bitcast.11), channel_id=1, source_target_pairs={{0,2},{1,3},{2,0},{3,1},{4,6},{5,7},{6,4},{7,5},{8,10},{9,11},{10,... | collective-permute-start | bytes 454664 | tf_op jit(solution)/shard_map/ppermute | solution.py:260
  13.0 1.3 %collective-permute-start.15 = (bf16[80,2048]{1,0:T(8,128)(2,1)S(1)}, bf16[80,2048]{1,0:T(8,128)(2,1)S(1)}, u32[]{:S(2)}, u32[]{:S(2)}) collective-permute-start(bf16[80,2048]{1,0:T(8,128)(2,1)S(1)} %get-tuple-element.12), channel_id=1, source_target_pairs={{0,1},{1,2},{2,3},{3,4},{4,5},{5,6},{6,7},{7,8},{8,9},{9,10},{10,1... | collective-permute-start | bytes 983048 | tf_op jit(solution)/shard_map/ppermute | solution.py:270
  14.3 1.3 %collective-permute-start.16 = (bf16[80,2048]{1,0:T(8,128)(2,1)S(1)}, bf16[80,2048]{1,0:T(8,128)(2,1)S(1)}, u32[]{:S(2)}, u32[]{:S(2)}) collective-permute-start(bf16[80,2048]{1,0:T(8,128)(2,1)S(1)} %get-tuple-element.13), channel_id=1, source_target_pairs={{1,0},{2,1},{3,2},{4,3},{5,4},{6,5},{7,6},{8,7},{9,8},{10,9},{11,1... | collective-permute-start | bytes 983048 | tf_op jit(solution)/shard_map/ppermute | solution.py:271
  15.7 1.6 %coupling.1.refs_20_ = bf16[16,64,1024]{2,1,0:T(8,128)(2,1)S(1)} custom-call(bf16[16,16,64,64]{3,2,1,0:T(8,128)(2,1)S(1)} %copy-done), custom_call_target="tpu_custom_call" | custom-call | flops 2000000000 | bytes 2000000 | tf_op jit(solution)/shard_map/coupling/pallas_call | solution.py:292
  17.4 0.0 collective-permute-done.7.refs_8_
  17.4 1.9 %collective-permute-start = (bf16[1,592,128]{2,1,0:T(8,128)(2,1)S(1)}, bf16[1,592,128]{2,1,0:T(8,128)(2,1)S(1)}, u32[]{:S(2)}, u32[]{:S(2)}) collective-permute-start(bf16[1,592,128]{2,1,0:T(8,128)(2,1)S(1)} %bitcast.12), channel_id=1, source_target_pairs={{0,1},{1,0},{2,3},{3,2},{4,5},{5,4},{6,7},{7,6},{8,9},{9,8},{10,11... | collective-permute-start | bytes 454664 | tf_op jit(solution)/shard_map/ppermute | solution.py:260
  19.3 0.0 collective-permute-done.15.left_ref
  19.3 4.2 %collective-permute-start.11 = (bf16[1,592,128]{2,1,0:T(8,128)(2,1)S(1)}, bf16[1,592,128]{2,1,0:T(8,128)(2,1)S(1)}, u32[]{:S(2)}, u32[]{:S(2)}) collective-permute-start(bf16[1,592,128]{2,1,0:T(8,128)(2,1)S(1)} %collective-permute-done.7.refs_8_), channel_id=1, source_target_pairs={{0,4},{1,5},{2,6},{3,7},{4,0},{5,1},{6,2},{7,3},{8,12},{9,13},{10,... | collective-permute-start | bytes 454664 | tf_op jit(solution)/shard_map/ppermute | solution.py:260
  23.5 0.0 collective-permute-done.16.right_ref
  23.5 0.2 collective-permute-start.9
  23.7 4.1 %near3.1.refs_19_ = f32[64,512]{1,0:T(8,128)S(1)} custom-call(s32[1]{0:T(128)} %bitcast.me_ref, s32[16,24]{1,0:T(8,128)S(1)} %copy-done.9, bf16[80,2048]{1,0:T(8,128)(2,1)S(1)} %get-tuple-element.11.own_ref, bf16[80,2048]{1,0:T(8,128)(2,1)S(1)} %collective-permute-done.15.left_ref, bf16[80,2048]{1,0:T(8,128)(2,1)S(1)} %collective-permute-done.16.right_ref, ...), custom_call_target="tpu_custom_call" | custom-call | flops 4000000000 | bytes 4000000 | tf_op jit(solution)/shard_map/near3/pallas_call | solution.py:305
  27.8 4.1 %near2.1.refs_18_ = f32[64,512]{1,0:T(8,128)S(1)} custom-call(s32[1]{0:T(128)} %bitcast.me_ref, s32[16,24]{1,0:T(8,128)S(1)} %copy-done.9, bf16[80,2048]{1,0:T(8,128)(2,1)S(1)} %get-tuple-element.11.own_ref, bf16[80,2048]{1,0:T(8,128)(2,1)S(1)} %collective-permute-done.15.left_ref, bf16[80,2048]{1,0:T(8,128)(2,1)S(1)} %collective-permute-done.16.right_ref, ...), custom_call_target="tpu_custom_call" | custom-call | flops 4000000000 | bytes 4000000 | tf_op jit(solution)/shard_map/near2/pallas_call | solution.py:305
  32.0 0.0 collective-permute-done.3.refs_4_
  32.0 4.1 %collective-permute-start.8 = (bf16[1,592,128]{2,1,0:T(8,128)(2,1)S(1)}, bf16[1,592,128]{2,1,0:T(8,128)(2,1)S(1)}, u32[]{:S(2)}, u32[]{:S(2)}) collective-permute-start(bf16[1,592,128]{2,1,0:T(8,128)(2,1)S(1)} %collective-permute-done.7.refs_8_), channel_id=1, source_target_pairs={{0,1},{1,0},{2,3},{3,2},{4,5},{5,4},{6,7},{7,6},{8,9},{9,8},{10,11... | collective-permute-start | bytes 454664 | tf_op jit(solution)/shard_map/ppermute | solution.py:260
  36.1 0.0 collective-permute-done.1.refs_2_
  36.1 0.3 collective-permute-start.5
  36.4 0.0 collective-permute-done.refs_1_
  36.4 0.0 collective-permute-start.4
  36.4 0.0 collective-permute-done.11.refs_12_
  36.4 1.8 %collective-permute-start.13 = (bf16[1,592,128]{2,1,0:T(8,128)(2,1)S(1)}, bf16[1,592,128]{2,1,0:T(8,128)(2,1)S(1)}, u32[]{:S(2)}, u32[]{:S(2)}) collective-permute-start(bf16[1,592,128]{2,1,0:T(8,128)(2,1)S(1)} %collective-permute-done.11.refs_12_), channel_id=1, source_target_pairs={{0,2},{1,3},{2,0},{3,1},{4,6},{5,7},{6,4},{7,5},{8,10},{9,11},{10,... | collective-permute-start | bytes 454664 | tf_op jit(solution)/shard_map/ppermute | solution.py:260
  38.2 4.1 %near1.1.refs_17_ = f32[64,512]{1,0:T(8,128)S(1)} custom-call(s32[1]{0:T(128)} %bitcast.me_ref, s32[16,24]{1,0:T(8,128)S(1)} %copy-done.9, bf16[80,2048]{1,0:T(8,128)(2,1)S(1)} %get-tuple-element.11.own_ref, bf16[80,2048]{1,0:T(8,128)(2,1)S(1)} %collective-permute-done.15.left_ref, bf16[80,2048]{1,0:T(8,128)(2,1)S(1)} %collective-permute-done.16.right_ref, ...), custom_call_target="tpu_custom_call" | custom-call | flops 4000000000 | bytes 4000000 | tf_op jit(solution)/shard_map/near1/pallas_call | solution.py:305
  42.3 0.0 copy-start.3
  42.3 0.0 copy-start.5
  42.4 0.0 copy-start.6
  42.4 0.0 collective-permute-done.9.refs_10_
  42.4 0.2 collective-permute-start.2
  42.6 0.0 collective-permute-done.8.refs_9_
  42.6 0.4 collective-permute-start.12
  43.0 0.0 collective-permute-done.5.refs_6_
  43.0 0.1 collective-permute-start.10
  43.1 0.0 collective-permute-done.4.refs_5_
  43.1 0.4 collective-permute-start.6
  43.5 1.8 %collective-permute-done.13.refs_14_ = bf16[1,592,128]{2,1,0:T(8,128)(2,1)S(1)} collective-permute-done((bf16[1,592,128]{2,1,0:T(8,128)(2,1)S(1)}, bf16[1,592,128]{2,1,0:T(8,128)(2,1)S(1)}, u32[]{:S(2)}, u32[]{:S(2)}) %collective-permute-start.13) | collective-permute-done | bytes 151584 | tf_op jit(solution)/shard_map/ppermute | solution.py:260
  45.2 0.0 collective-permute-start.14
  45.3 4.1 %near0.1.refs_16_ = f32[64,512]{1,0:T(8,128)S(1)} custom-call(s32[1]{0:T(128)} %bitcast.me_ref, s32[16,24]{1,0:T(8,128)S(1)} %copy-done.9, bf16[80,2048]{1,0:T(8,128)(2,1)S(1)} %get-tuple-element.11.own_ref, bf16[80,2048]{1,0:T(8,128)(2,1)S(1)} %collective-permute-done.15.left_ref, bf16[80,2048]{1,0:T(8,128)(2,1)S(1)} %collective-permute-done.16.right_ref, ...), custom_call_target="tpu_custom_call" | custom-call | flops 4000000000 | bytes 4000000 | tf_op jit(solution)/shard_map/near0/pallas_call | solution.py:305
  49.4 0.0 collective-permute-done.2.refs_3_
  49.4 0.0 collective-permute-done.10.refs_11_
  49.4 0.0 collective-permute-done.6.refs_7_
  49.5 7.2 %far.1 = f32[64,2048]{1,0:T(8,128)} custom-call(s32[1]{0:T(128)} %bitcast.me_ref, s32[16,16]{1,0:T(8,128)S(1)} %fusion.3.recv_ref, s32[2,8]{1,0:T(2,128)S(1)} %fusion.5.top_ref, bf16[1,592,128]{2,1,0:T(8,128)(2,1)S(1)} %bitcast.13, bf16[1,592,128]{2,1,0:T(8,128)(2,1)S(1)} %collective-permute-done.refs_1_, ...), custom_call_target="tpu_custom_call" | custom-call | flops 6000000000 | bytes 6000000 | tf_op jit(solution)/shard_map/far/pallas_call | solution.py:318
  (19 shorter events, 0.1 us)
Async XLA Ops:
  0.0 15.7 %copy-start.11 = (s32[2,8]{1,0:T(2,128)S(1)}, s32[2,8]{1,0:T(2,128)}, u32[]{:S(2)}) copy-start(s32[2,8]{1,0:T(2,128)} %param.19) | copy-start | bytes 196
  0.0 15.7 %copy-start = (bf16[16,16,64,64]{3,2,1,0:T(8,128)(2,1)S(1)}, bf16[16,16,64,64]{3,2,1,0:T(8,128)(2,1)}, u32[]{:S(2)}) copy-start(bf16[16,16,64,64]{3,2,1,0:T(8,128)(2,1)} %c_ref.1) | copy-start | bytes 6291460
  0.0 1.1 %copy-start.1 = (bf16[2048,64]{0,1:T(8,128)(2,1)S(1)}, bf16[2048,64]{0,1:T(8,128)(2,1)}, u32[]{:S(2)}) copy-start(bf16[2048,64]{0,1:T(8,128)(2,1)} %param.10) | copy-start | bytes 786436
  1.1 1.2 %copy-start.2 = (bf16[16,128,64]{1,2,0:T(8,128)(2,1)S(1)}, bf16[16,128,64]{1,2,0:T(8,128)(2,1)}, u32[]{:S(2)}) copy-start(bf16[16,128,64]{1,2,0:T(8,128)(2,1)} %param.12) | copy-start | bytes 786436
  2.3 0.9 %copy-start.4 = (bf16[16,64,64]{2,1,0:T(8,128)(2,1)S(1)}, bf16[16,64,64]{2,1,0:T(8,128)(2,1)}, u32[]{:S(2)}) copy-start(bf16[16,64,64]{2,1,0:T(8,128)(2,1)} %refs_22_.1) | copy-start | bytes 393220
  3.3 0.8 %copy-start.7 = (f32[4,2048]{1,0:T(4,128)S(1)}, f32[4,2048]{1,0:T(4,128)}, u32[]{:S(2)}) copy-start(f32[4,2048]{1,0:T(4,128)} %geo_hbm.1) | copy-start | bytes 98308
  4.0 0.7 %copy-start.8 = (s32[1,16,24]{2,1,0:T(8,128)S(1)}, s32[1,16,24]{2,1,0:T(8,128)}, u32[]{:S(2)}) copy-start(s32[1,16,24]{2,1,0:T(8,128)} %param.18) | copy-start | bytes 4612
  4.7 10.9 %copy-start.10 = (s32[16,16]{1,0:T(8,128)S(1)}, s32[16,16]{1,0:T(8,128)}, u32[]{:S(2)}) copy-start(s32[16,16]{1,0:T(8,128)} %param.17) | copy-start | bytes 3076
  5.8 17.9 %copy-start.9 = (s32[16,24]{1,0:T(8,128)S(1)}, s32[16,24]{1,0:T(8,128)}, u32[]{:S(2)}) copy-start(s32[16,24]{1,0:T(8,128)} %list_ref.7) | copy-start | bytes 4612
  5.8 11.5 %collective-permute-start.7 = (bf16[1,592,128]{2,1,0:T(8,128)(2,1)S(1)}, bf16[1,592,128]{2,1,0:T(8,128)(2,1)S(1)}, u32[]{:S(2)}, u32[]{:S(2)}) collective-permute-start(bf16[1,592,128]{2,1,0:T(8,128)(2,1)S(1)} %bitcast.9), channel_id=1, source_target_pairs={{0,8},{1,9},{2,10},{3,11},{4,12},{5,13},{6,14},{7,15},{8,0},{9,1},... | collective-permute-start | bytes 454664 | tf_op jit(solution)/shard_map/ppermute | solution.py:260
  9.9 22.0 %collective-permute-start.3 = (bf16[1,592,128]{2,1,0:T(8,128)(2,1)S(1)}, bf16[1,592,128]{2,1,0:T(8,128)(2,1)S(1)}, u32[]{:S(2)}, u32[]{:S(2)}) collective-permute-start(bf16[1,592,128]{2,1,0:T(8,128)(2,1)S(1)} %bitcast.10), channel_id=1, source_target_pairs={{0,4},{1,5},{2,6},{3,7},{4,0},{5,1},{6,2},{7,3},{8,12},{9,13},{10,... | collective-permute-start | bytes 454664 | tf_op jit(solution)/shard_map/ppermute | solution.py:260
  11.5 24.6 %collective-permute-start.1 = (bf16[1,592,128]{2,1,0:T(8,128)(2,1)S(1)}, bf16[1,592,128]{2,1,0:T(8,128)(2,1)S(1)}, u32[]{:S(2)}, u32[]{:S(2)}) collective-permute-start(bf16[1,592,128]{2,1,0:T(8,128)(2,1)S(1)} %bitcast.11), channel_id=1, source_target_pairs={{0,2},{1,3},{2,0},{3,1},{4,6},{5,7},{6,4},{7,5},{8,10},{9,11},{10,... | collective-permute-start | bytes 454664 | tf_op jit(solution)/shard_map/ppermute | solution.py:260
  13.0 6.3 %collective-permute-start.15 = (bf16[80,2048]{1,0:T(8,128)(2,1)S(1)}, bf16[80,2048]{1,0:T(8,128)(2,1)S(1)}, u32[]{:S(2)}, u32[]{:S(2)}) collective-permute-start(bf16[80,2048]{1,0:T(8,128)(2,1)S(1)} %get-tuple-element.12), channel_id=1, source_target_pairs={{0,1},{1,2},{2,3},{3,4},{4,5},{5,6},{6,7},{7,8},{8,9},{9,10},{10,1... | collective-permute-start | bytes 983048 | tf_op jit(solution)/shard_map/ppermute | solution.py:270
  14.3 9.1 %collective-permute-start.16 = (bf16[80,2048]{1,0:T(8,128)(2,1)S(1)}, bf16[80,2048]{1,0:T(8,128)(2,1)S(1)}, u32[]{:S(2)}, u32[]{:S(2)}) collective-permute-start(bf16[80,2048]{1,0:T(8,128)(2,1)S(1)} %get-tuple-element.13), channel_id=1, source_target_pairs={{1,0},{2,1},{3,2},{4,3},{5,4},{6,5},{7,6},{8,7},{9,8},{10,9},{11,1... | collective-permute-start | bytes 983048 | tf_op jit(solution)/shard_map/ppermute | solution.py:271
  17.4 19.0 %collective-permute-start = (bf16[1,592,128]{2,1,0:T(8,128)(2,1)S(1)}, bf16[1,592,128]{2,1,0:T(8,128)(2,1)S(1)}, u32[]{:S(2)}, u32[]{:S(2)}) collective-permute-start(bf16[1,592,128]{2,1,0:T(8,128)(2,1)S(1)} %bitcast.12), channel_id=1, source_target_pairs={{0,1},{1,0},{2,3},{3,2},{4,5},{5,4},{6,7},{7,6},{8,9},{9,8},{10,11... | collective-permute-start | bytes 454664 | tf_op jit(solution)/shard_map/ppermute | solution.py:260
  19.3 17.1 %collective-permute-start.11 = (bf16[1,592,128]{2,1,0:T(8,128)(2,1)S(1)}, bf16[1,592,128]{2,1,0:T(8,128)(2,1)S(1)}, u32[]{:S(2)}, u32[]{:S(2)}) collective-permute-start(bf16[1,592,128]{2,1,0:T(8,128)(2,1)S(1)} %collective-permute-done.7.refs_8_), channel_id=1, source_target_pairs={{0,4},{1,5},{2,6},{3,7},{4,0},{5,1},{6,2},{7,3},{8,12},{9,13},{10,... | collective-permute-start | bytes 454664 | tf_op jit(solution)/shard_map/ppermute | solution.py:260
  23.5 18.9 %collective-permute-start.9 = (bf16[1,592,128]{2,1,0:T(8,128)(2,1)S(1)}, bf16[1,592,128]{2,1,0:T(8,128)(2,1)S(1)}, u32[]{:S(2)}, u32[]{:S(2)}) collective-permute-start(bf16[1,592,128]{2,1,0:T(8,128)(2,1)S(1)} %collective-permute-done.7.refs_8_), channel_id=1, source_target_pairs={{0,2},{1,3},{2,0},{3,1},{4,6},{5,7},{6,4},{7,5},{8,10},{9,11},{10,... | collective-permute-start | bytes 454664 | tf_op jit(solution)/shard_map/ppermute | solution.py:260
  32.0 10.6 %collective-permute-start.8 = (bf16[1,592,128]{2,1,0:T(8,128)(2,1)S(1)}, bf16[1,592,128]{2,1,0:T(8,128)(2,1)S(1)}, u32[]{:S(2)}, u32[]{:S(2)}) collective-permute-start(bf16[1,592,128]{2,1,0:T(8,128)(2,1)S(1)} %collective-permute-done.7.refs_8_), channel_id=1, source_target_pairs={{0,1},{1,0},{2,3},{3,2},{4,5},{5,4},{6,7},{7,6},{8,9},{9,8},{10,11... | collective-permute-start | bytes 454664 | tf_op jit(solution)/shard_map/ppermute | solution.py:260
  36.1 6.9 %collective-permute-start.5 = (bf16[1,592,128]{2,1,0:T(8,128)(2,1)S(1)}, bf16[1,592,128]{2,1,0:T(8,128)(2,1)S(1)}, u32[]{:S(2)}, u32[]{:S(2)}) collective-permute-start(bf16[1,592,128]{2,1,0:T(8,128)(2,1)S(1)} %collective-permute-done.3.refs_4_), channel_id=1, source_target_pairs={{0,2},{1,3},{2,0},{3,1},{4,6},{5,7},{6,4},{7,5},{8,10},{9,11},{10,... | collective-permute-start | bytes 454664 | tf_op jit(solution)/shard_map/ppermute | solution.py:260
  36.4 6.7 %collective-permute-start.4 = (bf16[1,592,128]{2,1,0:T(8,128)(2,1)S(1)}, bf16[1,592,128]{2,1,0:T(8,128)(2,1)S(1)}, u32[]{:S(2)}, u32[]{:S(2)}) collective-permute-start(bf16[1,592,128]{2,1,0:T(8,128)(2,1)S(1)} %collective-permute-done.3.refs_4_), channel_id=1, source_target_pairs={{0,1},{1,0},{2,3},{3,2},{4,5},{5,4},{6,7},{7,6},{8,9},{9,8},{10,11... | collective-permute-start | bytes 454664 | tf_op jit(solution)/shard_map/ppermute | solution.py:260
  36.4 8.9 %collective-permute-start.13 = (bf16[1,592,128]{2,1,0:T(8,128)(2,1)S(1)}, bf16[1,592,128]{2,1,0:T(8,128)(2,1)S(1)}, u32[]{:S(2)}, u32[]{:S(2)}) collective-permute-start(bf16[1,592,128]{2,1,0:T(8,128)(2,1)S(1)} %collective-permute-done.11.refs_12_), channel_id=1, source_target_pairs={{0,2},{1,3},{2,0},{3,1},{4,6},{5,7},{6,4},{7,5},{8,10},{9,11},{10,... | collective-permute-start | bytes 454664 | tf_op jit(solution)/shard_map/ppermute | solution.py:260
  42.3 7.1 %copy-start.3 = (bf16[16,128,64]{1,2,0:T(8,128)(2,1)S(1)}, bf16[16,128,64]{1,2,0:T(8,128)(2,1)}, u32[]{:S(2)}) copy-start(bf16[16,128,64]{1,2,0:T(8,128)(2,1)} %param.12) | copy-start | bytes 786436
  42.3 7.1 %copy-start.5 = (bf16[16,64,64]{2,1,0:T(8,128)(2,1)S(1)}, bf16[16,64,64]{2,1,0:T(8,128)(2,1)}, u32[]{:S(2)}) copy-start(bf16[16,64,64]{2,1,0:T(8,128)(2,1)} %refs_22_.1) | copy-start | bytes 393220
  42.4 7.1 %copy-start.6 = (bf16[2,8,64,64]{3,2,1,0:T(8,128)(2,1)S(1)}, bf16[2,8,64,64]{3,2,1,0:T(8,128)(2,1)}, u32[]{:S(2)}) copy-start(bf16[2,8,64,64]{3,2,1,0:T(8,128)(2,1)} %refs_21_.1) | copy-start | bytes 393220
  42.4 7.0 %collective-permute-start.2 = (bf16[1,592,128]{2,1,0:T(8,128)(2,1)S(1)}, bf16[1,592,128]{2,1,0:T(8,128)(2,1)S(1)}, u32[]{:S(2)}, u32[]{:S(2)}) collective-permute-start(bf16[1,592,128]{2,1,0:T(8,128)(2,1)S(1)} %collective-permute-done.1.refs_2_), channel_id=1, source_target_pairs={{0,1},{1,0},{2,3},{3,2},{4,5},{5,4},{6,7},{7,6},{8,9},{9,8},{10,11... | collective-permute-start | bytes 454664 | tf_op jit(solution)/shard_map/ppermute | solution.py:260
  42.6 6.8 %collective-permute-start.12 = (bf16[1,592,128]{2,1,0:T(8,128)(2,1)S(1)}, bf16[1,592,128]{2,1,0:T(8,128)(2,1)S(1)}, u32[]{:S(2)}, u32[]{:S(2)}) collective-permute-start(bf16[1,592,128]{2,1,0:T(8,128)(2,1)S(1)} %collective-permute-done.11.refs_12_), channel_id=1, source_target_pairs={{0,1},{1,0},{2,3},{3,2},{4,5},{5,4},{6,7},{7,6},{8,9},{9,8},{10,11... | collective-permute-start | bytes 454664 | tf_op jit(solution)/shard_map/ppermute | solution.py:260
  43.0 6.5 %collective-permute-start.10 = (bf16[1,592,128]{2,1,0:T(8,128)(2,1)S(1)}, bf16[1,592,128]{2,1,0:T(8,128)(2,1)S(1)}, u32[]{:S(2)}, u32[]{:S(2)}) collective-permute-start(bf16[1,592,128]{2,1,0:T(8,128)(2,1)S(1)} %collective-permute-done.9.refs_10_), channel_id=1, source_target_pairs={{0,1},{1,0},{2,3},{3,2},{4,5},{5,4},{6,7},{7,6},{8,9},{9,8},{10,11... | collective-permute-start | bytes 454664 | tf_op jit(solution)/shard_map/ppermute | solution.py:260
  43.1 6.3 %collective-permute-start.6 = (bf16[1,592,128]{2,1,0:T(8,128)(2,1)S(1)}, bf16[1,592,128]{2,1,0:T(8,128)(2,1)S(1)}, u32[]{:S(2)}, u32[]{:S(2)}) collective-permute-start(bf16[1,592,128]{2,1,0:T(8,128)(2,1)S(1)} %collective-permute-done.5.refs_6_), channel_id=1, source_target_pairs={{0,1},{1,0},{2,3},{3,2},{4,5},{5,4},{6,7},{7,6},{8,9},{9,8},{10,11... | collective-permute-start | bytes 454664 | tf_op jit(solution)/shard_map/ppermute | solution.py:260
  45.2 4.2 %collective-permute-start.14 = (bf16[1,592,128]{2,1,0:T(8,128)(2,1)S(1)}, bf16[1,592,128]{2,1,0:T(8,128)(2,1)S(1)}, u32[]{:S(2)}, u32[]{:S(2)}) collective-permute-start(bf16[1,592,128]{2,1,0:T(8,128)(2,1)S(1)} %collective-permute-done.13.refs_14_), channel_id=1, source_target_pairs={{0,1},{1,0},{2,3},{3,2},{4,5},{5,4},{6,7},{7,6},{8,9},{9,8},{10,11... | collective-permute-start | bytes 454664 | tf_op jit(solution)/shard_map/ppermute | solution.py:260

commit v3 on v2

--- a/solution.py
+++ b/solution.py
@@ -16,6 +16,7 @@
 NT = (((1,), (1,)), ((), ()))
 TN = (((0,), (0,)), ((), ()))
 VMEM = pl.BlockSpec(memory_space=pltpu.VMEM)
+ANY = pl.BlockSpec(memory_space=pl.ANY)
 SMEM = pl.BlockSpec(memory_space=pltpu.SMEM)
 FEATS = 16
 
@@ -56,7 +57,7 @@
     return jnp.where(rows < 5, high, jnp.where(rows < 10, mid, low)).astype(BF)
 
 
-def pack_kernel(me_ref, in_hbm, geo_hbm, basis_hbm, transfer_hbm, send_hbm, shard_ref, left_ref, right_ref, own_ref, target_ref, in_ref, geo_ref, basis_ref, transfer_ref, send_ref, sems):
+def pack_kernel(me_ref, in_hbm, geo_hbm, basis_hbm, transfer_hbm, send_hbm, shard_ref, inner_ref, outer_ref, own_ref, target_ref, in_ref, geo_ref, basis_ref, transfer_ref, send_ref, sems):
     pairs = ((geo_hbm, geo_ref), (in_hbm, in_ref), (basis_hbm, basis_ref), (transfer_hbm, transfer_ref), (send_hbm, send_ref))
     copies = [pltpu.make_async_copy(src, dst, sems.at[i]) for i, (src, dst) in enumerate(pairs)]
     for copy in copies:
@@ -71,17 +72,19 @@
     scaled = SCALE * geo_ref[3:4, :]
     gain = 1.0 / (scaled * scaled)
     rows = lax.broadcasted_iota(jnp.int32, (FEATS, points), 0)
-    right_ref[rhs:, :] = source_rows(rows, x - 1.0, y, z, gain)
-    left_ref[rhs:, :] = source_rows(rows, x + 1.0, y, z, gain)
+    side = (1 - 2 * (me_ref[0] & 1)).astype(F32)
+    inner_ref[rhs:, :] = source_rows(rows, x - side, y, z, gain)
+    outer_ref[rhs:, :] = source_rows(rows, x + side, y, z, gain)
     own_ref[rhs:, :] = source_rows(rows, x, y, z, gain)
     high, mid, low = parts_of(by_row(rows, (x, y, z, x * x + y * y + z * z, jnp.ones_like(x))))
     target_ref[0:FEATS, :] = high.astype(BF)
     target_ref[FEATS : 2 * FEATS, :] = jnp.where(rows < 10, mid, 0.0).astype(BF)
     target_ref[2 * FEATS : 3 * FEATS, :] = jnp.where(rows < 5, low, 0.0).astype(BF)
+    target_ref[3 * FEATS :, :] = jnp.zeros((FEATS, points), BF)
     copies[1].wait()
     all_in = in_ref[...]
-    right_ref[:rhs, :] = all_in
-    left_ref[:rhs, :] = all_in
+    inner_ref[:rhs, :] = all_in
+    outer_ref[:rhs, :] = all_in
     own_ref[:rhs, :] = all_in
 
     for copy in copies[2:]:
@@ -115,16 +118,17 @@
     shard_ref[at : at + send_ref.shape[0], 0 : send_ref.shape[1]] = send_ref[...].astype(F32).astype(BF)
 
 
-def near_kernel(count, first, me_ref, list_ref, own_ref, left_ref, right_ref, target_ref, out_ref, block_ref):
+def near_kernel(count, first, me_ref, list_ref, own_ref, inner_ref, outer_ref, target_ref, out_ref, block_ref):
     wide, points = own_ref.shape
     rhs, some = out_ref.shape
     leaves, near = list_ref.shape
     leaf = points // leaves
     me = me_ref[0]
     start = me * leaves - REACH
-    for side, ref in enumerate((left_ref, own_ref, right_ref)):
+    odd = me & 1
+    for base, ref in ((2 * (1 - odd) * leaves, inner_ref), (leaves, own_ref), (2 * odd * leaves, outer_ref)):
         for j in range(leaves):
-            block_ref[side * leaves + j] = ref[:, j * leaf : (j + 1) * leaf]
+            block_ref[base + j] = ref[:, j * leaf : (j + 1) * leaf]
 
     def blank(side):
         rows = lax.broadcasted_iota(jnp.int32, (wide - rhs, leaf), 0)
@@ -134,25 +138,47 @@
     pl.when(me == 0)(lambda: blank(0))
     pl.when(me == count - 1)(lambda: blank(2))
 
-    def one(l, carry):
-        at = pl.ds(pl.multiple_of(l * leaf, leaf), leaf)
-        targets = target_ref[:, pl.ds(pl.multiple_of((first + l) * leaf, leaf), leaf)].T
-        total = jnp.zeros((rhs, leaf), F32)
-        for k in range(0, near, 4):
-            ids = [list_ref[first + l, k + i] - start for i in range(4)]
-            feats = jnp.concatenate([block_ref[i, rhs:, :] for i in ids], axis=1)
-            feats = jnp.concatenate([feats, feats, feats], axis=0)
-            green = lax.rsqrt(dot(targets, feats)).astype(BF)
-            values = jnp.concatenate([block_ref[i, 0:rhs, :] for i in ids], axis=1)
-            total = total + dot(values, green, NT)
-        out_ref[:, at] = total
-        return carry
-
-    lax.fori_loop(0, some // leaf, one, 0)
-
-
-def coupling_kernel(c_ref, out_ref):
+    lanes = lax.broadcasted_iota(jnp.int32, (leaf, 2 * rhs), 1)
+    empty = jnp.zeros((4 * FEATS, leaf), BF)
+    blank_tile = jnp.zeros((leaf, leaf), BF)
+    for l in range(some // leaf):
+        rows = target_ref[:, (first + l) * leaf : (first + l + 1) * leaf]
+        low = jnp.concatenate([rows, empty], axis=0).T
+        high = jnp.concatenate([empty, rows], axis=0).T
+        targets = jnp.concatenate(
+            [
+                jnp.concatenate(two, axis=1)
+                for two in ((low, blank_tile), (high, blank_tile), (blank_tile, low), (blank_tile, high))
+            ],
+            axis=0,
+        )
+        total = jnp.zeros((leaf, 2 * rhs), F32)
+        for k in range(0, near, 8):
+            ids = [list_ref[first + l, k + i] - start for i in range(8)]
+            feats, values = [], []
+            for a, b in zip(ids[0::2], ids[1::2], strict=True):
+                feats += [jnp.concatenate([block_ref[a, rhs:, :], block_ref[b, rhs:, :]], axis=1)] * 4
+                values.append(jnp.concatenate([block_ref[a, 0:rhs, :], block_ref[b, 0:rhs, :]], axis=1))
+            green = lax.rsqrt(dot(targets, jnp.concatenate(feats, axis=0))).astype(BF)
+            out = dot(green, jnp.concatenate(values, axis=0), NT)
+            total = total + jnp.where(lanes < rhs, out[0:leaf, 0 : 2 * rhs], out[leaf : 2 * leaf, 0 : 2 * rhs])
+            total = total + jnp.where(lanes < rhs, out[2 * leaf : 3 * leaf, 2 * rhs :], out[3 * leaf :, 2 * rhs :])
+        turned = total.T
+        out_ref[:, l * leaf : (l + 1) * leaf] = turned[0:rhs] + turned[rhs:]
+
+
+def merge_kernel(a_ref, b_ref, out_ref):
+    deep = a_ref.shape[0]
+    out_ref[0:deep] = a_ref[...]
+    out_ref[deep:] = b_ref[...]
+
+
+def coupling_kernel(_, c_ref, top_ref, out_ref, top_out_ref):
     leaves, far, rank, _ = c_ref.shape
+    uppers, top, _, _ = top_ref.shape
+    for p in range(uppers):
+        for k in range(0, top, 2):
+            top_out_ref[p, :, k * rank : (k + 2) * rank] = jnp.concatenate([top_ref[p, k], top_ref[p, k + 1]], axis=1)
 
     def one(l, carry):
         for k in range(0, far, 2):
@@ -194,33 +220,36 @@
         both = all_ref[position, pl.ds(at, rank), :]
         return jnp.where(half_of == (index & 1), both, jnp.zeros_like(both))
 
-    fields = []
+    def sum_of(left, words, base):
+        total = jnp.zeros((rank, 2 * rhs), F32)
+        for quad in range(0, len(words), 4):
+            panels = jnp.concatenate([panel(*word, base) for word in words[quad : quad + 4]], axis=0)
+            total = total + dot(left[:, quad * rank : (quad + 4) * rank], panels)
+        return total + pltpu.roll(total, rhs, 1)
+
+    moved = []
     for p in range(uppers):
-        total = jnp.zeros((rank, 2 * rhs), F32)
-        for k in range(top):
-            word = top_ref[p, k]
-            total = total + dot(top_coupling_ref[p, k], panel(word >> 8, word & 255, leaves // 2 * rank))
-        fields.append((total + pltpu.roll(total, rhs, 1)).astype(BF))
+        words = [top_ref[p, k] for k in range(top)]
+        field = sum_of(top_coupling_ref[p], [(word >> 8, word & 255) for word in words], leaves // 2 * rank).astype(BF)
+        down = transfer_ref[p * BRANCH : (p + 1) * BRANCH].reshape(BRANCH * rank, rank)
+        moved.append(dot(down, field))
     copy.wait()
 
     step = leaves // nears
-    for part, near_ref in enumerate(near_refs):
-        for j in range(step):
-            l = part * step + j
-            total = jnp.zeros((rank, 2 * rhs), F32)
-            for quad in range(far // 4):
-                panels = []
-                for k in range(4 * quad, 4 * quad + 4):
-                    word = recv_ref[l, k]
-                    position = word >> 8
-                    panels.append(panel(position, owner_ref[position, word & 255], 0))
-                total = total + dot(
-                    coupling_ref[l, :, 4 * quad * rank : 4 * (quad + 1) * rank], jnp.concatenate(panels, axis=0)
-                )
-            total = total + pltpu.roll(total, rhs, 1)
-            total = (total + dot(transfer_ref[l], fields[l // BRANCH])).astype(BF)
-            out_ref[:, l * leaf : (l + 1) * leaf] = near_ref[:, j * leaf : (j + 1) * leaf] + dot(
-                total[:, 0:rhs], basis_ref[l], TN
+    for l in range(0, leaves, 2):
+        totals = []
+        for i in (l, l + 1):
+            words = [recv_ref[i, k] for k in range(far)]
+            words = [(word >> 8, owner_ref[word >> 8, word & 255]) for word in words]
+            at = i % BRANCH * rank
+            totals.append(sum_of(coupling_ref[i], words, 0) + moved[i // BRANCH][at : at + rank])
+        pair = jnp.where(lanes < rhs, totals[0], totals[1]).T.astype(BF)
+        out = dot(pair, jnp.concatenate([basis_ref[l], basis_ref[l + 1]], axis=1))
+        for i in range(2):
+            j = (l + i) % step
+            out_ref[:, (l + i) * leaf : (l + i + 1) * leaf] = (
+                near_refs[l // step][:, j * leaf : (j + 1) * leaf]
+                + out[i * rhs : (i + 1) * rhs, i * leaf : (i + 1) * leaf]
             )
 
 
@@ -239,19 +268,19 @@
     shard_rows = (leaves + uppers) // 2 * rank + table_rows
     wide = jax.ShapeDtypeStruct((rhs + FEATS, points), BF)
     staged = (in_t, geometry, basis_t, transfer, send_leaf[0])
-    shard, to_left, to_right, own, targets = pl.pallas_call(
+    shard, to_inner, to_outer, own, targets = pl.pallas_call(
         pack_kernel,
         out_shape=(
             jax.ShapeDtypeStruct((shard_rows, 2 * rhs), BF),
             wide,
             wide,
             wide,
-            jax.ShapeDtypeStruct((3 * FEATS, points), BF),
+            jax.ShapeDtypeStruct((4 * FEATS, points), BF),
         ),
         in_specs=[SMEM] + [pl.BlockSpec(memory_space=pltpu.HBM)] * 5,
         out_specs=(VMEM,) * 5,
         scratch_shapes=[pltpu.VMEM(a.shape, a.dtype) for a in staged] + [pltpu.SemaphoreType.DMA((5,))],
-        compiler_params=params(32),
+        compiler_params=params(60),
         cost_estimate=cost(2),
         name="pack",
     )(me_list, *staged)
@@ -264,40 +293,52 @@
     while high > 8:
         base = jnp.concatenate([base, swap(base, high)], axis=0)
         high //= 2
-    piece = {0: base}
-    piece[8] = swap(base, 8)
-    piece[4] = swap(base, 4)
-    left = lax.ppermute(to_right, "leaf", [(i, i + 1) for i in range(count - 1)])
-    right = lax.ppermute(to_left, "leaf", [(i + 1, i) for i in range(count - 1)])
-    piece[2] = swap(base, 2)
-    piece[12] = swap(piece[8], 4)
+    deep = base.shape[0]
+    far_side = swap(base, 8)
+    inner = swap(to_inner, 1)
+    outer = lax.ppermute(
+        to_outer, "leaf", [pair for i in range(1, count - 1, 2) for pair in ((i, i + 1), (i + 1, i))]
+    )
+    both = pl.pallas_call(
+        merge_kernel,
+        out_shape=jax.ShapeDtypeStruct((2 * deep, *base.shape[1:]), BF),
+        in_specs=[VMEM] * 2,
+        out_specs=VMEM,
+        compiler_params=params(32),
+        cost_estimate=cost(1),
+        name="merge",
+    )(base, far_side)
+    piece = {0: both}
+    piece[4] = swap(both, 4)
+    piece[2] = swap(both, 2)
     piece[6] = swap(piece[4], 2)
-    piece[10] = swap(piece[8], 2)
-    piece[14] = swap(piece[12], 2)
-    for j in (0, 2, 4, 8, 6, 10, 12, 14):
+    for j in (0, 4, 2, 6):
         piece[j + 1] = swap(piece[j], 1)
 
     def place(device):
         gap = lax.bitwise_xor(device, me)
         top = gap >> 4
-        deep = jnp.zeros_like(gap)
-        bits = (count // 16).bit_length() - 1
+        out = (gap & 7) * (2 * deep) + ((gap >> 3) & 1) * deep
+        bits = deep.bit_length() - 1
         for i in range(bits):
-            deep = deep + ((top >> (bits - 1 - i)) & 1) * (1 << i)
-        return (gap & 15) * (count // 16) + deep
+            out = out + ((top >> (bits - 1 - i)) & 1) * (1 << i)
+        return out
 
     recv_words = place(recv_slot // slots) * 256 + recv_slot % slots
     top_words = place(top_source // uppers) * 256 + top_source % uppers
 
-    coupling = pl.pallas_call(
+    coupling, top_wide = pl.pallas_call(
         coupling_kernel,
-        out_shape=jax.ShapeDtypeStruct((leaves, rank, far * rank), BF),
-        in_specs=[VMEM],
-        out_specs=VMEM,
+        out_shape=(
+            jax.ShapeDtypeStruct((leaves, rank, far * rank), BF),
+            jax.ShapeDtypeStruct((uppers, rank, top_source.shape[1] * rank), BF),
+        ),
+        in_specs=[ANY, VMEM, VMEM],
+        out_specs=(VMEM,) * 2,
         compiler_params=params(32),
         cost_estimate=cost(2),
         name="coupling",
-    )(leaf_coupling)
+    )(both, leaf_coupling, top_coupling)
 
     chunks = 4
     some = leaves // chunks
@@ -309,16 +350,16 @@
             out_specs=VMEM,
             scratch_shapes=[pltpu.VMEM((leaves + 2 * REACH, rhs + FEATS, leaf), BF)],
             compiler_params=params(32),
-            cost_estimate=cost(4),
+            cost_estimate=cost(2.5),
             name=f"near{c}",
-        )(me_list, near_list, own, left, right, targets)
+        )(me_list, near_list, own, inner, outer, targets)
         for c in range(chunks)
     ]
 
     out = pl.pallas_call(
-        functools.partial(far_kernel, 16, chunks),
+        functools.partial(far_kernel, len(piece), chunks),
         out_shape=jax.ShapeDtypeStruct((rhs, points), F32),
-        in_specs=[SMEM] * 3 + [VMEM] * (16 + chunks + 4),
+        in_specs=[SMEM] * 3 + [VMEM] * (len(piece) + chunks + 4),
         out_specs=VMEM,
         scratch_shapes=[
             pltpu.VMEM((count, shard_rows, 2 * rhs), BF),
@@ -329,7 +370,7 @@
         compiler_params=params(48),
         cost_estimate=cost(6),
         name="far",
-    )(me_list, recv_words, top_words, *[piece[j] for j in range(16)], *nears, coupling, top_coupling, transfer, basis_t)
+    )(me_list, recv_words, top_words, *[piece[j] for j in range(len(piece))], *nears, coupling, top_wide, transfer, basis_t)
     return out.T
 
 

time: 57 us -> 44.3 us (0.78)
  starting transfers between devices: 23.4 us -> 8.61 us
  waiting for transfers between devices: 1.82 us -> 10.3 us
  Pallas kernels: 26.5 us -> 21.6 us
  local copies, waits for them, and re-layouts: 4.74 us -> 3.13 us
    ppermute x15 -> x9, starting transfers between devices: 20.8 us -> 7.94 us  [swap(): return lax.ppermute(x, 'leaf', [(i, i ^ bit) for i in range(count)])]
    ppermute x15 -> x9, waiting for transfers between devices: 1.81 us -> 10.3 us  [swap(): return lax.ppermute(x, 'leaf', [(i, i ^ bit) for i in range(count)])]
    pallas_call x4, Pallas kernels: 16.6 us -> 11.6 us  [body(): pl.pallas_call(functools.partial(near_kernel, count, c * some), out_shape...]
    ppermute x2 -> x1, starting transfers between devices: 2.59 us -> 0.67 us  [body(): lax.ppermute(to_outer, 'leaf', [pair for i in range(1, count - 1, 2) for...]
    unnamed x24 -> x20, local copies, waits for them, and re-layouts: 4.74 us -> 3.13 us
    pallas_call x1, Pallas kernels: 1.1 us -> 2.55 us  [body(): pl.pallas_call(pack_kernel, out_shape=(jax.ShapeDtypeStruct((shard_rows,...]
    pallas_call x2 -> x3, Pallas kernels: 8.85 us -> 7.43 us  [the longest x1 5.68 us: body(): pl.pallas_call(functools.partial(far_kernel, len(piece), chunks), out_sha...]
  transfers between devices with their start and end apart: 17 -> 10, of which waited for: 1 -> 3; matrix products, arithmetic and copies ran while one was open for 0% -> 0% of each run, Pallas kernels for 32% -> 30%
where the time goes in v3:
time: 44.3 us; the launch traced here: 44 us
  Pallas kernels  21.6 us (49%)
  waiting for transfers between devices  10.3 us (23%)
  starting transfers between devices  8.61 us (19%)
  local copies, waits for them, and re-layouts  3.13 us (7%)
    pallas_call x4, Pallas kernels, body(): pl.pallas_call(functools.partial(near_kernel, count, c * some), out_shape...  11.6 us
    ppermute x9, waiting for transfers between devices, swap(): return lax.ppermute(x, 'leaf', [(i, i ^ bit) for i in range(count)])  10.3 us
    ppermute x9, starting transfers between devices, swap(): return lax.ppermute(x, 'leaf', [(i, i ^ bit) for i in range(count)])  7.94 us
    pallas_call x1, Pallas kernels, body(): pl.pallas_call(functools.partial(far_kernel, len(piece), chunks), out_sha...  5.68 us
    unnamed x20, local copies, waits for them, and re-layouts  3.13 us
    pallas_call x1, Pallas kernels, body(): pl.pallas_call(pack_kernel, out_shape=(jax.ShapeDtypeStruct((shard_rows,...  2.55 us
    pallas_call x1, Pallas kernels, body(): pl.pallas_call(coupling_kernel, out_shape=(jax.ShapeDtypeStruct((leaves,...  1.73 us
  transfers between devices with their start and end apart: 10, of which 3 were waited for; matrix products, arithmetic and copies ran while one was open for 0% of the time, Pallas kernels for 30%

profile of v3, /device:TPU:0, one launch (start us, length us, event | category | flops | bytes accessed | tf_op | source)
XLA Modules:
  0.0 44.0 jit_solution(7833843258449372826)
XLA Ops:
  0.0 0.0 copy-start.8
  0.0 0.0 copy-start.9
  0.0 0.0 copy-start.1
  0.0 2.5 %pack.1 = (bf16[592,128]{1,0:T(8,128)(2,1)}, bf16[80,2048]{1,0:T(8,128)(2,1)}, bf16[80,2048]{1,0:T(8,128)(2,1)}, bf16[80,2048]{1,0:T(8,128)(2,1)}, bf16[64,2048]{1,0:T(8,128)(2,1)}) custom-call(s32[1]{0:T(128)} %bitcast.me_ref, bf16[64,2048]{1,0:T(8,128)(2,1)} %bitcast.10, f32[4,2048]{1,0:T(4,128)} %geo_hbm.1, bf16[16,64,128]{2,1,0:T(8,128)(2,1)} %bitcast.6, ...), custom_call_target="tpu_custom_call" | custom-call | flops 2000000000 | bytes 2000000 | tf_op jit(solution)/shard_map/pack/pallas_call | solution.py:271
  2.6 4.1 %collective-permute-start = (bf16[1,592,128]{2,1,0:T(8,128)(2,1)}, bf16[1,592,128]{2,1,0:T(8,128)(2,1)S(1)}, u32[]{:S(2)}, u32[]{:S(2)}) collective-permute-start(bf16[1,592,128]{2,1,0:T(8,128)(2,1)} %bitcast.8), channel_id=1, source_target_pairs={{0,8},{1,9},{2,10},{3,11},{4,12},{5,13},{6,14},{7,15},{8,0},{9,1},... | collective-permute-start | bytes 454664 | tf_op jit(solution)/shard_map/ppermute | solution.py:289
  6.7 0.0 collective-permute-start.8
  6.7 0.7 %collective-permute-start.9 = (bf16[80,2048]{1,0:T(8,128)(2,1)}, bf16[80,2048]{1,0:T(8,128)(2,1)S(1)}, u32[]{:S(2)}, u32[]{:S(2)}) collective-permute-start(bf16[80,2048]{1,0:T(8,128)(2,1)} %get-tuple-element.15), channel_id=1, source_target_pairs={{1,2},{2,1},{3,4},{4,3},{5,6},{6,5},{7,8},{8,7},{9,10},{10,9},{11,... | collective-permute-start | bytes 983048 | tf_op jit(solution)/shard_map/ppermute | solution.py:299
  7.4 0.0 copy-done.8
  7.4 6.8 %collective-permute-done.b_ref = bf16[1,592,128]{2,1,0:T(8,128)(2,1)S(1)} collective-permute-done((bf16[1,592,128]{2,1,0:T(8,128)(2,1)}, bf16[1,592,128]{2,1,0:T(8,128)(2,1)S(1)}, u32[]{:S(2)}, u32[]{:S(2)}) %collective-permute-start) | collective-permute-done | bytes 151584 | tf_op jit(solution)/shard_map/ppermute | solution.py:289
  14.1 0.0 copy-start.4
  14.1 0.9 %copy-done.4 = bf16[592,128]{1,0:T(8,128)(2,1)S(1)} copy-done((bf16[592,128]{1,0:T(8,128)(2,1)S(1)}, bf16[592,128]{1,0:T(8,128)(2,1)}, u32[]{:S(2)}) %copy-start.4) | copy-done | bytes 151576
  15.1 0.0 copy-start.5
  15.1 0.0 copy-start.6
  15.1 0.0 copy-start.7
  15.1 0.8 %collective-permute-start.4 = (bf16[2,592,128]{2,1,0:T(8,128)(2,1)S(1)}, bf16[2,592,128]{2,1,0:T(8,128)(2,1)S(1)}, u32[]{:S(2)}, u32[]{:S(2)}) collective-permute-start(bf16[2,592,128]{2,1,0:T(8,128)(2,1)S(1)} %merge.1._.refs_0_), channel_id=1, source_target_pairs={{0,4},{1,5},{2,6},{3,7},{4,0},{5,1},{6,2},{7,3},{8,12},{9,13},{10,... | collective-permute-start | bytes 909320 | tf_op jit(solution)/shard_map/ppermute | solution.py:289
  15.9 0.0 copy-done.9
  15.9 1.7 %collective-permute-start.2 = (bf16[2,592,128]{2,1,0:T(8,128)(2,1)S(1)}, bf16[2,592,128]{2,1,0:T(8,128)(2,1)S(1)}, u32[]{:S(2)}, u32[]{:S(2)}) collective-permute-start(bf16[2,592,128]{2,1,0:T(8,128)(2,1)S(1)} %merge.1._.refs_0_), channel_id=1, source_target_pairs={{0,2},{1,3},{2,0},{3,1},{4,6},{5,7},{6,4},{7,5},{8,10},{9,11},{10,... | collective-permute-start | bytes 909320 | tf_op jit(solution)/shard_map/ppermute | solution.py:289
  17.6 0.0 collective-permute-start.1
  17.7 0.0 copy-done.1
  17.7 0.0 copy-start
  17.7 2.2 %copy-done = bf16[16,16,64,64]{3,2,1,0:T(8,128)(2,1)S(1)} copy-done((bf16[16,16,64,64]{3,2,1,0:T(8,128)(2,1)S(1)}, bf16[16,16,64,64]{3,2,1,0:T(8,128)(2,1)}, u32[]{:S(2)}) %copy-start) | copy-done | bytes 2097176
  19.8 1.7 %coupling.1 = (bf16[16,64,1024]{2,1,0:T(8,128)(2,1)S(1)}, bf16[2,64,512]{2,1,0:T(8,128)(2,1)S(1)}) custom-call(bf16[2,592,128]{2,1,0:T(8,128)(2,1)S(1)} %merge.1._.refs_0_, bf16[16,16,64,64]{3,2,1,0:T(8,128)(2,1)S(1)} %copy-done, bf16[2,8,64,64]{3,2,1,0:T(8,128)(2,1)S(1)} %copy-done.1), custom_call_target="tpu_custom_call" | custom-call | flops 2000000000 | bytes 2000000 | tf_op jit(solution)/shard_map/coupling/pallas_call | solution.py:330
  21.6 2.5 %collective-permute-done.4.refs_4_ = bf16[2,592,128]{2,1,0:T(8,128)(2,1)S(1)} collective-permute-done((bf16[2,592,128]{2,1,0:T(8,128)(2,1)S(1)}, bf16[2,592,128]{2,1,0:T(8,128)(2,1)S(1)}, u32[]{:S(2)}, u32[]{:S(2)}) %collective-permute-start.4) | collective-permute-done | bytes 303136 | tf_op jit(solution)/shard_map/ppermute | solution.py:289
  24.1 0.7 %collective-permute-start.6 = (bf16[2,592,128]{2,1,0:T(8,128)(2,1)S(1)}, bf16[2,592,128]{2,1,0:T(8,128)(2,1)S(1)}, u32[]{:S(2)}, u32[]{:S(2)}) collective-permute-start(bf16[2,592,128]{2,1,0:T(8,128)(2,1)S(1)} %collective-permute-done.4.refs_4_), channel_id=1, source_target_pairs={{0,2},{1,3},{2,0},{3,1},{4,6},{5,7},{6,4},{7,5},{8,10},{9,11},{10,... | collective-permute-start | bytes 909320 | tf_op jit(solution)/shard_map/ppermute | solution.py:289
  24.8 0.0 collective-permute-done.8.inner_ref
  24.8 0.0 collective-permute-done.9.outer_ref
  24.8 0.0 copy-done.5
  24.9 0.0 copy-done.6
  24.9 0.0 copy-done.7
  24.9 2.9 %near3.1.refs_11_ = f32[64,512]{1,0:T(8,128)S(1)} custom-call(s32[1]{0:T(128)} %bitcast.me_ref, s32[16,24]{1,0:T(8,128)S(1)} %copy-done.5, bf16[80,2048]{1,0:T(8,128)(2,1)S(1)} %copy-done.6, bf16[80,2048]{1,0:T(8,128)(2,1)S(1)} %collective-permute-done.8.inner_ref, bf16[80,2048]{1,0:T(8,128)(2,1)S(1)} %collective-permute-done.9.outer_ref, ...), custom_call_target="tpu_custom_call" | custom-call | flops 2500000000 | bytes 2500000 | tf_op jit(solution)/shard_map/near3/pallas_call | solution.py:346
  27.7 2.9 %near2.1.refs_10_ = f32[64,512]{1,0:T(8,128)S(1)} custom-call(s32[1]{0:T(128)} %bitcast.me_ref, s32[16,24]{1,0:T(8,128)S(1)} %copy-done.5, bf16[80,2048]{1,0:T(8,128)(2,1)S(1)} %copy-done.6, bf16[80,2048]{1,0:T(8,128)(2,1)S(1)} %collective-permute-done.8.inner_ref, bf16[80,2048]{1,0:T(8,128)(2,1)S(1)} %collective-permute-done.9.outer_ref, ...), custom_call_target="tpu_custom_call" | custom-call | flops 2500000000 | bytes 2500000 | tf_op jit(solution)/shard_map/near2/pallas_call | solution.py:346
  30.6 0.1 collective-permute-start.5
  30.7 0.0 collective-permute-done.2.refs_2_
  30.7 0.5 %collective-permute-start.3 = (bf16[2,592,128]{2,1,0:T(8,128)(2,1)S(1)}, bf16[2,592,128]{2,1,0:T(8,128)(2,1)S(1)}, u32[]{:S(2)}, u32[]{:S(2)}) collective-permute-start(bf16[2,592,128]{2,1,0:T(8,128)(2,1)S(1)} %collective-permute-done.2.refs_2_), channel_id=1, source_target_pairs={{0,1},{1,0},{2,3},{3,2},{4,5},{5,4},{6,7},{7,6},{8,9},{9,8},{10,11... | collective-permute-start | bytes 909320 | tf_op jit(solution)/shard_map/ppermute | solution.py:289
  31.2 1.0 %collective-permute-done.6.refs_6_ = bf16[2,592,128]{2,1,0:T(8,128)(2,1)S(1)} collective-permute-done((bf16[2,592,128]{2,1,0:T(8,128)(2,1)S(1)}, bf16[2,592,128]{2,1,0:T(8,128)(2,1)S(1)}, u32[]{:S(2)}, u32[]{:S(2)}) %collective-permute-start.6) | collective-permute-done | bytes 303136 | tf_op jit(solution)/shard_map/ppermute | solution.py:289
  32.2 0.0 collective-permute-start.7
  32.2 2.9 %near1.1.refs_9_ = f32[64,512]{1,0:T(8,128)S(1)} custom-call(s32[1]{0:T(128)} %bitcast.me_ref, s32[16,24]{1,0:T(8,128)S(1)} %copy-done.5, bf16[80,2048]{1,0:T(8,128)(2,1)S(1)} %copy-done.6, bf16[80,2048]{1,0:T(8,128)(2,1)S(1)} %collective-permute-done.8.inner_ref, bf16[80,2048]{1,0:T(8,128)(2,1)S(1)} %collective-permute-done.9.outer_ref, ...), custom_call_target="tpu_custom_call" | custom-call | flops 2500000000 | bytes 2500000 | tf_op jit(solution)/shard_map/near1/pallas_call | solution.py:346
  35.0 0.0 copy-start.2
  35.1 0.0 copy-start.3
  35.1 3.0 %near0.1.refs_8_ = f32[64,512]{1,0:T(8,128)S(1)} custom-call(s32[1]{0:T(128)} %bitcast.me_ref, s32[16,24]{1,0:T(8,128)S(1)} %copy-done.5, bf16[80,2048]{1,0:T(8,128)(2,1)S(1)} %copy-done.6, bf16[80,2048]{1,0:T(8,128)(2,1)S(1)} %collective-permute-done.8.inner_ref, bf16[80,2048]{1,0:T(8,128)(2,1)S(1)} %collective-permute-done.9.outer_ref, ...), custom_call_target="tpu_custom_call" | custom-call | flops 2500000000 | bytes 2500000 | tf_op jit(solution)/shard_map/near0/pallas_call | solution.py:346
  38.1 0.0 collective-permute-done.1.refs_1_
  38.1 0.0 collective-permute-done.5.refs_5_
  38.1 0.0 collective-permute-done.3.refs_3_
  38.1 0.0 collective-permute-done.7.refs_7_
  38.2 0.0 copy-done.2
  38.2 0.0 copy-done.3
  38.2 5.7 %far.1 = f32[64,2048]{1,0:T(8,128)} custom-call(s32[1]{0:T(128)} %bitcast.me_ref, s32[16,16]{1,0:T(8,128)S(1)} %fusion.1.recv_ref, s32[2,8]{1,0:T(2,128)S(1)} %fusion.3.top_ref, bf16[2,592,128]{2,1,0:T(8,128)(2,1)S(1)} %merge.1._.refs_0_, bf16[2,592,128]{2,1,0:T(8,128)(2,1)S(1)} %collective-permute-done.1.refs_1_, ...), custom_call_target="tpu_custom_call" | custom-call | flops 6000000000 | bytes 6000000 | tf_op jit(solution)/shard_map/far/pallas_call | solution.py:359
  (3 shorter events, 0.1 us)
Async XLA Ops:
  0.0 7.4 %copy-start.8 = (s32[16,16]{1,0:T(8,128)S(1)}, s32[16,16]{1,0:T(8,128)}, u32[]{:S(2)}) copy-start(s32[16,16]{1,0:T(8,128)} %param.17) | copy-start | bytes 3076
  0.0 15.9 %copy-start.9 = (s32[2,8]{1,0:T(2,128)S(1)}, s32[2,8]{1,0:T(2,128)}, u32[]{:S(2)}) copy-start(s32[2,8]{1,0:T(2,128)} %param.19) | copy-start | bytes 196
  0.0 17.6 %copy-start.1 = (bf16[2,8,64,64]{3,2,1,0:T(8,128)(2,1)S(1)}, bf16[2,8,64,64]{3,2,1,0:T(8,128)(2,1)}, u32[]{:S(2)}) copy-start(bf16[2,8,64,64]{3,2,1,0:T(8,128)(2,1)} %top_ref.1) | copy-start | bytes 393220
  2.6 11.6 %collective-permute-start = (bf16[1,592,128]{2,1,0:T(8,128)(2,1)}, bf16[1,592,128]{2,1,0:T(8,128)(2,1)S(1)}, u32[]{:S(2)}, u32[]{:S(2)}) collective-permute-start(bf16[1,592,128]{2,1,0:T(8,128)(2,1)} %bitcast.8), channel_id=1, source_target_pairs={{0,8},{1,9},{2,10},{3,11},{4,12},{5,13},{6,14},{7,15},{8,0},{9,1},... | collective-permute-start | bytes 454664 | tf_op jit(solution)/shard_map/ppermute | solution.py:289
  6.7 18.2 %collective-permute-start.8 = (bf16[80,2048]{1,0:T(8,128)(2,1)}, bf16[80,2048]{1,0:T(8,128)(2,1)S(1)}, u32[]{:S(2)}, u32[]{:S(2)}) collective-permute-start(bf16[80,2048]{1,0:T(8,128)(2,1)} %get-tuple-element.14), channel_id=1, source_target_pairs={{0,1},{1,0},{2,3},{3,2},{4,5},{5,4},{6,7},{7,6},{8,9},{9,8},{10,11... | collective-permute-start | bytes 983048 | tf_op jit(solution)/shard_map/ppermute | solution.py:289
  6.7 18.2 %collective-permute-start.9 = (bf16[80,2048]{1,0:T(8,128)(2,1)}, bf16[80,2048]{1,0:T(8,128)(2,1)S(1)}, u32[]{:S(2)}, u32[]{:S(2)}) collective-permute-start(bf16[80,2048]{1,0:T(8,128)(2,1)} %get-tuple-element.15), channel_id=1, source_target_pairs={{1,2},{2,1},{3,4},{4,3},{5,6},{6,5},{7,8},{8,7},{9,10},{10,9},{11,... | collective-permute-start | bytes 983048 | tf_op jit(solution)/shard_map/ppermute | solution.py:299
  14.1 0.9 %copy-start.4 = (bf16[592,128]{1,0:T(8,128)(2,1)S(1)}, bf16[592,128]{1,0:T(8,128)(2,1)}, u32[]{:S(2)}) copy-start(bf16[592,128]{1,0:T(8,128)(2,1)} %get-tuple-element.12) | copy-start | bytes 454660
  15.1 9.8 %copy-start.5 = (s32[16,24]{1,0:T(8,128)S(1)}, s32[16,24]{1,0:T(8,128)}, u32[]{:S(2)}) copy-start(s32[16,24]{1,0:T(8,128)} %list_ref.7) | copy-start | bytes 4612
  15.1 9.8 %copy-start.6 = (bf16[80,2048]{1,0:T(8,128)(2,1)S(1)}, bf16[80,2048]{1,0:T(8,128)(2,1)}, u32[]{:S(2)}) copy-start(bf16[80,2048]{1,0:T(8,128)(2,1)} %get-tuple-element.13.own_ref) | copy-start | bytes 983044
  15.1 9.8 %copy-start.7 = (bf16[64,2048]{1,0:T(8,128)(2,1)S(1)}, bf16[64,2048]{1,0:T(8,128)(2,1)}, u32[]{:S(2)}) copy-start(bf16[64,2048]{1,0:T(8,128)(2,1)} %get-tuple-element.16.target_ref) | copy-start | bytes 786436
  15.1 9.0 %collective-permute-start.4 = (bf16[2,592,128]{2,1,0:T(8,128)(2,1)S(1)}, bf16[2,592,128]{2,1,0:T(8,128)(2,1)S(1)}, u32[]{:S(2)}, u32[]{:S(2)}) collective-permute-start(bf16[2,592,128]{2,1,0:T(8,128)(2,1)S(1)} %merge.1._.refs_0_), channel_id=1, source_target_pairs={{0,4},{1,5},{2,6},{3,7},{4,0},{5,1},{6,2},{7,3},{8,12},{9,13},{10,... | collective-permute-start | bytes 909320 | tf_op jit(solution)/shard_map/ppermute | solution.py:289
  15.9 14.8 %collective-permute-start.2 = (bf16[2,592,128]{2,1,0:T(8,128)(2,1)S(1)}, bf16[2,592,128]{2,1,0:T(8,128)(2,1)S(1)}, u32[]{:S(2)}, u32[]{:S(2)}) collective-permute-start(bf16[2,592,128]{2,1,0:T(8,128)(2,1)S(1)} %merge.1._.refs_0_), channel_id=1, source_target_pairs={{0,2},{1,3},{2,0},{3,1},{4,6},{5,7},{6,4},{7,5},{8,10},{9,11},{10,... | collective-permute-start | bytes 909320 | tf_op jit(solution)/shard_map/ppermute | solution.py:289
  17.6 20.5 %collective-permute-start.1 = (bf16[2,592,128]{2,1,0:T(8,128)(2,1)S(1)}, bf16[2,592,128]{2,1,0:T(8,128)(2,1)S(1)}, u32[]{:S(2)}, u32[]{:S(2)}) collective-permute-start(bf16[2,592,128]{2,1,0:T(8,128)(2,1)S(1)} %merge.1._.refs_0_), channel_id=1, source_target_pairs={{0,1},{1,0},{2,3},{3,2},{4,5},{5,4},{6,7},{7,6},{8,9},{9,8},{10,11... | collective-permute-start | bytes 909320 | tf_op jit(solution)/shard_map/ppermute | solution.py:289
  17.7 2.2 %copy-start = (bf16[16,16,64,64]{3,2,1,0:T(8,128)(2,1)S(1)}, bf16[16,16,64,64]{3,2,1,0:T(8,128)(2,1)}, u32[]{:S(2)}) copy-start(bf16[16,16,64,64]{3,2,1,0:T(8,128)(2,1)} %c_ref.1) | copy-start | bytes 6291460
  24.1 8.1 %collective-permute-start.6 = (bf16[2,592,128]{2,1,0:T(8,128)(2,1)S(1)}, bf16[2,592,128]{2,1,0:T(8,128)(2,1)S(1)}, u32[]{:S(2)}, u32[]{:S(2)}) collective-permute-start(bf16[2,592,128]{2,1,0:T(8,128)(2,1)S(1)} %collective-permute-done.4.refs_4_), channel_id=1, source_target_pairs={{0,2},{1,3},{2,0},{3,1},{4,6},{5,7},{6,4},{7,5},{8,10},{9,11},{10,... | collective-permute-start | bytes 909320 | tf_op jit(solution)/shard_map/ppermute | solution.py:289
  30.6 7.5 %collective-permute-start.5 = (bf16[2,592,128]{2,1,0:T(8,128)(2,1)S(1)}, bf16[2,592,128]{2,1,0:T(8,128)(2,1)S(1)}, u32[]{:S(2)}, u32[]{:S(2)}) collective-permute-start(bf16[2,592,128]{2,1,0:T(8,128)(2,1)S(1)} %collective-permute-done.4.refs_4_), channel_id=1, source_target_pairs={{0,1},{1,0},{2,3},{3,2},{4,5},{5,4},{6,7},{7,6},{8,9},{9,8},{10,11... | collective-permute-start | bytes 909320 | tf_op jit(solution)/shard_map/ppermute | solution.py:289
  30.7 7.4 %collective-permute-start.3 = (bf16[2,592,128]{2,1,0:T(8,128)(2,1)S(1)}, bf16[2,592,128]{2,1,0:T(8,128)(2,1)S(1)}, u32[]{:S(2)}, u32[]{:S(2)}) collective-permute-start(bf16[2,592,128]{2,1,0:T(8,128)(2,1)S(1)} %collective-permute-done.2.refs_2_), channel_id=1, source_target_pairs={{0,1},{1,0},{2,3},{3,2},{4,5},{5,4},{6,7},{7,6},{8,9},{9,8},{10,11... | collective-permute-start | bytes 909320 | tf_op jit(solution)/shard_map/ppermute | solution.py:289
  32.2 6.0 %collective-permute-start.7 = (bf16[2,592,128]{2,1,0:T(8,128)(2,1)S(1)}, bf16[2,592,128]{2,1,0:T(8,128)(2,1)S(1)}, u32[]{:S(2)}, u32[]{:S(2)}) collective-permute-start(bf16[2,592,128]{2,1,0:T(8,128)(2,1)S(1)} %collective-permute-done.6.refs_6_), channel_id=1, source_target_pairs={{0,1},{1,0},{2,3},{3,2},{4,5},{5,4},{6,7},{7,6},{8,9},{9,8},{10,11... | collective-permute-start | bytes 909320 | tf_op jit(solution)/shard_map/ppermute | solution.py:289
  35.0 3.1 %copy-start.2 = (bf16[16,128,64]{1,2,0:T(8,128)(2,1)S(1)}, bf16[16,128,64]{1,2,0:T(8,128)(2,1)}, u32[]{:S(2)}) copy-start(bf16[16,128,64]{1,2,0:T(8,128)(2,1)} %param.12) | copy-start | bytes 786436
  35.1 3.1 %copy-start.3 = (bf16[16,64,64]{2,1,0:T(8,128)(2,1)S(1)}, bf16[16,64,64]{2,1,0:T(8,128)(2,1)}, u32[]{:S(2)}) copy-start(bf16[16,64,64]{2,1,0:T(8,128)(2,1)} %refs_14_.1) | copy-start | bytes 393220

commit v4 on v3

--- a/solution.py
+++ b/solution.py
@@ -118,7 +118,7 @@
     shard_ref[at : at + send_ref.shape[0], 0 : send_ref.shape[1]] = send_ref[...].astype(F32).astype(BF)
 
 
-def near_kernel(count, first, me_ref, list_ref, own_ref, inner_ref, outer_ref, target_ref, out_ref, block_ref):
+def near_kernel(count, first, me_ref, list_ref, own_ref, inner_ref, outer_ref, target_ref, _, out_ref, block_ref):
     wide, points = own_ref.shape
     rhs, some = out_ref.shape
     leaves, near = list_ref.shape
@@ -167,13 +167,13 @@
         out_ref[:, l * leaf : (l + 1) * leaf] = turned[0:rhs] + turned[rhs:]
 
 
-def merge_kernel(a_ref, b_ref, out_ref):
+def merge_kernel(a_ref, b_ref, _, out_ref):
     deep = a_ref.shape[0]
     out_ref[0:deep] = a_ref[...]
     out_ref[deep:] = b_ref[...]
 
 
-def coupling_kernel(_, c_ref, top_ref, out_ref, top_out_ref):
+def coupling_kernel(c_ref, top_ref, out_ref, top_out_ref):
     leaves, far, rank, _ = c_ref.shape
     uppers, top, _, _ = top_ref.shape
     for p in range(uppers):
@@ -280,7 +280,7 @@
         in_specs=[SMEM] + [pl.BlockSpec(memory_space=pltpu.HBM)] * 5,
         out_specs=(VMEM,) * 5,
         scratch_shapes=[pltpu.VMEM(a.shape, a.dtype) for a in staged] + [pltpu.SemaphoreType.DMA((5,))],
-        compiler_params=params(60),
+        compiler_params=params(54),
         cost_estimate=cost(2),
         name="pack",
     )(me_list, *staged)
@@ -299,22 +299,6 @@
     outer = lax.ppermute(
         to_outer, "leaf", [pair for i in range(1, count - 1, 2) for pair in ((i, i + 1), (i + 1, i))]
     )
-    both = pl.pallas_call(
-        merge_kernel,
-        out_shape=jax.ShapeDtypeStruct((2 * deep, *base.shape[1:]), BF),
-        in_specs=[VMEM] * 2,
-        out_specs=VMEM,
-        compiler_params=params(32),
-        cost_estimate=cost(1),
-        name="merge",
-    )(base, far_side)
-    piece = {0: both}
-    piece[4] = swap(both, 4)
-    piece[2] = swap(both, 2)
-    piece[6] = swap(piece[4], 2)
-    for j in (0, 4, 2, 6):
-        piece[j + 1] = swap(piece[j], 1)
-
     def place(device):
         gap = lax.bitwise_xor(device, me)
         top = gap >> 4
@@ -333,28 +317,51 @@
             jax.ShapeDtypeStruct((leaves, rank, far * rank), BF),
             jax.ShapeDtypeStruct((uppers, rank, top_source.shape[1] * rank), BF),
         ),
-        in_specs=[ANY, VMEM, VMEM],
+        in_specs=[VMEM, VMEM],
         out_specs=(VMEM,) * 2,
         compiler_params=params(32),
-        cost_estimate=cost(2),
+        cost_estimate=cost(0.05),
         name="coupling",
-    )(both, leaf_coupling, top_coupling)
-
-    chunks = 4
+    )(leaf_coupling, top_coupling)
+
+    chunks = 2
     some = leaves // chunks
-    nears = [
-        pl.pallas_call(
+
+    def near(c, after):
+        return pl.pallas_call(
             functools.partial(near_kernel, count, c * some),
             out_shape=jax.ShapeDtypeStruct((rhs, some * leaf), F32),
-            in_specs=[SMEM] * 2 + [VMEM] * 4,
+            in_specs=[SMEM] * 2 + [VMEM] * 4 + [ANY],
             out_specs=VMEM,
             scratch_shapes=[pltpu.VMEM((leaves + 2 * REACH, rhs + FEATS, leaf), BF)],
             compiler_params=params(32),
-            cost_estimate=cost(2.5),
+            cost_estimate=cost(5),
             name=f"near{c}",
-        )(me_list, near_list, own, inner, outer, targets)
-        for c in range(chunks)
-    ]
+        )(me_list, near_list, own, inner, outer, targets, after)
+
+    def after(x, others):
+        return lax.optimization_barrier((x, *others))[0]
+
+    both = pl.pallas_call(
+        merge_kernel,
+        out_shape=jax.ShapeDtypeStruct((2 * deep, *base.shape[1:]), BF),
+        in_specs=[VMEM] * 2 + [ANY],
+        out_specs=VMEM,
+        compiler_params=params(32),
+        cost_estimate=cost(3),
+        name="merge",
+    )(base, far_side, coupling)
+    piece = {0: both}
+    piece[4] = swap(both, 4)
+    piece[2] = swap(both, 2)
+    nears = [near(0, both)]
+    piece[4] = after(piece[4], nears)
+    piece[6] = swap(piece[4], 2)
+    for j in (0, 4, 2):
+        piece[j + 1] = swap(piece[j], 1)
+    nears += [near(1, piece[4])]
+    piece[6] = after(piece[6], nears)
+    piece[7] = swap(piece[6], 1)
 
     out = pl.pallas_call(
         functools.partial(far_kernel, len(piece), chunks),

time: 44.3 us -> 41.7 us (0.941)
  the two profiles are of different devices: /device:TPU:0 before, /device:TPU:15 now
where the time goes in v4:
time: 41.7 us; the launch traced here: 41.5 us
  Pallas kernels  19.3 us (46%)
  starting transfers between devices  14.7 us (35%)
  waiting for transfers between devices  7.18 us (17%)
    ppermute x9, starting transfers between devices, swap(): return lax.ppermute(x, 'leaf', [(i, i ^ bit) for i in range(count)])  12.8 us
    pallas_call x2, Pallas kernels, near(): pl.pallas_call(functools.partial(near_kernel, count, c * some), out_shape...  9.17 us
    ppermute x9, waiting for transfers between devices, swap(): return lax.ppermute(x, 'leaf', [(i, i ^ bit) for i in range(count)])  5.96 us
    pallas_call x1, Pallas kernels, body(): pl.pallas_call(functools.partial(far_kernel, len(piece), chunks), out_sha...  5.68 us
    pallas_call x1, Pallas kernels, body(): pl.pallas_call(pack_kernel, out_shape=(jax.ShapeDtypeStruct((shard_rows,...  2.65 us
    ppermute x1, starting transfers between devices, body(): lax.ppermute(to_outer, 'leaf', [pair for i in range(1, count - 1, 2) for...  1.91 us
    pallas_call x1, Pallas kernels, body(): pl.pallas_call(coupling_kernel, out_shape=(jax.ShapeDtypeStruct((leaves,...  1.73 us
    ppermute x1, waiting for transfers between devices, body(): lax.ppermute(to_outer, 'leaf', [pair for i in range(1, count - 1, 2) for...  1.22 us
  transfers between devices with their start and end apart: 10, of which 5 were waited for; matrix products, arithmetic and copies ran while one was open for 0% of the time, Pallas kernels for 26%

profile of v4, /device:TPU:15, one launch (start us, length us, event | category | flops | bytes accessed | tf_op | source)
XLA Modules:
  0.0 41.5 jit_solution(9174903444216364646)
XLA Ops:
  0.0 0.0 copy-start.1
  0.0 0.0 copy-start
  0.0 2.7 %pack.1 = (bf16[592,128]{1,0:T(8,128)(2,1)}, bf16[80,2048]{1,0:T(8,128)(2,1)}, bf16[80,2048]{1,0:T(8,128)(2,1)}, bf16[80,2048]{1,0:T(8,128)(2,1)}, bf16[64,2048]{1,0:T(8,128)(2,1)}) custom-call(s32[1]{0:T(128)} %bitcast.me_ref, bf16[64,2048]{1,0:T(8,128)(2,1)} %bitcast.10, f32[4,2048]{1,0:T(4,128)} %geo_hbm.1, bf16[16,64,128]{2,1,0:T(8,128)(2,1)} %bitcast.6, ...), custom_call_target="tpu_custom_call" | custom-call | flops 2000000000 | bytes 2000000 | tf_op jit(solution)/shard_map/pack/pallas_call | solution.py:271
  2.7 0.0 copy-start.4
  2.7 2.4 %collective-permute-start = (bf16[1,592,128]{2,1,0:T(8,128)(2,1)}, bf16[1,592,128]{2,1,0:T(8,128)(2,1)S(1)}, u32[]{:S(2)}, u32[]{:S(2)}) collective-permute-start(bf16[1,592,128]{2,1,0:T(8,128)(2,1)} %bitcast.8), channel_id=1, source_target_pairs={{0,8},{1,9},{2,10},{3,11},{4,12},{5,13},{6,14},{7,15},{8,0},{9,1},... | collective-permute-start | bytes 454664 | tf_op jit(solution)/shard_map/ppermute | solution.py:289
  5.1 1.0 %collective-permute-start.5 = (bf16[80,2048]{1,0:T(8,128)(2,1)}, bf16[80,2048]{1,0:T(8,128)(2,1)S(1)}, u32[]{:S(2)}, u32[]{:S(2)}) collective-permute-start(bf16[80,2048]{1,0:T(8,128)(2,1)} %get-tuple-element.17), channel_id=1, source_target_pairs={{0,1},{1,0},{2,3},{3,2},{4,5},{5,4},{6,7},{7,6},{8,9},{9,8},{10,11... | collective-permute-start | bytes 983048 | tf_op jit(solution)/shard_map/ppermute | solution.py:289
  6.0 1.9 %collective-permute-start.6 = (bf16[80,2048]{1,0:T(8,128)(2,1)}, bf16[80,2048]{1,0:T(8,128)(2,1)S(1)}, u32[]{:S(2)}, u32[]{:S(2)}) collective-permute-start(bf16[80,2048]{1,0:T(8,128)(2,1)} %get-tuple-element.18), channel_id=1, source_target_pairs={{1,2},{2,1},{3,4},{4,3},{5,6},{6,5},{7,8},{8,7},{9,10},{10,9},{11,... | collective-permute-start | bytes 983048 | tf_op jit(solution)/shard_map/ppermute | solution.py:299
  7.9 0.0 copy-done.1
  7.9 0.0 copy-done
  7.9 1.7 %coupling.1 = (bf16[16,64,1024]{2,1,0:T(8,128)(2,1)S(1)}, bf16[2,64,512]{2,1,0:T(8,128)(2,1)S(1)}) custom-call(bf16[16,16,64,64]{3,2,1,0:T(8,128)(2,1)S(1)} %copy-done, bf16[2,8,64,64]{3,2,1,0:T(8,128)(2,1)S(1)} %copy-done.1), custom_call_target="tpu_custom_call" | custom-call | flops 50000000 | bytes 50000 | tf_op jit(solution)/shard_map/coupling/pallas_call | solution.py:314
  9.7 2.5 %collective-permute-done.b_ref = bf16[1,592,128]{2,1,0:T(8,128)(2,1)S(1)} collective-permute-done((bf16[1,592,128]{2,1,0:T(8,128)(2,1)}, bf16[1,592,128]{2,1,0:T(8,128)(2,1)S(1)}, u32[]{:S(2)}, u32[]{:S(2)}) %collective-permute-start) | collective-permute-done | bytes 151584 | tf_op jit(solution)/shard_map/ppermute | solution.py:289
  12.2 0.0 copy-done.4
  12.2 0.0 copy-start.5
  12.2 0.0 copy-start.6
  12.2 0.0 copy-start.7
  12.2 0.1 collective-permute-start.4
  12.3 0.2 collective-permute-start.2
  12.6 2.0 %collective-permute-start.1 = (bf16[2,592,128]{2,1,0:T(8,128)(2,1)S(1)}, bf16[2,592,128]{2,1,0:T(8,128)(2,1)S(1)}, u32[]{:S(2)}, u32[]{:S(2)}) collective-permute-start(bf16[2,592,128]{2,1,0:T(8,128)(2,1)S(1)} %merge.1._.refs_0_), channel_id=1, source_target_pairs={{0,1},{1,0},{2,3},{3,2},{4,5},{5,4},{6,7},{7,6},{8,9},{9,8},{10,11... | collective-permute-start | bytes 909320 | tf_op jit(solution)/shard_map/ppermute | solution.py:289
  14.6 0.0 collective-permute-done.5.inner_ref
  14.6 1.2 %collective-permute-done.6.outer_ref = bf16[80,2048]{1,0:T(8,128)(2,1)S(1)} collective-permute-done((bf16[80,2048]{1,0:T(8,128)(2,1)}, bf16[80,2048]{1,0:T(8,128)(2,1)S(1)}, u32[]{:S(2)}, u32[]{:S(2)}) %collective-permute-start.6) | collective-permute-done | bytes 327712 | tf_op jit(solution)/shard_map/ppermute | solution.py:299
  15.8 0.0 copy-done.5
  15.8 0.0 copy-done.6
  15.8 0.0 copy-done.7
  15.8 4.5 %near0.1.refs_8_ = f32[64,1024]{1,0:T(8,128)S(1)} custom-call(s32[1]{0:T(128)} %bitcast.me_ref, s32[16,24]{1,0:T(8,128)S(1)} %copy-done.5, bf16[80,2048]{1,0:T(8,128)(2,1)S(1)} %copy-done.6, bf16[80,2048]{1,0:T(8,128)(2,1)S(1)} %collective-permute-done.5.inner_ref, bf16[80,2048]{1,0:T(8,128)(2,1)S(1)} %collective-permute-done.6.outer_ref, ...), custom_call_target="tpu_custom_call" | custom-call | flops 5000000000 | bytes 5000000 | tf_op jit(solution)/shard_map/near0/pallas_call | solution.py:331
  20.3 0.0 copy-start.9
  20.3 0.0 copy-start.8
  20.4 0.0 copy-start.2
  20.4 0.0 copy-start.3
  20.4 0.1 collective-permute-done.4._.refs_4_
  20.5 5.9 %collective-permute-start.8 = (bf16[2,592,128]{2,1,0:T(8,128)(2,1)S(1)}, bf16[2,592,128]{2,1,0:T(8,128)(2,1)S(1)}, u32[]{:S(2)}, u32[]{:S(2)}) collective-permute-start(bf16[2,592,128]{2,1,0:T(8,128)(2,1)S(1)} %collective-permute-done.4._.refs_4_), channel_id=1, source_target_pairs={{0,2},{1,3},{2,0},{3,1},{4,6},{5,7},{6,4},{7,5},{8,10},{9,11},{10,... | collective-permute-start | bytes 909320 | tf_op jit(solution)/shard_map/ppermute | solution.py:289
  26.3 0.0 collective-permute-start.7
  26.3 0.0 collective-permute-done.2.refs_2_
  26.3 0.5 %collective-permute-start.3 = (bf16[2,592,128]{2,1,0:T(8,128)(2,1)S(1)}, bf16[2,592,128]{2,1,0:T(8,128)(2,1)S(1)}, u32[]{:S(2)}, u32[]{:S(2)}) collective-permute-start(bf16[2,592,128]{2,1,0:T(8,128)(2,1)S(1)} %collective-permute-done.2.refs_2_), channel_id=1, source_target_pairs={{0,1},{1,0},{2,3},{3,2},{4,5},{5,4},{6,7},{7,6},{8,9},{9,8},{10,11... | collective-permute-start | bytes 909320 | tf_op jit(solution)/shard_map/ppermute | solution.py:289
  26.9 4.7 %near1.1.refs_9_ = f32[64,1024]{1,0:T(8,128)S(1)} custom-call(s32[1]{0:T(128)} %bitcast.me_ref, s32[16,24]{1,0:T(8,128)S(1)} %copy-done.5, bf16[80,2048]{1,0:T(8,128)(2,1)S(1)} %copy-done.6, bf16[80,2048]{1,0:T(8,128)(2,1)S(1)} %collective-permute-done.5.inner_ref, bf16[80,2048]{1,0:T(8,128)(2,1)S(1)} %collective-permute-done.6.outer_ref, ...), custom_call_target="tpu_custom_call" | custom-call | flops 5000000000 | bytes 5000000 | tf_op jit(solution)/shard_map/near1/pallas_call | solution.py:331
  31.5 2.2 %collective-permute-done.8.refs_6_ = bf16[2,592,128]{2,1,0:T(8,128)(2,1)S(1)} collective-permute-done((bf16[2,592,128]{2,1,0:T(8,128)(2,1)S(1)}, bf16[2,592,128]{2,1,0:T(8,128)(2,1)S(1)}, u32[]{:S(2)}, u32[]{:S(2)}) %collective-permute-start.8) | collective-permute-done | bytes 303136 | tf_op jit(solution)/shard_map/ppermute | solution.py:289
  33.7 0.7 %collective-permute-start.9 = (bf16[2,592,128]{2,1,0:T(8,128)(2,1)S(1)}, bf16[2,592,128]{2,1,0:T(8,128)(2,1)S(1)}, u32[]{:S(2)}, u32[]{:S(2)}) collective-permute-start(bf16[2,592,128]{2,1,0:T(8,128)(2,1)S(1)} %collective-permute-done.8.refs_6_), channel_id=1, source_target_pairs={{0,1},{1,0},{2,3},{3,2},{4,5},{5,4},{6,7},{7,6},{8,9},{9,8},{10,11... | collective-permute-start | bytes 909320 | tf_op jit(solution)/shard_map/ppermute | solution.py:289
  34.5 0.0 copy-done.9
  34.5 0.0 copy-done.8
  34.5 0.0 collective-permute-done.1.refs_1_
  34.5 0.0 collective-permute-done.7.refs_5_
  34.5 0.0 collective-permute-done.3.refs_3_
  34.6 1.1 %collective-permute-done.9.refs_7_ = bf16[2,592,128]{2,1,0:T(8,128)(2,1)S(1)} collective-permute-done((bf16[2,592,128]{2,1,0:T(8,128)(2,1)S(1)}, bf16[2,592,128]{2,1,0:T(8,128)(2,1)S(1)}, u32[]{:S(2)}, u32[]{:S(2)}) %collective-permute-start.9) | collective-permute-done | bytes 303136 | tf_op jit(solution)/shard_map/ppermute | solution.py:289
  35.7 0.0 copy-done.2
  35.7 0.0 copy-done.3
  35.7 5.7 %far.1 = f32[64,2048]{1,0:T(8,128)} custom-call(s32[1]{0:T(128)} %bitcast.me_ref, s32[16,16]{1,0:T(8,128)S(1)} %fusion.1.recv_ref, s32[2,8]{1,0:T(2,128)S(1)} %fusion.3.top_ref, bf16[2,592,128]{2,1,0:T(8,128)(2,1)S(1)} %merge.1._.refs_0_, bf16[2,592,128]{2,1,0:T(8,128)(2,1)S(1)} %collective-permute-done.1.refs_1_, ...), custom_call_target="tpu_custom_call" | custom-call | flops 6000000000 | bytes 6000000 | tf_op jit(solution)/shard_map/far/pallas_call | solution.py:366
  (3 shorter events, 0.1 us)
Async XLA Ops:
  0.0 7.9 %copy-start.1 = (bf16[2,8,64,64]{3,2,1,0:T(8,128)(2,1)S(1)}, bf16[2,8,64,64]{3,2,1,0:T(8,128)(2,1)}, u32[]{:S(2)}) copy-start(bf16[2,8,64,64]{3,2,1,0:T(8,128)(2,1)} %top_ref.1) | copy-start | bytes 393220
  0.0 7.9 %copy-start = (bf16[16,16,64,64]{3,2,1,0:T(8,128)(2,1)S(1)}, bf16[16,16,64,64]{3,2,1,0:T(8,128)(2,1)}, u32[]{:S(2)}) copy-start(bf16[16,16,64,64]{3,2,1,0:T(8,128)(2,1)} %c_ref.1) | copy-start | bytes 6291460
  2.7 9.5 %copy-start.4 = (bf16[592,128]{1,0:T(8,128)(2,1)S(1)}, bf16[592,128]{1,0:T(8,128)(2,1)}, u32[]{:S(2)}) copy-start(bf16[592,128]{1,0:T(8,128)(2,1)} %get-tuple-element.14) | copy-start | bytes 454660
  2.7 9.5 %collective-permute-start = (bf16[1,592,128]{2,1,0:T(8,128)(2,1)}, bf16[1,592,128]{2,1,0:T(8,128)(2,1)S(1)}, u32[]{:S(2)}, u32[]{:S(2)}) collective-permute-start(bf16[1,592,128]{2,1,0:T(8,128)(2,1)} %bitcast.8), channel_id=1, source_target_pairs={{0,8},{1,9},{2,10},{3,11},{4,12},{5,13},{6,14},{7,15},{8,0},{9,1},... | collective-permute-start | bytes 454664 | tf_op jit(solution)/shard_map/ppermute | solution.py:289
  5.1 9.5 %collective-permute-start.5 = (bf16[80,2048]{1,0:T(8,128)(2,1)}, bf16[80,2048]{1,0:T(8,128)(2,1)S(1)}, u32[]{:S(2)}, u32[]{:S(2)}) collective-permute-start(bf16[80,2048]{1,0:T(8,128)(2,1)} %get-tuple-element.17), channel_id=1, source_target_pairs={{0,1},{1,0},{2,3},{3,2},{4,5},{5,4},{6,7},{7,6},{8,9},{9,8},{10,11... | collective-permute-start | bytes 983048 | tf_op jit(solution)/shard_map/ppermute | solution.py:289
  6.0 9.8 %collective-permute-start.6 = (bf16[80,2048]{1,0:T(8,128)(2,1)}, bf16[80,2048]{1,0:T(8,128)(2,1)S(1)}, u32[]{:S(2)}, u32[]{:S(2)}) collective-permute-start(bf16[80,2048]{1,0:T(8,128)(2,1)} %get-tuple-element.18), channel_id=1, source_target_pairs={{1,2},{2,1},{3,4},{4,3},{5,6},{6,5},{7,8},{8,7},{9,10},{10,9},{11,... | collective-permute-start | bytes 983048 | tf_op jit(solution)/shard_map/ppermute | solution.py:299
  12.2 3.6 %copy-start.5 = (s32[16,24]{1,0:T(8,128)S(1)}, s32[16,24]{1,0:T(8,128)}, u32[]{:S(2)}) copy-start(s32[16,24]{1,0:T(8,128)} %list_ref.3) | copy-start | bytes 4612
  12.2 3.6 %copy-start.6 = (bf16[80,2048]{1,0:T(8,128)(2,1)S(1)}, bf16[80,2048]{1,0:T(8,128)(2,1)}, u32[]{:S(2)}) copy-start(bf16[80,2048]{1,0:T(8,128)(2,1)} %get-tuple-element.16.own_ref) | copy-start | bytes 983044
  12.2 3.6 %copy-start.7 = (bf16[64,2048]{1,0:T(8,128)(2,1)S(1)}, bf16[64,2048]{1,0:T(8,128)(2,1)}, u32[]{:S(2)}) copy-start(bf16[64,2048]{1,0:T(8,128)(2,1)} %get-tuple-element.19.target_ref) | copy-start | bytes 786436
  12.2 8.2 %collective-permute-start.4 = (bf16[2,592,128]{2,1,0:T(8,128)(2,1)S(1)}, bf16[2,592,128]{2,1,0:T(8,128)(2,1)S(1)}, u32[]{:S(2)}, u32[]{:S(2)}) collective-permute-start(bf16[2,592,128]{2,1,0:T(8,128)(2,1)S(1)} %merge.1._.refs_0_), channel_id=1, source_target_pairs={{0,4},{1,5},{2,6},{3,7},{4,0},{5,1},{6,2},{7,3},{8,12},{9,13},{10,... | collective-permute-start | bytes 909320 | tf_op jit(solution)/shard_map/ppermute | solution.py:289
  12.3 14.0 %collective-permute-start.2 = (bf16[2,592,128]{2,1,0:T(8,128)(2,1)S(1)}, bf16[2,592,128]{2,1,0:T(8,128)(2,1)S(1)}, u32[]{:S(2)}, u32[]{:S(2)}) collective-permute-start(bf16[2,592,128]{2,1,0:T(8,128)(2,1)S(1)} %merge.1._.refs_0_), channel_id=1, source_target_pairs={{0,2},{1,3},{2,0},{3,1},{4,6},{5,7},{6,4},{7,5},{8,10},{9,11},{10,... | collective-permute-start | bytes 909320 | tf_op jit(solution)/shard_map/ppermute | solution.py:289
  12.6 22.0 %collective-permute-start.1 = (bf16[2,592,128]{2,1,0:T(8,128)(2,1)S(1)}, bf16[2,592,128]{2,1,0:T(8,128)(2,1)S(1)}, u32[]{:S(2)}, u32[]{:S(2)}) collective-permute-start(bf16[2,592,128]{2,1,0:T(8,128)(2,1)S(1)} %merge.1._.refs_0_), channel_id=1, source_target_pairs={{0,1},{1,0},{2,3},{3,2},{4,5},{5,4},{6,7},{7,6},{8,9},{9,8},{10,11... | collective-permute-start | bytes 909320 | tf_op jit(solution)/shard_map/ppermute | solution.py:289
  20.3 14.2 %copy-start.9 = (s32[2,8]{1,0:T(2,128)S(1)}, s32[2,8]{1,0:T(2,128)}, u32[]{:S(2)}) copy-start(s32[2,8]{1,0:T(2,128)} %param.19) | copy-start | bytes 196
  20.3 14.2 %copy-start.8 = (s32[16,16]{1,0:T(8,128)S(1)}, s32[16,16]{1,0:T(8,128)}, u32[]{:S(2)}) copy-start(s32[16,16]{1,0:T(8,128)} %param.17) | copy-start | bytes 3076
  20.4 15.3 %copy-start.2 = (bf16[16,128,64]{1,2,0:T(8,128)(2,1)S(1)}, bf16[16,128,64]{1,2,0:T(8,128)(2,1)}, u32[]{:S(2)}) copy-start(bf16[16,128,64]{1,2,0:T(8,128)(2,1)} %param.12) | copy-start | bytes 786436
  20.4 15.3 %copy-start.3 = (bf16[16,64,64]{2,1,0:T(8,128)(2,1)S(1)}, bf16[16,64,64]{2,1,0:T(8,128)(2,1)}, u32[]{:S(2)}) copy-start(bf16[16,64,64]{2,1,0:T(8,128)(2,1)} %refs_12_.1) | copy-start | bytes 393220
  20.5 13.3 %collective-permute-start.8 = (bf16[2,592,128]{2,1,0:T(8,128)(2,1)S(1)}, bf16[2,592,128]{2,1,0:T(8,128)(2,1)S(1)}, u32[]{:S(2)}, u32[]{:S(2)}) collective-permute-start(bf16[2,592,128]{2,1,0:T(8,128)(2,1)S(1)} %collective-permute-done.4._.refs_4_), channel_id=1, source_target_pairs={{0,2},{1,3},{2,0},{3,1},{4,6},{5,7},{6,4},{7,5},{8,10},{9,11},{10,... | collective-permute-start | bytes 909320 | tf_op jit(solution)/shard_map/ppermute | solution.py:289
  26.3 8.2 %collective-permute-start.7 = (bf16[2,592,128]{2,1,0:T(8,128)(2,1)S(1)}, bf16[2,592,128]{2,1,0:T(8,128)(2,1)S(1)}, u32[]{:S(2)}, u32[]{:S(2)}) collective-permute-start(bf16[2,592,128]{2,1,0:T(8,128)(2,1)S(1)} %collective-permute-done.4._.refs_4_), channel_id=1, source_target_pairs={{0,1},{1,0},{2,3},{3,2},{4,5},{5,4},{6,7},{7,6},{8,9},{9,8},{10,11... | collective-permute-start | bytes 909320 | tf_op jit(solution)/shard_map/ppermute | solution.py:289
  26.3 8.2 %collective-permute-start.3 = (bf16[2,592,128]{2,1,0:T(8,128)(2,1)S(1)}, bf16[2,592,128]{2,1,0:T(8,128)(2,1)S(1)}, u32[]{:S(2)}, u32[]{:S(2)}) collective-permute-start(bf16[2,592,128]{2,1,0:T(8,128)(2,1)S(1)} %collective-permute-done.2.refs_2_), channel_id=1, source_target_pairs={{0,1},{1,0},{2,3},{3,2},{4,5},{5,4},{6,7},{7,6},{8,9},{9,8},{10,11... | collective-permute-start | bytes 909320 | tf_op jit(solution)/shard_map/ppermute | solution.py:289
  33.7 2.0 %collective-permute-start.9 = (bf16[2,592,128]{2,1,0:T(8,128)(2,1)S(1)}, bf16[2,592,128]{2,1,0:T(8,128)(2,1)S(1)}, u32[]{:S(2)}, u32[]{:S(2)}) collective-permute-start(bf16[2,592,128]{2,1,0:T(8,128)(2,1)S(1)} %collective-permute-done.8.refs_6_), channel_id=1, source_target_pairs={{0,1},{1,0},{2,3},{3,2},{4,5},{5,4},{6,7},{7,6},{8,9},{9,8},{10,11... | collective-permute-start | bytes 909320 | tf_op jit(solution)/shard_map/ppermute | solution.py:289

commit v5 on v4

--- a/solution.py
+++ b/solution.py
@@ -57,7 +57,7 @@
     return jnp.where(rows < 5, high, jnp.where(rows < 10, mid, low)).astype(BF)
 
 
-def pack_kernel(me_ref, in_hbm, geo_hbm, basis_hbm, transfer_hbm, send_hbm, shard_ref, inner_ref, outer_ref, own_ref, target_ref, in_ref, geo_ref, basis_ref, transfer_ref, send_ref, sems):
+def pack_kernel(me_ref, in_hbm, geo_hbm, basis_hbm, transfer_hbm, send_hbm, shard_ref, inner_ref, first_ref, second_ref, own_ref, target_ref, in_ref, geo_ref, basis_ref, transfer_ref, send_ref, sems):
     pairs = ((geo_hbm, geo_ref), (in_hbm, in_ref), (basis_hbm, basis_ref), (transfer_hbm, transfer_ref), (send_hbm, send_ref))
     copies = [pltpu.make_async_copy(src, dst, sems.at[i]) for i, (src, dst) in enumerate(pairs)]
     for copy in copies:
@@ -74,7 +74,11 @@
     rows = lax.broadcasted_iota(jnp.int32, (FEATS, points), 0)
     side = (1 - 2 * (me_ref[0] & 1)).astype(F32)
     inner_ref[rhs:, :] = source_rows(rows, x - side, y, z, gain)
-    outer_ref[rhs:, :] = source_rows(rows, x + side, y, z, gain)
+    odd = (me_ref[0] & 1) == 1
+    half = points // 2
+    outer = source_rows(rows, x + side, y, z, gain)
+    first_ref[rhs:, :] = jnp.where(odd, outer[:, half:], outer[:, :half])
+    second_ref[rhs:, :] = jnp.where(odd, outer[:, :half], outer[:, half:])
     own_ref[rhs:, :] = source_rows(rows, x, y, z, gain)
     high, mid, low = parts_of(by_row(rows, (x, y, z, x * x + y * y + z * z, jnp.ones_like(x))))
     target_ref[0:FEATS, :] = high.astype(BF)
@@ -84,7 +88,8 @@
     copies[1].wait()
     all_in = in_ref[...]
     inner_ref[:rhs, :] = all_in
-    outer_ref[:rhs, :] = all_in
+    first_ref[:rhs, :] = jnp.where(odd, all_in[:, half:], all_in[:, :half])
+    second_ref[:rhs, :] = jnp.where(odd, all_in[:, :half], all_in[:, half:])
     own_ref[:rhs, :] = all_in
 
     for copy in copies[2:]:
@@ -118,7 +123,8 @@
     shard_ref[at : at + send_ref.shape[0], 0 : send_ref.shape[1]] = send_ref[...].astype(F32).astype(BF)
 
 
-def near_kernel(count, first, me_ref, list_ref, own_ref, inner_ref, outer_ref, target_ref, _, out_ref, block_ref):
+def near_kernel(count, chunk, me_ref, list_ref, own_ref, inner_ref, *refs):
+    outer_refs, (target_ref, _, out_ref, block_ref) = refs[: chunk + 1], refs[chunk + 1 :]
     wide, points = own_ref.shape
     rhs, some = out_ref.shape
     leaves, near = list_ref.shape
@@ -126,8 +132,13 @@
     me = me_ref[0]
     start = me * leaves - REACH
     odd = me & 1
-    for base, ref in ((2 * (1 - odd) * leaves, inner_ref), (leaves, own_ref), (2 * odd * leaves, outer_ref)):
-        for j in range(leaves):
+    first = (leaves // 2) * ((1 - odd) if chunk == 0 else odd)
+    half = leaves // 2
+    near_half, far_half = half * (1 - odd), half * odd
+    fills = [(2 * (1 - odd) * leaves, inner_ref), (leaves, own_ref)]
+    fills += [(2 * odd * leaves + at, ref) for at, ref in zip((near_half, far_half), outer_refs)]
+    for base, ref in fills:
+        for j in range(ref.shape[1] // leaf):
             block_ref[base + j] = ref[:, j * leaf : (j + 1) * leaf]
 
     def blank(side):
@@ -142,7 +153,7 @@
     empty = jnp.zeros((4 * FEATS, leaf), BF)
     blank_tile = jnp.zeros((leaf, leaf), BF)
     for l in range(some // leaf):
-        rows = target_ref[:, (first + l) * leaf : (first + l + 1) * leaf]
+        rows = target_ref[:, pl.ds(pl.multiple_of((first + l) * leaf, leaf), leaf)]
         low = jnp.concatenate([rows, empty], axis=0).T
         high = jnp.concatenate([empty, rows], axis=0).T
         targets = jnp.concatenate(
@@ -247,9 +258,11 @@
         out = dot(pair, jnp.concatenate([basis_ref[l], basis_ref[l + 1]], axis=1))
         for i in range(2):
             j = (l + i) % step
+            columns = slice(j * leaf, (j + 1) * leaf)
+            swapped = near_refs[1 - l // step][:, columns]
+            near = jnp.where(me & 1 == 1, near_refs[l // step][:, columns], swapped)
             out_ref[:, (l + i) * leaf : (l + i + 1) * leaf] = (
-                near_refs[l // step][:, j * leaf : (j + 1) * leaf]
-                + out[i * rhs : (i + 1) * rhs, i * leaf : (i + 1) * leaf]
+                near + out[i * rhs : (i + 1) * rhs, i * leaf : (i + 1) * leaf]
             )
 
 
@@ -267,18 +280,20 @@
     table_rows = -(-count // 16) * 16
     shard_rows = (leaves + uppers) // 2 * rank + table_rows
     wide = jax.ShapeDtypeStruct((rhs + FEATS, points), BF)
+    narrow = jax.ShapeDtypeStruct((rhs + FEATS, points // 2), BF)
     staged = (in_t, geometry, basis_t, transfer, send_leaf[0])
-    shard, to_inner, to_outer, own, targets = pl.pallas_call(
+    shard, to_inner, to_first, to_second, own, targets = pl.pallas_call(
         pack_kernel,
         out_shape=(
             jax.ShapeDtypeStruct((shard_rows, 2 * rhs), BF),
             wide,
-            wide,
+            narrow,
+            narrow,
             wide,
             jax.ShapeDtypeStruct((4 * FEATS, points), BF),
         ),
         in_specs=[SMEM] + [pl.BlockSpec(memory_space=pltpu.HBM)] * 5,
-        out_specs=(VMEM,) * 5,
+        out_specs=(VMEM,) * 6,
         scratch_shapes=[pltpu.VMEM(a.shape, a.dtype) for a in staged] + [pltpu.SemaphoreType.DMA((5,))],
         compiler_params=params(54),
         cost_estimate=cost(2),
@@ -296,9 +311,9 @@
     deep = base.shape[0]
     far_side = swap(base, 8)
     inner = swap(to_inner, 1)
-    outer = lax.ppermute(
-        to_outer, "leaf", [pair for i in range(1, count - 1, 2) for pair in ((i, i + 1), (i + 1, i))]
-    )
+    outer_pairs = [pair for i in range(1, count - 1, 2) for pair in ((i, i + 1), (i + 1, i))]
+    outers = [lax.ppermute(to_first, "leaf", outer_pairs)]
+    outers.append(lax.ppermute(to_second, "leaf", outer_pairs))
     def place(device):
         gap = lax.bitwise_xor(device, me)
         top = gap >> 4
@@ -329,15 +344,15 @@
 
     def near(c, after):
         return pl.pallas_call(
-            functools.partial(near_kernel, count, c * some),
+            functools.partial(near_kernel, count, c),
             out_shape=jax.ShapeDtypeStruct((rhs, some * leaf), F32),
-            in_specs=[SMEM] * 2 + [VMEM] * 4 + [ANY],
+            in_specs=[SMEM] * 2 + [VMEM] * (4 + c) + [ANY],
             out_specs=VMEM,
             scratch_shapes=[pltpu.VMEM((leaves + 2 * REACH, rhs + FEATS, leaf), BF)],
             compiler_params=params(32),
             cost_estimate=cost(5),
             name=f"near{c}",
-        )(me_list, near_list, own, inner, outer, targets, after)
+        )(me_list, near_list, own, inner, *outers[: c + 1], targets, after)
 
     def after(x, others):
         return lax.optimization_barrier((x, *others))[0]

time: 41.7 us -> 40.9 us (0.981)
  the two profiles are of different devices: /device:TPU:15 before, /device:TPU:0 now
where the time goes in v5:
time: 40.9 us; the launch traced here: 40.8 us
  Pallas kernels  19.2 us (47%)
  starting transfers between devices  10.6 us (26%)
  waiting for transfers between devices  10.5 us (26%)
    ppermute x9, waiting for transfers between devices, swap(): return lax.ppermute(x, 'leaf', [(i, i ^ bit) for i in range(count)])  10.5 us
    ppermute x9, starting transfers between devices, swap(): return lax.ppermute(x, 'leaf', [(i, i ^ bit) for i in range(count)])  9.32 us
    pallas_call x2, Pallas kernels, near(): pl.pallas_call(functools.partial(near_kernel, count, c), out_shape=jax.Sh...  9.16 us
    pallas_call x1, Pallas kernels, body(): pl.pallas_call(functools.partial(far_kernel, len(piece), chunks), out_sha...  5.66 us
    pallas_call x1, Pallas kernels, body(): pl.pallas_call(pack_kernel, out_shape=(jax.ShapeDtypeStruct((shard_rows,...  2.64 us
    pallas_call x1, Pallas kernels, body(): pl.pallas_call(coupling_kernel, out_shape=(jax.ShapeDtypeStruct((leaves,...  1.73 us
  transfers between devices with their start and end apart: 11, of which 5 were waited for; matrix products, arithmetic and copies ran while one was open for 0% of the time, Pallas kernels for 27%

profile of v5, /device:TPU:0, one launch (start us, length us, event | category | flops | bytes accessed | tf_op | source)
XLA Modules:
  0.0 40.8 jit_solution(9411592982883857651)
XLA Ops:
  0.0 0.0 copy-start.1
  0.0 0.0 copy-start
  0.0 2.6 %pack.1 = (bf16[592,128]{1,0:T(8,128)(2,1)}, bf16[80,2048]{1,0:T(8,128)(2,1)}, bf16[80,1024]{1,0:T(8,128)(2,1)}, bf16[80,1024]{1,0:T(8,128)(2,1)}, bf16[80,2048]{1,0:T(8,128)(2,1)}, /*index=5*/bf16[64,2048]{1,0:T(8,128)(2,1)}) custom-call(s32[1]{0:T(128)} %bitcast.me_ref, bf16[64,2048]{1,0:T(8,128)(2,1)} %bitcast.10, f32[4,2048]{1,0:T(4,128)} %geo_hbm.1, ...), custom_call_target="tpu_custom_call" | custom-call | flops 2000000000 | bytes 2000000 | tf_op jit(solution)/shard_map/pack/pallas_call | solution.py:285
  2.7 0.0 copy-start.4
  2.7 4.1 %collective-permute-start = (bf16[1,592,128]{2,1,0:T(8,128)(2,1)}, bf16[1,592,128]{2,1,0:T(8,128)(2,1)S(1)}, u32[]{:S(2)}, u32[]{:S(2)}) collective-permute-start(bf16[1,592,128]{2,1,0:T(8,128)(2,1)} %bitcast.8), channel_id=1, source_target_pairs={{0,8},{1,9},{2,10},{3,11},{4,12},{5,13},{6,14},{7,15},{8,0},{9,1},... | collective-permute-start | bytes 454664 | tf_op jit(solution)/shard_map/ppermute | solution.py:304
  6.8 0.0 collective-permute-start.5
  6.8 0.7 %collective-permute-start.6 = (bf16[80,1024]{1,0:T(8,128)(2,1)}, bf16[80,1024]{1,0:T(8,128)(2,1)S(1)}, u32[]{:S(2)}, u32[]{:S(2)}) collective-permute-start(bf16[80,1024]{1,0:T(8,128)(2,1)} %get-tuple-element.19), channel_id=1, source_target_pairs={{1,2},{2,1},{3,4},{4,3},{5,6},{6,5},{7,8},{8,7},{9,10},{10,9},{11,... | collective-permute-start | bytes 491528 | tf_op jit(solution)/shard_map/ppermute | solution.py:315
  7.4 0.7 %collective-permute-start.9 = (bf16[80,1024]{1,0:T(8,128)(2,1)}, bf16[80,1024]{1,0:T(8,128)(2,1)S(1)}, u32[]{:S(2)}, u32[]{:S(2)}) collective-permute-start(bf16[80,1024]{1,0:T(8,128)(2,1)} %get-tuple-element.22), channel_id=1, source_target_pairs={{1,2},{2,1},{3,4},{4,3},{5,6},{6,5},{7,8},{8,7},{9,10},{10,9},{11,... | collective-permute-start | bytes 491528 | tf_op jit(solution)/shard_map/ppermute | solution.py:316
  8.1 0.0 copy-done.1
  8.1 0.0 copy-done
  8.1 1.7 %coupling.1 = (bf16[16,64,1024]{2,1,0:T(8,128)(2,1)S(1)}, bf16[2,64,512]{2,1,0:T(8,128)(2,1)S(1)}) custom-call(bf16[16,16,64,64]{3,2,1,0:T(8,128)(2,1)S(1)} %copy-done, bf16[2,8,64,64]{3,2,1,0:T(8,128)(2,1)S(1)} %copy-done.1), custom_call_target="tpu_custom_call" | custom-call | flops 50000000 | bytes 50000 | tf_op jit(solution)/shard_map/coupling/pallas_call | solution.py:329
  9.9 4.4 %collective-permute-done.b_ref = bf16[1,592,128]{2,1,0:T(8,128)(2,1)S(1)} collective-permute-done((bf16[1,592,128]{2,1,0:T(8,128)(2,1)}, bf16[1,592,128]{2,1,0:T(8,128)(2,1)S(1)}, u32[]{:S(2)}, u32[]{:S(2)}) %collective-permute-start) | collective-permute-done | bytes 151584 | tf_op jit(solution)/shard_map/ppermute | solution.py:304
  14.2 0.0 copy-done.4
  14.2 0.0 copy-start.5
  14.2 0.0 copy-start.6
  14.2 0.0 copy-start.7
  14.3 2.4 %collective-permute-start.4 = (bf16[2,592,128]{2,1,0:T(8,128)(2,1)S(1)}, bf16[2,592,128]{2,1,0:T(8,128)(2,1)S(1)}, u32[]{:S(2)}, u32[]{:S(2)}) collective-permute-start(bf16[2,592,128]{2,1,0:T(8,128)(2,1)S(1)} %merge.1.refs_2_.refs_0_), channel_id=1, source_target_pairs={{0,4},{1,5},{2,6},{3,7},{4,0},{5,1},{6,2},{7,3},{8,12},{9,13},{10,... | collective-permute-start | bytes 909320 | tf_op jit(solution)/shard_map/ppermute | solution.py:304
  16.7 0.6 %collective-permute-start.2 = (bf16[2,592,128]{2,1,0:T(8,128)(2,1)S(1)}, bf16[2,592,128]{2,1,0:T(8,128)(2,1)S(1)}, u32[]{:S(2)}, u32[]{:S(2)}) collective-permute-start(bf16[2,592,128]{2,1,0:T(8,128)(2,1)S(1)} %merge.1.refs_2_.refs_0_), channel_id=1, source_target_pairs={{0,2},{1,3},{2,0},{3,1},{4,6},{5,7},{6,4},{7,5},{8,10},{9,11},{10,... | collective-permute-start | bytes 909320 | tf_op jit(solution)/shard_map/ppermute | solution.py:304
  17.3 0.0 collective-permute-done.6.refs_0_
  17.3 0.8 %collective-permute-start.1 = (bf16[2,592,128]{2,1,0:T(8,128)(2,1)S(1)}, bf16[2,592,128]{2,1,0:T(8,128)(2,1)S(1)}, u32[]{:S(2)}, u32[]{:S(2)}) collective-permute-start(bf16[2,592,128]{2,1,0:T(8,128)(2,1)S(1)} %merge.1.refs_2_.refs_0_), channel_id=1, source_target_pairs={{0,1},{1,0},{2,3},{3,2},{4,5},{5,4},{6,7},{7,6},{8,9},{9,8},{10,11... | collective-permute-start | bytes 909320 | tf_op jit(solution)/shard_map/ppermute | solution.py:304
  18.2 0.0 collective-permute-done.5.inner_ref
  18.2 0.0 copy-done.5
  18.2 0.0 copy-done.6
  18.2 0.0 copy-done.7
  18.2 4.5 %near0.1.refs_8_ = f32[64,1024]{1,0:T(8,128)S(1)} custom-call(s32[1]{0:T(128)} %bitcast.me_ref, s32[16,24]{1,0:T(8,128)S(1)} %copy-done.5, bf16[80,2048]{1,0:T(8,128)(2,1)S(1)} %copy-done.6, bf16[80,2048]{1,0:T(8,128)(2,1)S(1)} %collective-permute-done.5.inner_ref, bf16[80,1024]{1,0:T(8,128)(2,1)S(1)} %collective-permute-done.6.refs_0_, ...), custom_call_target="tpu_custom_call" | custom-call | flops 5000000000 | bytes 5000000 | tf_op jit(solution)/shard_map/near0/pallas_call | solution.py:346
  22.7 0.0 copy-start.9
  22.7 0.0 copy-start.8
  22.7 0.0 copy-start.2
  22.7 0.0 copy-start.3
  22.7 2.0 %collective-permute-done.4.refs_3_.refs_4_ = bf16[2,592,128]{2,1,0:T(8,128)(2,1)S(1)} collective-permute-done((bf16[2,592,128]{2,1,0:T(8,128)(2,1)S(1)}, bf16[2,592,128]{2,1,0:T(8,128)(2,1)S(1)}, u32[]{:S(2)}, u32[]{:S(2)}) %collective-permute-start.4) | collective-permute-done | bytes 303136 | tf_op jit(solution)/shard_map/ppermute | solution.py:304
  24.8 0.9 %collective-permute-start.8 = (bf16[2,592,128]{2,1,0:T(8,128)(2,1)S(1)}, bf16[2,592,128]{2,1,0:T(8,128)(2,1)S(1)}, u32[]{:S(2)}, u32[]{:S(2)}) collective-permute-start(bf16[2,592,128]{2,1,0:T(8,128)(2,1)S(1)} %collective-permute-done.4.refs_3_.refs_4_), channel_id=1, source_target_pairs={{0,2},{1,3},{2,0},{3,1},{4,6},{5,7},{6,4},{7,5},{8,10},{9,11},{10,... | collective-permute-start | bytes 909320 | tf_op jit(solution)/shard_map/ppermute | solution.py:304
  25.7 0.1 collective-permute-start.7
  25.7 0.1 collective-permute-done.2.refs_2_
  25.8 0.4 collective-permute-start.3
  26.2 0.0 collective-permute-done.9.refs_1_
  26.2 4.7 %near1.1.refs_9_ = f32[64,1024]{1,0:T(8,128)S(1)} custom-call(s32[1]{0:T(128)} %bitcast.me_ref, s32[16,24]{1,0:T(8,128)S(1)} %copy-done.5, bf16[80,2048]{1,0:T(8,128)(2,1)S(1)} %copy-done.6, bf16[80,2048]{1,0:T(8,128)(2,1)S(1)} %collective-permute-done.5.inner_ref, bf16[80,1024]{1,0:T(8,128)(2,1)S(1)} %collective-permute-done.6.refs_0_, ...), custom_call_target="tpu_custom_call" | custom-call | flops 5000000000 | bytes 5000000 | tf_op jit(solution)/shard_map/near1/pallas_call | solution.py:346
  30.9 2.5 %collective-permute-done.8.refs_6_ = bf16[2,592,128]{2,1,0:T(8,128)(2,1)S(1)} collective-permute-done((bf16[2,592,128]{2,1,0:T(8,128)(2,1)S(1)}, bf16[2,592,128]{2,1,0:T(8,128)(2,1)S(1)}, u32[]{:S(2)}, u32[]{:S(2)}) %collective-permute-start.8) | collective-permute-done | bytes 303136 | tf_op jit(solution)/shard_map/ppermute | solution.py:304
  33.4 0.0 collective-permute-start.10
  33.4 0.0 copy-done.9
  33.4 0.0 copy-done.8
  33.4 0.0 collective-permute-done.1.refs_1_
  33.4 0.0 collective-permute-done.7.refs_5_
  33.4 0.0 collective-permute-done.3.refs_3_
  33.5 1.5 %collective-permute-done.10.refs_7_ = bf16[2,592,128]{2,1,0:T(8,128)(2,1)S(1)} collective-permute-done((bf16[2,592,128]{2,1,0:T(8,128)(2,1)S(1)}, bf16[2,592,128]{2,1,0:T(8,128)(2,1)S(1)}, u32[]{:S(2)}, u32[]{:S(2)}) %collective-permute-start.10) | collective-permute-done | bytes 303136 | tf_op jit(solution)/shard_map/ppermute | solution.py:304
  35.0 0.0 copy-done.2
  35.0 0.0 copy-done.3
  35.0 5.7 %far.1 = f32[64,2048]{1,0:T(8,128)} custom-call(s32[1]{0:T(128)} %bitcast.me_ref, s32[16,16]{1,0:T(8,128)S(1)} %fusion.1.recv_ref, s32[2,8]{1,0:T(2,128)S(1)} %fusion.3.top_ref, bf16[2,592,128]{2,1,0:T(8,128)(2,1)S(1)} %merge.1.refs_2_.refs_0_, bf16[2,592,128]{2,1,0:T(8,128)(2,1)S(1)} %collective-permute-done.1.refs_1_, ...), custom_call_target="tpu_custom_call" | custom-call | flops 6000000000 | bytes 6000000 | tf_op jit(solution)/shard_map/far/pallas_call | solution.py:381
  (3 shorter events, 0.1 us)
Async XLA Ops:
  0.0 8.1 %copy-start.1 = (bf16[2,8,64,64]{3,2,1,0:T(8,128)(2,1)S(1)}, bf16[2,8,64,64]{3,2,1,0:T(8,128)(2,1)}, u32[]{:S(2)}) copy-start(bf16[2,8,64,64]{3,2,1,0:T(8,128)(2,1)} %top_ref.1) | copy-start | bytes 393220
  0.0 8.1 %copy-start = (bf16[16,16,64,64]{3,2,1,0:T(8,128)(2,1)S(1)}, bf16[16,16,64,64]{3,2,1,0:T(8,128)(2,1)}, u32[]{:S(2)}) copy-start(bf16[16,16,64,64]{3,2,1,0:T(8,128)(2,1)} %c_ref.1) | copy-start | bytes 6291460
  2.7 11.6 %copy-start.4 = (bf16[592,128]{1,0:T(8,128)(2,1)S(1)}, bf16[592,128]{1,0:T(8,128)(2,1)}, u32[]{:S(2)}) copy-start(bf16[592,128]{1,0:T(8,128)(2,1)} %get-tuple-element.15) | copy-start | bytes 454660
  2.7 11.6 %collective-permute-start = (bf16[1,592,128]{2,1,0:T(8,128)(2,1)}, bf16[1,592,128]{2,1,0:T(8,128)(2,1)S(1)}, u32[]{:S(2)}, u32[]{:S(2)}) collective-permute-start(bf16[1,592,128]{2,1,0:T(8,128)(2,1)} %bitcast.8), channel_id=1, source_target_pairs={{0,8},{1,9},{2,10},{3,11},{4,12},{5,13},{6,14},{7,15},{8,0},{9,1},... | collective-permute-start | bytes 454664 | tf_op jit(solution)/shard_map/ppermute | solution.py:304
  6.8 11.4 %collective-permute-start.5 = (bf16[80,2048]{1,0:T(8,128)(2,1)}, bf16[80,2048]{1,0:T(8,128)(2,1)S(1)}, u32[]{:S(2)}, u32[]{:S(2)}) collective-permute-start(bf16[80,2048]{1,0:T(8,128)(2,1)} %get-tuple-element.18), channel_id=1, source_target_pairs={{0,1},{1,0},{2,3},{3,2},{4,5},{5,4},{6,7},{7,6},{8,9},{9,8},{10,11... | collective-permute-start | bytes 983048 | tf_op jit(solution)/shard_map/ppermute | solution.py:304
  6.8 10.6 %collective-permute-start.6 = (bf16[80,1024]{1,0:T(8,128)(2,1)}, bf16[80,1024]{1,0:T(8,128)(2,1)S(1)}, u32[]{:S(2)}, u32[]{:S(2)}) collective-permute-start(bf16[80,1024]{1,0:T(8,128)(2,1)} %get-tuple-element.19), channel_id=1, source_target_pairs={{1,2},{2,1},{3,4},{4,3},{5,6},{6,5},{7,8},{8,7},{9,10},{10,9},{11,... | collective-permute-start | bytes 491528 | tf_op jit(solution)/shard_map/ppermute | solution.py:315
  7.4 18.7 %collective-permute-start.9 = (bf16[80,1024]{1,0:T(8,128)(2,1)}, bf16[80,1024]{1,0:T(8,128)(2,1)S(1)}, u32[]{:S(2)}, u32[]{:S(2)}) collective-permute-start(bf16[80,1024]{1,0:T(8,128)(2,1)} %get-tuple-element.22), channel_id=1, source_target_pairs={{1,2},{2,1},{3,4},{4,3},{5,6},{6,5},{7,8},{8,7},{9,10},{10,9},{11,... | collective-permute-start | bytes 491528 | tf_op jit(solution)/shard_map/ppermute | solution.py:316
  14.2 4.0 %copy-start.5 = (s32[16,24]{1,0:T(8,128)S(1)}, s32[16,24]{1,0:T(8,128)}, u32[]{:S(2)}) copy-start(s32[16,24]{1,0:T(8,128)} %list_ref.3) | copy-start | bytes 4612
  14.2 4.0 %copy-start.6 = (bf16[80,2048]{1,0:T(8,128)(2,1)S(1)}, bf16[80,2048]{1,0:T(8,128)(2,1)}, u32[]{:S(2)}) copy-start(bf16[80,2048]{1,0:T(8,128)(2,1)} %get-tuple-element.17.own_ref) | copy-start | bytes 983044
  14.2 4.0 %copy-start.7 = (bf16[64,2048]{1,0:T(8,128)(2,1)S(1)}, bf16[64,2048]{1,0:T(8,128)(2,1)}, u32[]{:S(2)}) copy-start(bf16[64,2048]{1,0:T(8,128)(2,1)} %get-tuple-element.20.refs_1_.refs_2_) | copy-start | bytes 786436
  14.3 10.5 %collective-permute-start.4 = (bf16[2,592,128]{2,1,0:T(8,128)(2,1)S(1)}, bf16[2,592,128]{2,1,0:T(8,128)(2,1)S(1)}, u32[]{:S(2)}, u32[]{:S(2)}) collective-permute-start(bf16[2,592,128]{2,1,0:T(8,128)(2,1)S(1)} %merge.1.refs_2_.refs_0_), channel_id=1, source_target_pairs={{0,4},{1,5},{2,6},{3,7},{4,0},{5,1},{6,2},{7,3},{8,12},{9,13},{10,... | collective-permute-start | bytes 909320 | tf_op jit(solution)/shard_map/ppermute | solution.py:304
  16.7 9.1 %collective-permute-start.2 = (bf16[2,592,128]{2,1,0:T(8,128)(2,1)S(1)}, bf16[2,592,128]{2,1,0:T(8,128)(2,1)S(1)}, u32[]{:S(2)}, u32[]{:S(2)}) collective-permute-start(bf16[2,592,128]{2,1,0:T(8,128)(2,1)S(1)} %merge.1.refs_2_.refs_0_), channel_id=1, source_target_pairs={{0,2},{1,3},{2,0},{3,1},{4,6},{5,7},{6,4},{7,5},{8,10},{9,11},{10,... | collective-permute-start | bytes 909320 | tf_op jit(solution)/shard_map/ppermute | solution.py:304
  17.3 16.1 %collective-permute-start.1 = (bf16[2,592,128]{2,1,0:T(8,128)(2,1)S(1)}, bf16[2,592,128]{2,1,0:T(8,128)(2,1)S(1)}, u32[]{:S(2)}, u32[]{:S(2)}) collective-permute-start(bf16[2,592,128]{2,1,0:T(8,128)(2,1)S(1)} %merge.1.refs_2_.refs_0_), channel_id=1, source_target_pairs={{0,1},{1,0},{2,3},{3,2},{4,5},{5,4},{6,7},{7,6},{8,9},{9,8},{10,11... | collective-permute-start | bytes 909320 | tf_op jit(solution)/shard_map/ppermute | solution.py:304
  22.7 10.7 %copy-start.9 = (s32[2,8]{1,0:T(2,128)S(1)}, s32[2,8]{1,0:T(2,128)}, u32[]{:S(2)}) copy-start(s32[2,8]{1,0:T(2,128)} %param.19) | copy-start | bytes 196
  22.7 10.7 %copy-start.8 = (s32[16,16]{1,0:T(8,128)S(1)}, s32[16,16]{1,0:T(8,128)}, u32[]{:S(2)}) copy-start(s32[16,16]{1,0:T(8,128)} %param.17) | copy-start | bytes 3076
  22.7 12.2 %copy-start.2 = (bf16[16,128,64]{1,2,0:T(8,128)(2,1)S(1)}, bf16[16,128,64]{1,2,0:T(8,128)(2,1)}, u32[]{:S(2)}) copy-start(bf16[16,128,64]{1,2,0:T(8,128)(2,1)} %param.12) | copy-start | bytes 786436
  22.7 12.2 %copy-start.3 = (bf16[16,64,64]{2,1,0:T(8,128)(2,1)S(1)}, bf16[16,64,64]{2,1,0:T(8,128)(2,1)}, u32[]{:S(2)}) copy-start(bf16[16,64,64]{2,1,0:T(8,128)(2,1)} %refs_12_.1) | copy-start | bytes 393220
  24.8 8.6 %collective-permute-start.8 = (bf16[2,592,128]{2,1,0:T(8,128)(2,1)S(1)}, bf16[2,592,128]{2,1,0:T(8,128)(2,1)S(1)}, u32[]{:S(2)}, u32[]{:S(2)}) collective-permute-start(bf16[2,592,128]{2,1,0:T(8,128)(2,1)S(1)} %collective-permute-done.4.refs_3_.refs_4_), channel_id=1, source_target_pairs={{0,2},{1,3},{2,0},{3,1},{4,6},{5,7},{6,4},{7,5},{8,10},{9,11},{10,... | collective-permute-start | bytes 909320 | tf_op jit(solution)/shard_map/ppermute | solution.py:304
  25.7 7.8 %collective-permute-start.7 = (bf16[2,592,128]{2,1,0:T(8,128)(2,1)S(1)}, bf16[2,592,128]{2,1,0:T(8,128)(2,1)S(1)}, u32[]{:S(2)}, u32[]{:S(2)}) collective-permute-start(bf16[2,592,128]{2,1,0:T(8,128)(2,1)S(1)} %collective-permute-done.4.refs_3_.refs_4_), channel_id=1, source_target_pairs={{0,1},{1,0},{2,3},{3,2},{4,5},{5,4},{6,7},{7,6},{8,9},{9,8},{10,11... | collective-permute-start | bytes 909320 | tf_op jit(solution)/shard_map/ppermute | solution.py:304
  25.8 7.6 %collective-permute-start.3 = (bf16[2,592,128]{2,1,0:T(8,128)(2,1)S(1)}, bf16[2,592,128]{2,1,0:T(8,128)(2,1)S(1)}, u32[]{:S(2)}, u32[]{:S(2)}) collective-permute-start(bf16[2,592,128]{2,1,0:T(8,128)(2,1)S(1)} %collective-permute-done.2.refs_2_), channel_id=1, source_target_pairs={{0,1},{1,0},{2,3},{3,2},{4,5},{5,4},{6,7},{7,6},{8,9},{9,8},{10,11... | collective-permute-start | bytes 909320 | tf_op jit(solution)/shard_map/ppermute | solution.py:304
  33.4 1.6 %collective-permute-start.10 = (bf16[2,592,128]{2,1,0:T(8,128)(2,1)S(1)}, bf16[2,592,128]{2,1,0:T(8,128)(2,1)S(1)}, u32[]{:S(2)}, u32[]{:S(2)}) collective-permute-start(bf16[2,592,128]{2,1,0:T(8,128)(2,1)S(1)} %collective-permute-done.8.refs_6_), channel_id=1, source_target_pairs={{0,1},{1,0},{2,3},{3,2},{4,5},{5,4},{6,7},{7,6},{8,9},{9,8},{10,11... | collective-permute-start | bytes 909320 | tf_op jit(solution)/shard_map/ppermute | solution.py:304

commit v6 on v5

--- a/solution.py
+++ b/solution.py
@@ -178,13 +178,13 @@
         out_ref[:, l * leaf : (l + 1) * leaf] = turned[0:rhs] + turned[rhs:]
 
 
-def merge_kernel(a_ref, b_ref, _, out_ref):
+def merge_kernel(a_ref, b_ref, out_ref):
     deep = a_ref.shape[0]
     out_ref[0:deep] = a_ref[...]
     out_ref[deep:] = b_ref[...]
 
 
-def coupling_kernel(c_ref, top_ref, out_ref, top_out_ref):
+def coupling_kernel(_, c_ref, top_ref, out_ref, top_out_ref):
     leaves, far, rank, _ = c_ref.shape
     uppers, top, _, _ = top_ref.shape
     for p in range(uppers):
@@ -326,19 +326,6 @@
     recv_words = place(recv_slot // slots) * 256 + recv_slot % slots
     top_words = place(top_source // uppers) * 256 + top_source % uppers
 
-    coupling, top_wide = pl.pallas_call(
-        coupling_kernel,
-        out_shape=(
-            jax.ShapeDtypeStruct((leaves, rank, far * rank), BF),
-            jax.ShapeDtypeStruct((uppers, rank, top_source.shape[1] * rank), BF),
-        ),
-        in_specs=[VMEM, VMEM],
-        out_specs=(VMEM,) * 2,
-        compiler_params=params(32),
-        cost_estimate=cost(0.05),
-        name="coupling",
-    )(leaf_coupling, top_coupling)
-
     chunks = 2
     some = leaves // chunks
 
@@ -360,12 +347,12 @@
     both = pl.pallas_call(
         merge_kernel,
         out_shape=jax.ShapeDtypeStruct((2 * deep, *base.shape[1:]), BF),
-        in_specs=[VMEM] * 2 + [ANY],
+        in_specs=[VMEM] * 2,
         out_specs=VMEM,
         compiler_params=params(32),
         cost_estimate=cost(3),
         name="merge",
-    )(base, far_side, coupling)
+    )(base, far_side)
     piece = {0: both}
     piece[4] = swap(both, 4)
     piece[2] = swap(both, 2)
@@ -375,7 +362,19 @@
     for j in (0, 4, 2):
         piece[j + 1] = swap(piece[j], 1)
     nears += [near(1, piece[4])]
-    piece[6] = after(piece[6], nears)
+    coupling, top_wide = pl.pallas_call(
+        coupling_kernel,
+        out_shape=(
+            jax.ShapeDtypeStruct((leaves, rank, far * rank), BF),
+            jax.ShapeDtypeStruct((uppers, rank, top_source.shape[1] * rank), BF),
+        ),
+        in_specs=[ANY, VMEM, VMEM],
+        out_specs=(VMEM,) * 2,
+        compiler_params=params(32),
+        cost_estimate=cost(0.05),
+        name="coupling",
+    )(nears[1], leaf_coupling, top_coupling)
+    piece[6] = after(piece[6], [*nears, coupling])
     piece[7] = swap(piece[6], 1)
 
     out = pl.pallas_call(

time: 40.9 us -> 40.1 us (0.980)
  starting transfers between devices: 10.6 us -> 9.01 us
  local copies, waits for them, and re-layouts: 0.05 us -> 0.96 us
    ppermute x9, starting transfers between devices: 9.32 us -> 7.68 us  [swap(): return lax.ppermute(x, 'leaf', [(i, i ^ bit) for i in range(count)])]
    unnamed x20, local copies, waits for them, and re-layouts: 0.05 us -> 0.96 us
  transfers between devices with their start and end apart: 11 -> 11, of which waited for: 5 -> 4; matrix products, arithmetic and copies ran while one was open for 0% -> 0% of each run, Pallas kernels for 27% -> 27%
where the time goes in v6:
time: 40.1 us; the launch traced here: 39.9 us
  Pallas kernels  19.1 us (48%)
  waiting for transfers between devices  10.5 us (26%)
  starting transfers between devices  9.01 us (22%)
  local copies, waits for them, and re-layouts  0.96 us (2%)
    ppermute x9, waiting for transfers between devices, swap(): return lax.ppermute(x, 'leaf', [(i, i ^ bit) for i in range(count)])  10.5 us
    pallas_call x2, Pallas kernels, near(): pl.pallas_call(functools.partial(near_kernel, count, c), out_shape=jax.Sh...  9.16 us
    ppermute x9, starting transfers between devices, swap(): return lax.ppermute(x, 'leaf', [(i, i ^ bit) for i in range(count)])  7.68 us
    pallas_call x1, Pallas kernels, body(): pl.pallas_call(functools.partial(far_kernel, len(piece), chunks), out_sha...  5.67 us
    pallas_call x1, Pallas kernels, body(): pl.pallas_call(pack_kernel, out_shape=(jax.ShapeDtypeStruct((shard_rows,...  2.5 us
    pallas_call x1, Pallas kernels, body(): pl.pallas_call(coupling_kernel, out_shape=(jax.ShapeDtypeStruct((leaves,...  1.73 us
    unnamed x20, local copies, waits for them, and re-layouts  0.96 us
  transfers between devices with their start and end apart: 11, of which 4 were waited for; matrix products, arithmetic and copies ran while one was open for 0% of the time, Pallas kernels for 27%

profile of v6, /device:TPU:0, one launch (start us, length us, event | category | flops | bytes accessed | tf_op | source)
XLA Modules:
  0.0 39.9 jit_solution(7222858913137695364)
XLA Ops:
  0.0 2.5 %pack.1 = (bf16[592,128]{1,0:T(8,128)(2,1)}, bf16[80,2048]{1,0:T(8,128)(2,1)}, bf16[80,1024]{1,0:T(8,128)(2,1)}, bf16[80,1024]{1,0:T(8,128)(2,1)}, bf16[80,2048]{1,0:T(8,128)(2,1)}, /*index=5*/bf16[64,2048]{1,0:T(8,128)(2,1)}) custom-call(s32[1]{0:T(128)} %bitcast.me_ref, bf16[64,2048]{1,0:T(8,128)(2,1)} %bitcast.10, f32[4,2048]{1,0:T(4,128)} %geo_hbm.1, ...), custom_call_target="tpu_custom_call" | custom-call | flops 2000000000 | bytes 2000000 | tf_op jit(solution)/shard_map/pack/pallas_call | solution.py:285
  2.5 4.1 %collective-permute-start = (bf16[1,592,128]{2,1,0:T(8,128)(2,1)}, bf16[1,592,128]{2,1,0:T(8,128)(2,1)S(1)}, u32[]{:S(2)}, u32[]{:S(2)}) collective-permute-start(bf16[1,592,128]{2,1,0:T(8,128)(2,1)} %bitcast.8), channel_id=1, source_target_pairs={{0,8},{1,9},{2,10},{3,11},{4,12},{5,13},{6,14},{7,15},{8,0},{9,1},... | collective-permute-start | bytes 454664 | tf_op jit(solution)/shard_map/ppermute | solution.py:304
  6.6 0.0 collective-permute-start.5
  6.6 0.7 %collective-permute-start.6 = (bf16[80,1024]{1,0:T(8,128)(2,1)}, bf16[80,1024]{1,0:T(8,128)(2,1)S(1)}, u32[]{:S(2)}, u32[]{:S(2)}) collective-permute-start(bf16[80,1024]{1,0:T(8,128)(2,1)} %get-tuple-element.18), channel_id=1, source_target_pairs={{1,2},{2,1},{3,4},{4,3},{5,6},{6,5},{7,8},{8,7},{9,10},{10,9},{11,... | collective-permute-start | bytes 491528 | tf_op jit(solution)/shard_map/ppermute | solution.py:315
  7.3 0.7 %collective-permute-start.9 = (bf16[80,1024]{1,0:T(8,128)(2,1)}, bf16[80,1024]{1,0:T(8,128)(2,1)S(1)}, u32[]{:S(2)}, u32[]{:S(2)}) collective-permute-start(bf16[80,1024]{1,0:T(8,128)(2,1)} %get-tuple-element.21), channel_id=1, source_target_pairs={{1,2},{2,1},{3,4},{4,3},{5,6},{6,5},{7,8},{8,7},{9,10},{10,9},{11,... | collective-permute-start | bytes 491528 | tf_op jit(solution)/shard_map/ppermute | solution.py:316
  8.0 6.1 %collective-permute-done.b_ref = bf16[1,592,128]{2,1,0:T(8,128)(2,1)S(1)} collective-permute-done((bf16[1,592,128]{2,1,0:T(8,128)(2,1)}, bf16[1,592,128]{2,1,0:T(8,128)(2,1)S(1)}, u32[]{:S(2)}, u32[]{:S(2)}) %collective-permute-start) | collective-permute-done | bytes 151584 | tf_op jit(solution)/shard_map/ppermute | solution.py:304
  14.1 0.0 copy-start.4
  14.1 0.9 %copy-done.4 = bf16[592,128]{1,0:T(8,128)(2,1)S(1)} copy-done((bf16[592,128]{1,0:T(8,128)(2,1)S(1)}, bf16[592,128]{1,0:T(8,128)(2,1)}, u32[]{:S(2)}) %copy-start.4) | copy-done | bytes 151576
  15.0 0.0 copy-start.5
  15.0 0.0 copy-start.6
  15.0 0.0 copy-start.7
  15.0 0.8 %collective-permute-start.4 = (bf16[2,592,128]{2,1,0:T(8,128)(2,1)S(1)}, bf16[2,592,128]{2,1,0:T(8,128)(2,1)S(1)}, u32[]{:S(2)}, u32[]{:S(2)}) collective-permute-start(bf16[2,592,128]{2,1,0:T(8,128)(2,1)S(1)} %merge.1.refs_2_.refs_0_), channel_id=1, source_target_pairs={{0,4},{1,5},{2,6},{3,7},{4,0},{5,1},{6,2},{7,3},{8,12},{9,13},{10,... | collective-permute-start | bytes 909320 | tf_op jit(solution)/shard_map/ppermute | solution.py:304
  15.8 1.7 %collective-permute-start.2 = (bf16[2,592,128]{2,1,0:T(8,128)(2,1)S(1)}, bf16[2,592,128]{2,1,0:T(8,128)(2,1)S(1)}, u32[]{:S(2)}, u32[]{:S(2)}) collective-permute-start(bf16[2,592,128]{2,1,0:T(8,128)(2,1)S(1)} %merge.1.refs_2_.refs_0_), channel_id=1, source_target_pairs={{0,2},{1,3},{2,0},{3,1},{4,6},{5,7},{6,4},{7,5},{8,10},{9,11},{10,... | collective-permute-start | bytes 909320 | tf_op jit(solution)/shard_map/ppermute | solution.py:304
  17.5 0.0 collective-permute-done.6.refs_0_
  17.5 0.0 collective-permute-start.1
  17.5 0.0 collective-permute-done.5.inner_ref
  17.5 0.0 copy-done.5
  17.5 0.0 copy-done.6
  17.5 0.0 copy-done.7
  17.5 4.5 %near0.1.refs_8_ = f32[64,1024]{1,0:T(8,128)S(1)} custom-call(s32[1]{0:T(128)} %bitcast.me_ref, s32[16,24]{1,0:T(8,128)S(1)} %copy-done.5, bf16[80,2048]{1,0:T(8,128)(2,1)S(1)} %copy-done.6, bf16[80,2048]{1,0:T(8,128)(2,1)S(1)} %collective-permute-done.5.inner_ref, bf16[80,1024]{1,0:T(8,128)(2,1)S(1)} %collective-permute-done.6.refs_0_, ...), custom_call_target="tpu_custom_call" | custom-call | flops 5000000000 | bytes 5000000 | tf_op jit(solution)/shard_map/near0/pallas_call | solution.py:333
  22.0 0.0 copy-start
  22.0 0.0 copy-start.1
  22.0 2.6 %collective-permute-done.4.refs_3_.refs_4_ = bf16[2,592,128]{2,1,0:T(8,128)(2,1)S(1)} collective-permute-done((bf16[2,592,128]{2,1,0:T(8,128)(2,1)S(1)}, bf16[2,592,128]{2,1,0:T(8,128)(2,1)S(1)}, u32[]{:S(2)}, u32[]{:S(2)}) %collective-permute-start.4) | collective-permute-done | bytes 303136 | tf_op jit(solution)/shard_map/ppermute | solution.py:304
  24.6 0.6 %collective-permute-start.8 = (bf16[2,592,128]{2,1,0:T(8,128)(2,1)S(1)}, bf16[2,592,128]{2,1,0:T(8,128)(2,1)S(1)}, u32[]{:S(2)}, u32[]{:S(2)}) collective-permute-start(bf16[2,592,128]{2,1,0:T(8,128)(2,1)S(1)} %collective-permute-done.4.refs_3_.refs_4_), channel_id=1, source_target_pairs={{0,2},{1,3},{2,0},{3,1},{4,6},{5,7},{6,4},{7,5},{8,10},{9,11},{10,... | collective-permute-start | bytes 909320 | tf_op jit(solution)/shard_map/ppermute | solution.py:304
  25.2 0.0 collective-permute-start.7
  25.2 0.0 collective-permute-done.2.refs_2_
  25.2 0.5 %collective-permute-start.3 = (bf16[2,592,128]{2,1,0:T(8,128)(2,1)S(1)}, bf16[2,592,128]{2,1,0:T(8,128)(2,1)S(1)}, u32[]{:S(2)}, u32[]{:S(2)}) collective-permute-start(bf16[2,592,128]{2,1,0:T(8,128)(2,1)S(1)} %collective-permute-done.2.refs_2_), channel_id=1, source_target_pairs={{0,1},{1,0},{2,3},{3,2},{4,5},{5,4},{6,7},{7,6},{8,9},{9,8},{10,11... | collective-permute-start | bytes 909320 | tf_op jit(solution)/shard_map/ppermute | solution.py:304
  25.7 0.0 collective-permute-done.9.refs_1_
  25.7 4.7 %near1.1._.refs_9_ = f32[64,1024]{1,0:T(8,128)S(1)} custom-call(s32[1]{0:T(128)} %bitcast.me_ref, s32[16,24]{1,0:T(8,128)S(1)} %copy-done.5, bf16[80,2048]{1,0:T(8,128)(2,1)S(1)} %copy-done.6, bf16[80,2048]{1,0:T(8,128)(2,1)S(1)} %collective-permute-done.5.inner_ref, bf16[80,1024]{1,0:T(8,128)(2,1)S(1)} %collective-permute-done.6.refs_0_, ...), custom_call_target="tpu_custom_call" | custom-call | flops 5000000000 | bytes 5000000 | tf_op jit(solution)/shard_map/near1/pallas_call | solution.py:333
  30.4 0.0 copy-done
  30.4 0.0 copy-done.1
  30.4 0.0 copy-start.9
  30.5 0.0 copy-start.8
  30.5 0.0 copy-start.2
  30.5 0.0 copy-start.3
  30.5 1.7 %coupling.1 = (bf16[16,64,1024]{2,1,0:T(8,128)(2,1)S(1)}, bf16[2,64,512]{2,1,0:T(8,128)(2,1)S(1)}) custom-call(f32[64,1024]{1,0:T(8,128)S(1)} %near1.1._.refs_9_, bf16[16,16,64,64]{3,2,1,0:T(8,128)(2,1)S(1)} %copy-done, bf16[2,8,64,64]{3,2,1,0:T(8,128)(2,1)S(1)} %copy-done.1), custom_call_target="tpu_custom_call" | custom-call | flops 50000000 | bytes 50000 | tf_op jit(solution)/shard_map/coupling/pallas_call | solution.py:365
  32.2 0.3 collective-permute-done.8.refs_6_
  32.5 0.0 collective-permute-start.10
  32.5 0.0 copy-done.9
  32.5 0.0 copy-done.8
  32.6 0.0 collective-permute-done.1.refs_1_
  32.6 0.0 collective-permute-done.3.refs_3_
  32.6 0.0 collective-permute-done.7.refs_5_
  32.6 1.5 %collective-permute-done.10.refs_7_ = bf16[2,592,128]{2,1,0:T(8,128)(2,1)S(1)} collective-permute-done((bf16[2,592,128]{2,1,0:T(8,128)(2,1)S(1)}, bf16[2,592,128]{2,1,0:T(8,128)(2,1)S(1)}, u32[]{:S(2)}, u32[]{:S(2)}) %collective-permute-start.10) | collective-permute-done | bytes 303136 | tf_op jit(solution)/shard_map/ppermute | solution.py:304
  34.1 0.0 copy-done.2
  34.1 0.0 copy-done.3
  34.1 5.7 %far.1 = f32[64,2048]{1,0:T(8,128)} custom-call(s32[1]{0:T(128)} %bitcast.me_ref, s32[16,16]{1,0:T(8,128)S(1)} %fusion.1.recv_ref, s32[2,8]{1,0:T(2,128)S(1)} %fusion.3.top_ref, bf16[2,592,128]{2,1,0:T(8,128)(2,1)S(1)} %merge.1.refs_2_.refs_0_, bf16[2,592,128]{2,1,0:T(8,128)(2,1)S(1)} %collective-permute-done.1.refs_1_, ...), custom_call_target="tpu_custom_call" | custom-call | flops 6000000000 | bytes 6000000 | tf_op jit(solution)/shard_map/far/pallas_call | solution.py:380
  (3 shorter events, 0.1 us)
Async XLA Ops:
  2.5 11.6 %collective-permute-start = (bf16[1,592,128]{2,1,0:T(8,128)(2,1)}, bf16[1,592,128]{2,1,0:T(8,128)(2,1)S(1)}, u32[]{:S(2)}, u32[]{:S(2)}) collective-permute-start(bf16[1,592,128]{2,1,0:T(8,128)(2,1)} %bitcast.8), channel_id=1, source_target_pairs={{0,8},{1,9},{2,10},{3,11},{4,12},{5,13},{6,14},{7,15},{8,0},{9,1},... | collective-permute-start | bytes 454664 | tf_op jit(solution)/shard_map/ppermute | solution.py:304
  6.6 10.9 %collective-permute-start.5 = (bf16[80,2048]{1,0:T(8,128)(2,1)}, bf16[80,2048]{1,0:T(8,128)(2,1)S(1)}, u32[]{:S(2)}, u32[]{:S(2)}) collective-permute-start(bf16[80,2048]{1,0:T(8,128)(2,1)} %get-tuple-element.17), channel_id=1, source_target_pairs={{0,1},{1,0},{2,3},{3,2},{4,5},{5,4},{6,7},{7,6},{8,9},{9,8},{10,11... | collective-permute-start | bytes 983048 | tf_op jit(solution)/shard_map/ppermute | solution.py:304
  6.6 10.9 %collective-permute-start.6 = (bf16[80,1024]{1,0:T(8,128)(2,1)}, bf16[80,1024]{1,0:T(8,128)(2,1)S(1)}, u32[]{:S(2)}, u32[]{:S(2)}) collective-permute-start(bf16[80,1024]{1,0:T(8,128)(2,1)} %get-tuple-element.18), channel_id=1, source_target_pairs={{1,2},{2,1},{3,4},{4,3},{5,6},{6,5},{7,8},{8,7},{9,10},{10,9},{11,... | collective-permute-start | bytes 491528 | tf_op jit(solution)/shard_map/ppermute | solution.py:315
  7.3 18.4 %collective-permute-start.9 = (bf16[80,1024]{1,0:T(8,128)(2,1)}, bf16[80,1024]{1,0:T(8,128)(2,1)S(1)}, u32[]{:S(2)}, u32[]{:S(2)}) collective-permute-start(bf16[80,1024]{1,0:T(8,128)(2,1)} %get-tuple-element.21), channel_id=1, source_target_pairs={{1,2},{2,1},{3,4},{4,3},{5,6},{6,5},{7,8},{8,7},{9,10},{10,9},{11,... | collective-permute-start | bytes 491528 | tf_op jit(solution)/shard_map/ppermute | solution.py:316
  14.1 0.9 %copy-start.4 = (bf16[592,128]{1,0:T(8,128)(2,1)S(1)}, bf16[592,128]{1,0:T(8,128)(2,1)}, u32[]{:S(2)}) copy-start(bf16[592,128]{1,0:T(8,128)(2,1)} %get-tuple-element.15) | copy-start | bytes 454660
  15.0 2.5 %copy-start.5 = (s32[16,24]{1,0:T(8,128)S(1)}, s32[16,24]{1,0:T(8,128)}, u32[]{:S(2)}) copy-start(s32[16,24]{1,0:T(8,128)} %list_ref.3) | copy-start | bytes 4612
  15.0 2.5 %copy-start.6 = (bf16[80,2048]{1,0:T(8,128)(2,1)S(1)}, bf16[80,2048]{1,0:T(8,128)(2,1)}, u32[]{:S(2)}) copy-start(bf16[80,2048]{1,0:T(8,128)(2,1)} %get-tuple-element.16.own_ref) | copy-start | bytes 983044
  15.0 2.5 %copy-start.7 = (bf16[64,2048]{1,0:T(8,128)(2,1)S(1)}, bf16[64,2048]{1,0:T(8,128)(2,1)}, u32[]{:S(2)}) copy-start(bf16[64,2048]{1,0:T(8,128)(2,1)} %get-tuple-element.19.refs_1_.refs_2_) | copy-start | bytes 786436
  15.0 9.6 %collective-permute-start.4 = (bf16[2,592,128]{2,1,0:T(8,128)(2,1)S(1)}, bf16[2,592,128]{2,1,0:T(8,128)(2,1)S(1)}, u32[]{:S(2)}, u32[]{:S(2)}) collective-permute-start(bf16[2,592,128]{2,1,0:T(8,128)(2,1)S(1)} %merge.1.refs_2_.refs_0_), channel_id=1, source_target_pairs={{0,4},{1,5},{2,6},{3,7},{4,0},{5,1},{6,2},{7,3},{8,12},{9,13},{10,... | collective-permute-start | bytes 909320 | tf_op jit(solution)/shard_map/ppermute | solution.py:304
  15.8 9.4 %collective-permute-start.2 = (bf16[2,592,128]{2,1,0:T(8,128)(2,1)S(1)}, bf16[2,592,128]{2,1,0:T(8,128)(2,1)S(1)}, u32[]{:S(2)}, u32[]{:S(2)}) collective-permute-start(bf16[2,592,128]{2,1,0:T(8,128)(2,1)S(1)} %merge.1.refs_2_.refs_0_), channel_id=1, source_target_pairs={{0,2},{1,3},{2,0},{3,1},{4,6},{5,7},{6,4},{7,5},{8,10},{9,11},{10,... | collective-permute-start | bytes 909320 | tf_op jit(solution)/shard_map/ppermute | solution.py:304
  17.5 15.1 %collective-permute-start.1 = (bf16[2,592,128]{2,1,0:T(8,128)(2,1)S(1)}, bf16[2,592,128]{2,1,0:T(8,128)(2,1)S(1)}, u32[]{:S(2)}, u32[]{:S(2)}) collective-permute-start(bf16[2,592,128]{2,1,0:T(8,128)(2,1)S(1)} %merge.1.refs_2_.refs_0_), channel_id=1, source_target_pairs={{0,1},{1,0},{2,3},{3,2},{4,5},{5,4},{6,7},{7,6},{8,9},{9,8},{10,11... | collective-permute-start | bytes 909320 | tf_op jit(solution)/shard_map/ppermute | solution.py:304
  22.0 8.4 %copy-start = (bf16[16,16,64,64]{3,2,1,0:T(8,128)(2,1)S(1)}, bf16[16,16,64,64]{3,2,1,0:T(8,128)(2,1)}, u32[]{:S(2)}) copy-start(bf16[16,16,64,64]{3,2,1,0:T(8,128)(2,1)} %c_ref.1) | copy-start | bytes 6291460
  22.0 8.4 %copy-start.1 = (bf16[2,8,64,64]{3,2,1,0:T(8,128)(2,1)S(1)}, bf16[2,8,64,64]{3,2,1,0:T(8,128)(2,1)}, u32[]{:S(2)}) copy-start(bf16[2,8,64,64]{3,2,1,0:T(8,128)(2,1)} %top_ref.1) | copy-start | bytes 393220
  24.6 7.9 %collective-permute-start.8 = (bf16[2,592,128]{2,1,0:T(8,128)(2,1)S(1)}, bf16[2,592,128]{2,1,0:T(8,128)(2,1)S(1)}, u32[]{:S(2)}, u32[]{:S(2)}) collective-permute-start(bf16[2,592,128]{2,1,0:T(8,128)(2,1)S(1)} %collective-permute-done.4.refs_3_.refs_4_), channel_id=1, source_target_pairs={{0,2},{1,3},{2,0},{3,1},{4,6},{5,7},{6,4},{7,5},{8,10},{9,11},{10,... | collective-permute-start | bytes 909320 | tf_op jit(solution)/shard_map/ppermute | solution.py:304
  25.2 7.4 %collective-permute-start.7 = (bf16[2,592,128]{2,1,0:T(8,128)(2,1)S(1)}, bf16[2,592,128]{2,1,0:T(8,128)(2,1)S(1)}, u32[]{:S(2)}, u32[]{:S(2)}) collective-permute-start(bf16[2,592,128]{2,1,0:T(8,128)(2,1)S(1)} %collective-permute-done.4.refs_3_.refs_4_), channel_id=1, source_target_pairs={{0,1},{1,0},{2,3},{3,2},{4,5},{5,4},{6,7},{7,6},{8,9},{9,8},{10,11... | collective-permute-start | bytes 909320 | tf_op jit(solution)/shard_map/ppermute | solution.py:304
  25.2 7.4 %collective-permute-start.3 = (bf16[2,592,128]{2,1,0:T(8,128)(2,1)S(1)}, bf16[2,592,128]{2,1,0:T(8,128)(2,1)S(1)}, u32[]{:S(2)}, u32[]{:S(2)}) collective-permute-start(bf16[2,592,128]{2,1,0:T(8,128)(2,1)S(1)} %collective-permute-done.2.refs_2_), channel_id=1, source_target_pairs={{0,1},{1,0},{2,3},{3,2},{4,5},{5,4},{6,7},{7,6},{8,9},{9,8},{10,11... | collective-permute-start | bytes 909320 | tf_op jit(solution)/shard_map/ppermute | solution.py:304
  30.4 2.1 %copy-start.9 = (s32[2,8]{1,0:T(2,128)S(1)}, s32[2,8]{1,0:T(2,128)}, u32[]{:S(2)}) copy-start(s32[2,8]{1,0:T(2,128)} %param.19) | copy-start | bytes 196
  30.5 2.1 %copy-start.8 = (s32[16,16]{1,0:T(8,128)S(1)}, s32[16,16]{1,0:T(8,128)}, u32[]{:S(2)}) copy-start(s32[16,16]{1,0:T(8,128)} %param.17) | copy-start | bytes 3076
  30.5 3.6 %copy-start.2 = (bf16[16,128,64]{1,2,0:T(8,128)(2,1)S(1)}, bf16[16,128,64]{1,2,0:T(8,128)(2,1)}, u32[]{:S(2)}) copy-start(bf16[16,128,64]{1,2,0:T(8,128)(2,1)} %param.12) | copy-start | bytes 786436
  30.5 3.6 %copy-start.3 = (bf16[16,64,64]{2,1,0:T(8,128)(2,1)S(1)}, bf16[16,64,64]{2,1,0:T(8,128)(2,1)}, u32[]{:S(2)}) copy-start(bf16[16,64,64]{2,1,0:T(8,128)(2,1)} %refs_12_.1) | copy-start | bytes 393220
  32.5 1.6 %collective-permute-start.10 = (bf16[2,592,128]{2,1,0:T(8,128)(2,1)S(1)}, bf16[2,592,128]{2,1,0:T(8,128)(2,1)S(1)}, u32[]{:S(2)}, u32[]{:S(2)}) collective-permute-start(bf16[2,592,128]{2,1,0:T(8,128)(2,1)S(1)} %collective-permute-done.8.refs_6_), channel_id=1, source_target_pairs={{0,1},{1,0},{2,3},{3,2},{4,5},{5,4},{6,7},{7,6},{8,9},{9,8},{10,11... | collective-permute-start | bytes 909320 | tf_op jit(solution)/shard_map/ppermute | solution.py:304
